TPU v7x, 32 devices: a whole 2x2x4 slice. The times are simulated.
32 devices in a mesh: groups: 2 (over x), rows: 16 (over z, y, core).
Axes of the slice: x: 2, y: 2, z: 4, core: 2. Of those that a mesh axis runs over, the one named last changes fastest.
Arguments:
- frames: bfloat16 [2048, 3, 256], P(('groups', 'rows')), parts along dimension 0, may hold values from -6 to 6
- conv_tiles: bfloat16 [16, 27, 512, 128], P('rows'), may hold values from -0.0390625 to 0.0390625
- up_tiles: bfloat16 [16, 9, 256, 128], P('rows'), may hold values from -0.0625 to 0.0625
Outputs:
- upsampled_tiles: bfloat16 [32, 256, 128], P(('groups', 'rows')), parts along dimension 0
There are 2 independent parts, one for each index of `groups`. A program takes and returns all parts, laid end to end along the dimension named above; an argument that names none is the same for every part. Nothing has to cross between parts.
All inputs are finite; a program needn't handle non-finite values.
Results may differ from a plain program's by a relative error of at most 0.009.
Values may be sent and summed in bfloat16 or wider, within the bound.
No kernel may reach another device: no remote copies, remote signals or barrier semaphores. Data moves between devices by JAX's collectives and lax.ppermute only.
A program may use at most 64 MiB of HBM per device.

v0:
```python
import jax
import jax.numpy as jnp
from jax import lax
from jax.sharding import PartitionSpec as P

W = 64


def partner_2(block, axis, stride):
    count = lax.axis_size(axis)
    route = []
    for low in range(count):
        high = low | 1 << stride
        if high != low and high < count:
            route += [(low, high), (high, low)]
    return lax.ppermute(block, axis, route)


def shift_plane(planes, row_step, col_step):
    height = planes.shape[-2]
    width = planes.shape[-1]
    padded = jnp.pad(planes, [(0, 0)] * (planes.ndim - 2) + [(1, 1), (1, 1)])
    return padded[..., 1 + row_step : 1 + row_step + height, 1 + col_step : 1 + col_step + width]


def phase_groups(phase):
    if phase == 0:
        return [(-1, (0,)), (0, (1, 2))]
    return [(0, (0, 1)), (1, (2,))]


def upper_side(device_index, level):
    return device_index >> level & 1 == 1


def collect_channels(pieces, device_index):
    for level in range(3):
        partner = partner_2(pieces, "rows", level)
        pieces = jnp.where(
            upper_side(device_index, level),
            jnp.concatenate([partner, pieces], 0),
            jnp.concatenate([pieces, partner], 0),
        )
    return pieces


def halve_partials(totals, device_index, levels):
    for level in levels:
        middle = totals.shape[1] // 2
        upper_half = upper_side(device_index, level)
        kept_part = jnp.where(upper_half, totals[:, middle:], totals[:, :middle])
        sent_part = jnp.where(upper_half, totals[:, :middle], totals[:, middle:])
        totals = kept_part + partner_2(sent_part, "rows", level)
    return totals


def halve_outputs(totals, device_index):
    for level in (2, 1, 0):
        middle = totals.shape[1] // 2
        upper_half = upper_side(device_index, level)
        kept_part = jnp.where(upper_half, totals[:, middle:], totals[:, :middle])
        sent_part = jnp.where(upper_half, totals[:, :middle], totals[:, middle:])
        totals = kept_part + partner_2(sent_part.astype(jnp.bfloat16), "rows", level).astype(
            sent_part.dtype
        )
    return totals


def on_device(frames, conv_tiles, up_tiles):
    device_index = lax.axis_index("rows")
    bit_count = lax.axis_size("rows").bit_length() - 1
    pieces = collect_channels(frames, device_index)
    in_channels = pieces.shape[0]
    voxels = pieces.shape[2]
    height = voxels // W
    volume = pieces.reshape(in_channels, 3, height, W)
    filters = conv_tiles.shape[3]
    partial_value = jnp.zeros((filters, voxels), jnp.float32)
    for time_tap in range(3):
        planes = []
        for spatial_tap in range(9):
            row_tap = spatial_tap // 3
            col_tap = spatial_tap % 3
            planes.append(
                shift_plane(volume[:, time_tap], row_tap - 1, col_tap - 1).reshape(
                    in_channels, voxels
                )
            )
        columns = jnp.concatenate(planes, 0)
        weights = conv_tiles[0, 9 * time_tap : 9 * time_tap + 9].reshape(9 * in_channels, filters)
        partial_value = partial_value + lax.dot_general(
            weights, columns, (((0,), (0,)), ((), ())), preferred_element_type=jnp.float32
        )
    summed = halve_partials(partial_value, device_index, list(range(bit_count - 1, 2, -1)))
    hidden_block = jax.nn.silu(summed).astype(jnp.bfloat16)
    for level in range(3, bit_count):
        partner = partner_2(hidden_block, "rows", level)
        hidden_block = jnp.where(
            upper_side(device_index, level),
            jnp.concatenate([partner, hidden_block], 1),
            jnp.concatenate([hidden_block, partner], 1),
        )
    hidden_planes = hidden_block.reshape(filters, height, W)
    up_weight = up_tiles[0].astype(jnp.float32)
    out_channels = up_weight.shape[1]
    phase_rows = []
    for row_phase in range(2):
        phase_cols = []
        for col_phase in range(2):
            weight_parts = []
            plane_parts = []
            for row_shift, row_taps in phase_groups(row_phase):
                for col_shift, col_taps in phase_groups(col_phase):
                    combined = jnp.zeros((out_channels, filters), jnp.float32)
                    for row_tap in row_taps:
                        for col_tap in col_taps:
                            combined = combined + up_weight[3 * row_tap + col_tap]
                    weight_parts.append(combined.astype(jnp.bfloat16))
                    plane_parts.append(
                        shift_plane(hidden_planes, row_shift, col_shift).reshape(filters, voxels)
                    )
            stacked_weight = jnp.concatenate(weight_parts, 1)
            stacked_planes = jnp.concatenate(plane_parts, 0)
            phase_out = jnp.dot(stacked_weight, stacked_planes, preferred_element_type=jnp.float32)
            phase_cols.append(phase_out.reshape(out_channels, height, W))
        phase_rows.append(jnp.stack(phase_cols, 0))
    phased = jnp.stack(phase_rows, 0)
    result = phased.transpose(2, 3, 0, 4, 1).reshape(out_channels, 4 * voxels)
    summed_out = halve_outputs(result, device_index)
    return summed_out.astype(jnp.bfloat16).reshape(1, out_channels, summed_out.shape[1])


def solution(mesh):
    return jax.shard_map(
        on_device,
        mesh=mesh,
        in_specs=(
            P(("groups", "rows"), None, None),
            P("rows", None, None, None),
            P("rows", None, None, None),
        ),
        out_specs=P(("groups", "rows"), None, None),
        check_vma=False,
    )
```

profile of v0, /device:TPU:0, one launch (start us, length us, event | category | flops | bytes accessed | tf_op | source)
XLA Modules:
  0.0 54.9 jit_solution(10346275166659987350)
XLA Ops:
  0.0 1.1 %copy.5 = bf16[64,3,256]{0,2,1:T(8,128)(2,1)S(1)} copy(bf16[64,3,256]{2,0,1:T(8,128)(2,1)} %param.3) | data formatting | bytes 196608 | tf_op args[0]
  1.1 0.5 collective-permute-start
  1.6 1.1 %convert_element_type.121 = f32[1,9,256,128]{3,2,1,0:T(8,128)S(1)} convert(bf16[1,9,256,128]{3,2,1,0:T(8,128)(2,1)} %param.5) | non-fusion elementwise | flops 294912 | bytes 1769472 | tf_op jit(solution)/shard_map/convert_element_type | solution.py:104
  3.0 2.8 %collective-permute-start.1 = (bf16[128,3,256]{0,2,1:T(8,128)(2,1)S(1)}, bf16[128,3,256]{0,2,1:T(8,128)(2,1)S(1)}, u32[]{:S(2)}, u32[]{:S(2)}) collective-permute-start(bf16[128,3,256]{0,2,1:T(8,128)(2,1)S(1)} %maximum_select_fusion.3), channel_id=1, source_target_pairs={{0,2},{2,0},{1,3},{3,1},{4,6},{6,4},{5,7},{7,5},{8,10},{10,8},{9,1... | collective-permute-start | bytes 589832 | tf_op jit(solution)/shard_map/ppermute | solution.py:16
  5.8 2.3 %fusion.74 = (bf16[1,9,512,128]{3,2,1,0:T(8,128)(2,1)S(1)}, bf16[1,9,512,128]{3,2,1,0:T(8,128)(2,1)S(1)}, bf16[1,9,512,128]{3,2,1,0:T(8,128)(2,1)S(1)}) fusion(bf16[1,27,512,128]{3,2,1,0:T(8,128)(2,1)} %param.4), kind=kLoop, calls=%fused_computation.175 | loop fusion | bytes 7077888 | tf_op jit(solution)/shard_map/slice | solution.py:90
  8.2 3.0 %collective-permute-done.1 = bf16[128,3,256]{0,2,1:T(8,128)(2,1)S(1)} collective-permute-done((bf16[128,3,256]{0,2,1:T(8,128)(2,1)S(1)}, bf16[128,3,256]{0,2,1:T(8,128)(2,1)S(1)}, u32[]{:S(2)}, u32[]{:S(2)}) %collective-permute-start.1) | collective-permute-done | bytes 196640 | tf_op jit(solution)/shard_map/ppermute | solution.py:16
  11.3 1.9 %collective-permute-start.2 = (bf16[256,3,256]{0,2,1:T(8,128)(2,1)S(1)}, bf16[256,3,256]{0,2,1:T(8,128)(2,1)S(1)}, u32[]{:S(2)}, u32[]{:S(2)}) collective-permute-start(bf16[256,3,256]{0,2,1:T(8,128)(2,1)S(1)} %maximum_select_fusion.1), channel_id=1, source_target_pairs={{0,4},{4,0},{1,5},{5,1},{2,6},{6,2},{3,7},{7,3},{8,12},{12,8},{9,1... | collective-permute-start | bytes 1179656 | tf_op jit(solution)/shard_map/ppermute | solution.py:16
  13.6 8.5 %collective-permute-done.2 = bf16[256,3,256]{0,2,1:T(8,128)(2,1)S(1)} collective-permute-done((bf16[256,3,256]{0,2,1:T(8,128)(2,1)S(1)}, bf16[256,3,256]{0,2,1:T(8,128)(2,1)S(1)}, u32[]{:S(2)}, u32[]{:S(2)}) %collective-permute-start.2) | collective-permute-done | bytes 393248 | tf_op jit(solution)/shard_map/ppermute | solution.py:16
  22.5 0.5 pad_slice_fusion
  24.0 0.8 %fusion.76 = f32[256,128]{1,0:T(8,128)S(1)} fusion(bf16[4608,256]{0,1:T(8,128)(2,1)S(1)} %constant_dynamic-update-slice_fusion, bf16[4608,128]{1,0:T(8,128)(2,1)S(1)} %bitcast.170), kind=kOutput, calls=%fused_computation.177 | convolution fusion | flops 301989888 | bytes 3670016 | tf_op jit(solution)/shard_map/dot_general | solution.py:91
  24.8 0.8 %convolution_add_fusion.1 = f32[256,128]{1,0:T(8,128)S(1)} fusion(f32[256,128]{1,0:T(8,128)S(1)} %fusion.76, bf16[4608,256]{0,1:T(8,128)(2,1)S(1)} %constant_dynamic-update-slice_fusion.9, bf16[4608,128]{1,0:T(8,128)(2,1)S(1)} %bitcast.172), kind=kOutput, calls=%fused_computation.2 | convolution fusion | flops 302022656 | bytes 3801088 | tf_op jit(solution)/shard_map/dot_general | solution.py:91
  25.6 0.8 %fusion = f32[128,256]{0,1:T(8,128)S(1)} fusion(f32[256,128]{1,0:T(8,128)S(1)} %convolution_add_fusion.1, bf16[4608,256]{0,1:T(8,128)(2,1)S(1)} %constant_dynamic-update-slice_fusion.18, bf16[4608,128]{1,0:T(8,128)(2,1)S(1)} %bitcast.171), kind=kOutput, calls=%fused_computation.1 | convolution fusion | flops 302022656 | bytes 3801088 | tf_op jit(solution)/shard_map/dot_general | solution.py:91
  26.4 2.6 %collective-permute-start.3 = (f32[128,128]{0,1:T(8,128)S(1)}, f32[128,128]{0,1:T(8,128)S(1)}, u32[]{:S(2)}, u32[]{:S(2)}) collective-permute-start(f32[128,128]{0,1:T(8,128)S(1)} %slice_select_fusion), channel_id=1, source_target_pairs={{0,8},{8,0},{1,9},{9,1},{2,10},{10,2},{3,11},{11,3},{4,12},{12,4},... | collective-permute-start | bytes 196616 | tf_op jit(solution)/shard_map/ppermute | solution.py:16
  29.0 2.6 %collective-permute-done.3 = f32[128,128]{0,1:T(8,128)S(1)} collective-permute-done((f32[128,128]{0,1:T(8,128)S(1)}, f32[128,128]{0,1:T(8,128)S(1)}, u32[]{:S(2)}, u32[]{:S(2)}) %collective-permute-start.3) | collective-permute-done | bytes 65568 | tf_op jit(solution)/shard_map/ppermute | solution.py:16
  31.7 2.6 %collective-permute-start.4 = (bf16[128,128]{0,1:T(8,128)(2,1)S(1)}, bf16[128,128]{0,1:T(8,128)(2,1)S(1)}, u32[]{:S(2)}, u32[]{:S(2)}) collective-permute-start(bf16[128,128]{0,1:T(8,128)(2,1)S(1)} %multiply_convert_fusion), channel_id=1, source_target_pairs={{0,8},{8,0},{1,9},{9,1},{2,10},{10,2},{3,11},{11,3},{4,12},{12,4},... | collective-permute-start | bytes 98312 | tf_op jit(solution)/shard_map/ppermute | solution.py:16
  34.3 2.2 %collective-permute-done.4 = bf16[128,128]{0,1:T(8,128)(2,1)S(1)} collective-permute-done((bf16[128,128]{0,1:T(8,128)(2,1)S(1)}, bf16[128,128]{0,1:T(8,128)(2,1)S(1)}, u32[]{:S(2)}, u32[]{:S(2)}) %collective-permute-start.4) | collective-permute-done | bytes 32800 | tf_op jit(solution)/shard_map/ppermute | solution.py:16
  37.0 0.3 copy.9
  37.5 0.3 copy.10
  37.8 0.3 fusion.31
  38.1 0.3 copy.11
  38.3 0.3 fusion.46
  38.6 0.3 copy.12
  38.9 0.5 maximum_bitcast_fusion.1
  39.4 0.5 maximum_bitcast_fusion.2
  39.9 0.5 maximum_bitcast_fusion
  40.4 0.7 %reshape.195 = f32[256,1024]{0,1:T(8,128)S(1)} reshape(f32[256,4,2,64,2]{0,4,3,2,1:T(2,128)S(1)} %maximum_bitcast_fusion) | data formatting | bytes 2097152 | tf_op jit(solution)/shard_map/reshape | solution.py:128
  41.2 1.8 %collective-permute-start.5 = (bf16[256,512]{0,1:T(8,128)(2,1)S(1)}, bf16[256,512]{0,1:T(8,128)(2,1)S(1)}, u32[]{:S(2)}, u32[]{:S(2)}) collective-permute-start(bf16[256,512]{0,1:T(8,128)(2,1)S(1)} %select_convert_fusion), channel_id=1, source_target_pairs={{0,4},{4,0},{1,5},{5,1},{2,6},{6,2},{3,7},{7,3},{8,12},{12,8},{9,1... | collective-permute-start | bytes 786440 | tf_op jit(solution)/shard_map/ppermute | solution.py:16
  43.0 4.6 %collective-permute-done.5 = bf16[256,512]{0,1:T(8,128)(2,1)S(1)} collective-permute-done((bf16[256,512]{0,1:T(8,128)(2,1)S(1)}, bf16[256,512]{0,1:T(8,128)(2,1)S(1)}, u32[]{:S(2)}, u32[]{:S(2)}) %collective-permute-start.5) | collective-permute-done | bytes 262176 | tf_op jit(solution)/shard_map/ppermute | solution.py:16
  47.8 1.5 %collective-permute-start.6 = (bf16[256,256]{0,1:T(8,128)(2,1)S(1)}, bf16[256,256]{0,1:T(8,128)(2,1)S(1)}, u32[]{:S(2)}, u32[]{:S(2)}) collective-permute-start(bf16[256,256]{0,1:T(8,128)(2,1)S(1)} %select_convert_fusion.1), channel_id=1, source_target_pairs={{0,2},{2,0},{1,3},{3,1},{4,6},{6,4},{5,7},{7,5},{8,10},{10,8},{9,1... | collective-permute-start | bytes 393224 | tf_op jit(solution)/shard_map/ppermute | solution.py:16
  49.2 3.5 %collective-permute-done.6 = bf16[256,256]{0,1:T(8,128)(2,1)S(1)} collective-permute-done((bf16[256,256]{0,1:T(8,128)(2,1)S(1)}, bf16[256,256]{0,1:T(8,128)(2,1)S(1)}, u32[]{:S(2)}, u32[]{:S(2)}) %collective-permute-start.6) | collective-permute-done | bytes 131104 | tf_op jit(solution)/shard_map/ppermute | solution.py:16
  52.9 1.2 %collective-permute-done.7 = bf16[256,128]{0,1:T(8,128)(2,1)S(1)} collective-permute-done((bf16[256,128]{0,1:T(8,128)(2,1)S(1)}, bf16[256,128]{0,1:T(8,128)(2,1)S(1)}, u32[]{:S(2)}, u32[]{:S(2)}) %collective-permute-start.7) | collective-permute-done | bytes 65568 | tf_op jit(solution)/shard_map/ppermute | solution.py:16
  54.2 0.7 %copy.13 = bf16[1,256,128]{2,1,0:T(8,128)(2,1)} copy(bf16[1,256,128]{1,2,0:T(8,128)(2,1)S(1)} %fusion.67) | data formatting | bytes 131072 | tf_op jit(solution)/shard_map/reshape | solution.py:130
  (52 shorter events, 3.0 us)
Async XLA Ops:
  1.1 1.7 %collective-permute-start = (bf16[64,3,256]{0,2,1:T(8,128)(2,1)S(1)}, bf16[64,3,256]{0,2,1:T(8,128)(2,1)S(1)}, u32[]{:S(2)}, u32[]{:S(2)}) collective-permute-start(bf16[64,3,256]{0,2,1:T(8,128)(2,1)S(1)} %copy.5), channel_id=1, source_target_pairs={{0,1},{1,0},{2,3},{3,2},{4,5},{5,4},{6,7},{7,6},{8,9},{9,8},{10,11... | collective-permute-start | bytes 294920 | tf_op jit(solution)/shard_map/ppermute | solution.py:16
  3.0 8.2 %collective-permute-start.1 = (bf16[128,3,256]{0,2,1:T(8,128)(2,1)S(1)}, bf16[128,3,256]{0,2,1:T(8,128)(2,1)S(1)}, u32[]{:S(2)}, u32[]{:S(2)}) collective-permute-start(bf16[128,3,256]{0,2,1:T(8,128)(2,1)S(1)} %maximum_select_fusion.3), channel_id=1, source_target_pairs={{0,2},{2,0},{1,3},{3,1},{4,6},{6,4},{5,7},{7,5},{8,10},{10,8},{9,1... | collective-permute-start | bytes 589832 | tf_op jit(solution)/shard_map/ppermute | solution.py:16
  11.3 10.8 %collective-permute-start.2 = (bf16[256,3,256]{0,2,1:T(8,128)(2,1)S(1)}, bf16[256,3,256]{0,2,1:T(8,128)(2,1)S(1)}, u32[]{:S(2)}, u32[]{:S(2)}) collective-permute-start(bf16[256,3,256]{0,2,1:T(8,128)(2,1)S(1)} %maximum_select_fusion.1), channel_id=1, source_target_pairs={{0,4},{4,0},{1,5},{5,1},{2,6},{6,2},{3,7},{7,3},{8,12},{12,8},{9,1... | collective-permute-start | bytes 1179656 | tf_op jit(solution)/shard_map/ppermute | solution.py:16
  26.4 5.2 %collective-permute-start.3 = (f32[128,128]{0,1:T(8,128)S(1)}, f32[128,128]{0,1:T(8,128)S(1)}, u32[]{:S(2)}, u32[]{:S(2)}) collective-permute-start(f32[128,128]{0,1:T(8,128)S(1)} %slice_select_fusion), channel_id=1, source_target_pairs={{0,8},{8,0},{1,9},{9,1},{2,10},{10,2},{3,11},{11,3},{4,12},{12,4},... | collective-permute-start | bytes 196616 | tf_op jit(solution)/shard_map/ppermute | solution.py:16
  31.7 4.9 %collective-permute-start.4 = (bf16[128,128]{0,1:T(8,128)(2,1)S(1)}, bf16[128,128]{0,1:T(8,128)(2,1)S(1)}, u32[]{:S(2)}, u32[]{:S(2)}) collective-permute-start(bf16[128,128]{0,1:T(8,128)(2,1)S(1)} %multiply_convert_fusion), channel_id=1, source_target_pairs={{0,8},{8,0},{1,9},{9,1},{2,10},{10,2},{3,11},{11,3},{4,12},{12,4},... | collective-permute-start | bytes 98312 | tf_op jit(solution)/shard_map/ppermute | solution.py:16
  41.2 6.4 %collective-permute-start.5 = (bf16[256,512]{0,1:T(8,128)(2,1)S(1)}, bf16[256,512]{0,1:T(8,128)(2,1)S(1)}, u32[]{:S(2)}, u32[]{:S(2)}) collective-permute-start(bf16[256,512]{0,1:T(8,128)(2,1)S(1)} %select_convert_fusion), channel_id=1, source_target_pairs={{0,4},{4,0},{1,5},{5,1},{2,6},{6,2},{3,7},{7,3},{8,12},{12,8},{9,1... | collective-permute-start | bytes 786440 | tf_op jit(solution)/shard_map/ppermute | solution.py:16
  47.8 5.0 %collective-permute-start.6 = (bf16[256,256]{0,1:T(8,128)(2,1)S(1)}, bf16[256,256]{0,1:T(8,128)(2,1)S(1)}, u32[]{:S(2)}, u32[]{:S(2)}) collective-permute-start(bf16[256,256]{0,1:T(8,128)(2,1)S(1)} %select_convert_fusion.1), channel_id=1, source_target_pairs={{0,2},{2,0},{1,3},{3,1},{4,6},{6,4},{5,7},{7,5},{8,10},{10,8},{9,1... | collective-permute-start | bytes 393224 | tf_op jit(solution)/shard_map/ppermute | solution.py:16
  52.9 1.3 %collective-permute-start.7 = (bf16[256,128]{0,1:T(8,128)(2,1)S(1)}, bf16[256,128]{0,1:T(8,128)(2,1)S(1)}, u32[]{:S(2)}, u32[]{:S(2)}) collective-permute-start(bf16[256,128]{0,1:T(8,128)(2,1)S(1)} %select_convert_fusion.2), channel_id=1, source_target_pairs={{0,1},{1,0},{2,3},{3,2},{4,5},{5,4},{6,7},{7,6},{8,9},{9,8},{10,11... | collective-permute-start | bytes 196616 | tf_op jit(solution)/shard_map/ppermute | solution.py:16
where the time goes:
time: 55.1 us; the launch traced here: 54.9 us
  waiting for transfers between devices  25.7 us (47%)
  starting transfers between devices  13.8 us (25%)
  local copies, waits for them, and re-layouts  7.49 us (14%)
  other arithmetic  4.05 us (7%)
  matrix products  3.46 us (6%)
    ppermute x8, waiting for transfers between devices, partner_2(): return lax.ppermute(block, axis, route)  25.7 us
    ppermute x8, starting transfers between devices, partner_2(): return lax.ppermute(block, axis, route)  13.8 us
    dot_general x3, matrix products, on_device(): lax.dot_general(weights, columns, (((0,), (0,)), ((), ())), preferred_ele...  2.39 us
    slice x1, local copies, waits for them, and re-layouts, on_device(): conv_tiles[0, 9 * time_tap:9 * time_tap + 9]  2.35 us
    unnamed x25, local copies, waits for them, and re-layouts  1.52 us
    convert_element_type x1, other arithmetic, on_device(): up_weight = up_tiles[0].astype(jnp.float32)  1.15 us
  transfers between devices with their start and end apart: 8, of which 7 were waited for; matrix products, arithmetic and copies ran while one was open for 7% of the time, Pallas kernels for 0%

commit v1 on v0

v1 whole, which is shorter than its diff:
```python
import functools

import jax
import jax.numpy as jnp
from jax import lax
from jax.experimental import pallas as pl
from jax.experimental.pallas import tpu as pltpu
from jax.sharding import PartitionSpec as P

W = 64
BF = jnp.bfloat16
F32 = jnp.float32
VMEM = pl.BlockSpec(memory_space=pltpu.VMEM)
SMEM = pl.BlockSpec(memory_space=pltpu.SMEM)
LIMIT = 32 * 2**20


def swap(block, mask):
    count = lax.axis_size("rows")
    return lax.ppermute(block, "rows", [(i, i ^ mask) for i in range(count)])


def local(body, outs, scratch, flops, moved, *args):
    return pl.pallas_call(
        body,
        out_shape=outs,
        in_specs=[SMEM] + [VMEM] * (len(args) - 1),
        out_specs=jax.tree.map(lambda _: VMEM, outs),
        scratch_shapes=scratch,
        compiler_params=pltpu.CompilerParams(vmem_limit_bytes=LIMIT),
        cost_estimate=pl.CostEstimate(flops=flops, bytes_accessed=moved, transcendentals=0),
    )(*args)


def phase_groups(phase):
    if phase == 0:
        return [(-1, (0,)), (0, (1, 2))]
    return [(0, (0, 1)), (1, (2,))]


def shift_cols(plane, step):
    if step == 0:
        return plane
    voxels = plane.shape[0]
    col = lax.broadcasted_iota(jnp.int32, plane.shape, 0) % W
    rolled = pltpu.roll(plane, (-step) % voxels, 0)
    return jnp.where((col + step >= 0) & (col + step < W), rolled, 0)


def shift_rows(plane, step):
    if step == 0:
        return plane
    zeros = jnp.zeros((W,) + plane.shape[1:], plane.dtype)
    if step > 0:
        return jnp.concatenate([plane[W:], zeros], 0)
    return jnp.concatenate([zeros, plane[:-W]], 0)


def phase_body(me_ref, tiles_ref, out_ref):
    taps = [tiles_ref[t].astype(F32).T for t in range(9)]
    depth = taps[0].shape[0]
    for p in range(2):
        for q in range(2):
            place = 0
            for _, row_taps in phase_groups(p):
                for _, col_taps in phase_groups(q):
                    total = None
                    for b in row_taps:
                        for e in col_taps:
                            tap = taps[3 * b + e]
                            total = tap if total is None else total + tap
                    out_ref[2 * p + q, place * depth : (place + 1) * depth, :] = total.astype(BF)
                    place += 1


def conv_body(share, me_ref, *refs):
    *piece_refs, weight_ref, full_ref, sent_ref, order_ref, columns_ref = refs
    frames_of, channels, voxels = order_ref.shape
    if len(piece_refs) == 1:
        order_ref[...] = piece_refs[0][...]
    else:
        part = channels // share
        for mask, piece_ref in enumerate(piece_refs):
            place = pl.multiple_of((me_ref[0] % share ^ mask) * part, part)
            order_ref[:, pl.ds(place, part), :] = piece_ref[...]
    for a in range(frames_of):
        columns_ref[:, a * channels : (a + 1) * channels] = order_ref[a].T
    products = {}
    taps = [(b, e) for e in range(3) for b in range(3)]
    for first in range(0, 9, 2):
        pair = taps[first : first + 2]
        weights = jnp.concatenate(
            [
                jnp.concatenate([weight_ref[9 * a + 3 * b + e] for a in range(frames_of)], 0)
                for b, e in pair
            ],
            1,
        )
        product = jnp.dot(columns_ref[...], weights, preferred_element_type=F32)
        for place, tap in enumerate(pair):
            filters = product.shape[1] // len(pair)
            products[tap] = product[:, place * filters : (place + 1) * filters]
    total = None
    for e in range(3):
        rows = sum(shift_rows(products[b, e], b - 1) for b in range(3))
        moved = shift_cols(rows, e - 1)
        total = moved if total is None else total + moved
    full_ref[...] = total
    sent_ref[...] = total.astype(BF)


def up_body(me_ref, *refs):
    *sum_refs, weight_ref, keep_ref, send_ref = refs
    pre = sum_refs[0][...]
    for other_ref in sum_refs[1:]:
        pre = pre + other_ref[...].astype(F32)
    hidden = pre / (1 + jnp.exp(-pre))
    hidden = hidden.astype(BF).astype(F32)
    planes = {}
    for v in (-1, 0, 1):
        shifted = shift_cols(hidden, v).astype(BF)
        for u in (-1, 0, 1):
            planes[u, v] = shift_rows(shifted, u)
    results = {}
    for p in range(2):
        for q in range(2):
            columns = jnp.concatenate(
                [planes[u, v] for u, _ in phase_groups(p) for v, _ in phase_groups(q)], 1
            )
            results[p, q] = jnp.dot(columns, weight_ref[2 * p + q], preferred_element_type=F32)
    halves, lines = keep_ref.shape[:2]
    upper = me_ref[0] % 2 == 1

    def line(f, k):
        row, p = divmod(f * lines + k, 2)
        return [results[p, q][row * W : (row + 1) * W] for q in range(2)]

    for half in range(halves):
        for k in range(lines):
            even, odd = line(2 * half, k), line(2 * half + 1, k)
            for q in range(2):
                cells = slice(q * W, (q + 1) * W)
                keep_ref[half, k, cells, :] = jnp.where(upper, odd[q], even[q])
                send_ref[half, k, cells, :] = jnp.where(upper, even[q], odd[q]).astype(BF)


def chip_body(me_ref, keep_ref, mate_ref, *out_refs):
    halves = keep_ref.shape[0]
    mine = me_ref[0] // 2 % halves
    for mask, out_ref in enumerate(out_refs):
        place = mine ^ mask
        total = keep_ref[place] + mate_ref[place].astype(F32)
        out_ref[...] = total.astype(out_ref.dtype)


def final_body(me_ref, own_ref, *refs):
    *other_refs, out_ref = refs
    total = own_ref[...]
    for other_ref in other_refs:
        total = total + other_ref[...].astype(F32)
    total = total.astype(BF)
    cell = lax.broadcasted_iota(jnp.int32, (2 * W, 2 * W), 0)
    place = lax.broadcasted_iota(jnp.int32, (2 * W, 2 * W), 1)
    spread = (place == 2 * (cell % W) + cell // W).astype(BF)
    for k in range(total.shape[0]):
        woven = lax.dot_general(
            total[k], spread, (((0,), (0,)), ((), ())), preferred_element_type=F32
        )
        out_ref[0, :, k * 2 * W : (k + 1) * 2 * W] = woven.astype(BF)


def on_device(frames, conv_tiles, up_tiles):
    index = lax.axis_index("rows")
    me = index.reshape(1).astype(jnp.int32)
    count = lax.axis_size("rows")
    part, frames_of, voxels = frames.shape
    taps, channels, filters = conv_tiles.shape[1:]
    outputs = up_tiles.shape[2]
    share = channels // part
    blocks = count // share
    lines = 2 * (voxels // W) // share
    shape = jax.ShapeDtypeStruct

    mine = frames.transpose(1, 0, 2)
    pieces = [mine] + [None] * (share - 1)
    for mask in range(2, share, 2):
        pieces[mask] = swap(mine, mask)
    for mask in range(0, share, 2):
        pieces[mask + 1] = swap(pieces[mask], 1)
    if part % 16:
        for mask in [1 << level for level in range(share.bit_length() - 1)]:
            pieces = [
                jnp.where(index & mask != 0, pieces[j ^ mask], pieces[j]) for j in range(share)
            ]
        pieces = [jnp.concatenate(pieces, 1)]

    phases = local(
        phase_body,
        shape((4, 4 * filters, outputs), BF),
        [],
        32 * filters * outputs,
        50 * filters * outputs,
        me,
        up_tiles[0],
    )
    partial, sent = local(
        functools.partial(conv_body, share),
        (shape((voxels, filters), F32), shape((voxels, filters), BF)),
        [
            pltpu.VMEM((frames_of, channels, voxels), BF),
            pltpu.VMEM((voxels, frames_of * channels), BF),
        ],
        2 * taps * channels * filters * voxels,
        2 * taps * channels * filters,
        me,
        *pieces,
        conv_tiles[0],
    )
    others = [swap(sent, share * block) for block in range(1, blocks)]
    keep, send = local(
        up_body,
        (
            shape((share // 2, lines, 2 * W, outputs), F32),
            shape((share // 2, lines, 2 * W, outputs), BF),
        ),
        [],
        32 * filters * outputs * voxels,
        32 * filters * outputs,
        me,
        partial,
        *others,
        phases,
    )
    mate = swap(send, 1)
    one = (lines, 2 * W, outputs)
    own, *leaving = local(
        chip_body,
        (shape(one, F32),) + (shape(one, BF),) * (share // 2 - 1),
        [],
        keep.size,
        6 * keep.size,
        me,
        keep,
        mate,
    )
    arrived = [swap(block, 2 * (mask + 1)) for mask, block in enumerate(leaving)]
    return local(
        final_body,
        shape((1, outputs, lines * 2 * W), BF),
        [],
        own.size,
        12 * own.size,
        me,
        own,
        *arrived,
    )


def solution(mesh):
    return jax.shard_map(
        on_device,
        mesh=mesh,
        in_specs=(
            P(("groups", "rows"), None, None),
            P("rows", None, None, None),
            P("rows", None, None, None),
        ),
        out_specs=P(("groups", "rows"), None, None),
        check_vma=False,
    )
```

time: 55.1 us -> 31.8 us (0.58)
  waiting for transfers between devices: 25.7 us -> 14.4 us
  local copies, waits for them, and re-layouts: 7.49 us -> 2.9 us
  other arithmetic: 4.05 us -> 0 us
  matrix products: 3.46 us -> 0 us
  Pallas kernels: 0 us -> 2.88 us
  starting transfers between devices: 13.8 us -> 11.4 us
    ppermute x8 -> x12, waiting for transfers between devices: 25.7 us -> 14.4 us  [swap(): return lax.ppermute(block, 'rows', [(i, i ^ mask) for i in range(count)])]
    dot_general x7 -> x0, matrix products: 3.46 us -> none  [the longest x3 2.39 us: on_device(): lax.dot_general(weights, columns, (((0,), (0,)), ((), ())), preferred_ele...]
    slice x5 -> x0, local copies, waits for them, and re-layouts: 3.34 us -> none  [the longest x1 2.35 us: on_device(): conv_tiles[0, 9 * time_tap:9 * time_tap + 9]]
    pallas_call x0 -> x5, Pallas kernels: none -> 2.88 us  [local(): pl.pallas_call(body, out_shape=outs, in_specs=[SMEM] + [VMEM] * (len(args...]
    ppermute x8 -> x12, starting transfers between devices: 13.8 us -> 11.4 us  [swap(): return lax.ppermute(block, 'rows', [(i, i ^ mask) for i in range(count)])]
    reshape x2 -> x0, local copies, waits for them, and re-layouts: 1.45 us -> none  [the longest x1 0.73 us: on_device(): summed_out.astype(jnp.bfloat16)]
    convert_element_type x7 -> x0, other arithmetic: 1.44 us -> none  [the longest x1 1.15 us: on_device(): up_weight = up_tiles[0].astype(jnp.float32)]
    unnamed x25 -> x6, local copies, waits for them, and re-layouts: 1.52 us -> 2.9 us
  transfers between devices with their start and end apart: 8 -> 12, of which waited for: 7 -> 9; matrix products, arithmetic and copies ran while one was open for 7% -> 0% of each run, Pallas kernels for 0% -> 1%
where the time goes in v1:
time: 31.8 us; the launch traced here: 31.6 us
  waiting for transfers between devices  14.4 us (45%)
  starting transfers between devices  11.4 us (36%)
  local copies, waits for them, and re-layouts  2.9 us (9%)
  Pallas kernels  2.88 us (9%)
    ppermute x12, waiting for transfers between devices, swap(): return lax.ppermute(block, 'rows', [(i, i ^ mask) for i in range(count)])  14.4 us
    ppermute x12, starting transfers between devices, swap(): return lax.ppermute(block, 'rows', [(i, i ^ mask) for i in range(count)])  11.4 us
    unnamed x6, local copies, waits for them, and re-layouts  2.9 us
    pallas_call x5, Pallas kernels, local(): pl.pallas_call(body, out_shape=outs, in_specs=[SMEM] + [VMEM] * (len(args...  2.88 us
  transfers between devices with their start and end apart: 12, of which 9 were waited for; matrix products, arithmetic and copies ran while one was open for 0% of the time, Pallas kernels for 1%

profile of v1, /device:TPU:0, one launch (start us, length us, event | category | flops | bytes accessed | tf_op | source)
XLA Modules:
  0.0 31.6 jit_solution(9556389098595429641)
XLA Ops:
  0.0 4.0 %collective-permute-start.5 = (bf16[3,64,256]{2,1,0:T(8,128)(2,1)}, bf16[3,64,256]{2,1,0:T(8,128)(2,1)S(1)}, u32[]{:S(2)}, u32[]{:S(2)}) collective-permute-start(bf16[3,64,256]{2,1,0:T(8,128)(2,1)} %bitcast.6), channel_id=1, source_target_pairs={{0,6},{1,7},{2,4},{3,5},{4,2},{5,3},{6,0},{7,1},{8,14},{9,15},{10,... | collective-permute-start | bytes 294920 | tf_op jit(solution)/shard_map/ppermute | solution.py:20
  4.0 0.4 %collective-permute-start.3 = (bf16[3,64,256]{2,1,0:T(8,128)(2,1)}, bf16[3,64,256]{2,1,0:T(8,128)(2,1)S(1)}, u32[]{:S(2)}, u32[]{:S(2)}) collective-permute-start(bf16[3,64,256]{2,1,0:T(8,128)(2,1)} %bitcast.7), channel_id=1, source_target_pairs={{0,4},{1,5},{2,6},{3,7},{4,0},{5,1},{6,2},{7,3},{8,12},{9,13},{10,... | collective-permute-start | bytes 294920 | tf_op jit(solution)/shard_map/ppermute | solution.py:20
  4.4 0.1 collective-permute-start.1
  4.5 0.0 collective-permute-start
  4.6 3.2 %collective-permute-done.5.refs_6_ = bf16[3,64,256]{2,1,0:T(8,128)(2,1)S(1)} collective-permute-done((bf16[3,64,256]{2,1,0:T(8,128)(2,1)}, bf16[3,64,256]{2,1,0:T(8,128)(2,1)S(1)}, u32[]{:S(2)}, u32[]{:S(2)}) %collective-permute-start.5) | collective-permute-done | bytes 98336 | tf_op jit(solution)/shard_map/ppermute | solution.py:20
  7.7 0.0 collective-permute-start.6
  7.8 1.6 %collective-permute-done.3.refs_4_ = bf16[3,64,256]{2,1,0:T(8,128)(2,1)S(1)} collective-permute-done((bf16[3,64,256]{2,1,0:T(8,128)(2,1)}, bf16[3,64,256]{2,1,0:T(8,128)(2,1)S(1)}, u32[]{:S(2)}, u32[]{:S(2)}) %collective-permute-start.3) | collective-permute-done | bytes 98336 | tf_op jit(solution)/shard_map/ppermute | solution.py:20
  9.3 0.0 collective-permute-start.4
  9.3 0.0 collective-permute-done.1.refs_2_
  9.3 0.5 %collective-permute-start.2 = (bf16[3,64,256]{2,1,0:T(8,128)(2,1)S(1)}, bf16[3,64,256]{2,1,0:T(8,128)(2,1)S(1)}, u32[]{:S(2)}, u32[]{:S(2)}) collective-permute-start(bf16[3,64,256]{2,1,0:T(8,128)(2,1)S(1)} %collective-permute-done.1.refs_2_), channel_id=1, source_target_pairs={{0,1},{1,0},{2,3},{3,2},{4,5},{5,4},{6,7},{7,6},{8,9},{9,8},{10,11... | collective-permute-start | bytes 294920 | tf_op jit(solution)/shard_map/ppermute | solution.py:20
  9.9 0.0 collective-permute-done.refs_1_
  9.9 0.0 collective-permute-done.6.refs_7_
  9.9 0.8 %collective-permute-done.4.refs_5_ = bf16[3,64,256]{2,1,0:T(8,128)(2,1)S(1)} collective-permute-done((bf16[3,64,256]{2,1,0:T(8,128)(2,1)S(1)}, bf16[3,64,256]{2,1,0:T(8,128)(2,1)S(1)}, u32[]{:S(2)}, u32[]{:S(2)}) %collective-permute-start.4) | collective-permute-done | bytes 98336 | tf_op jit(solution)/shard_map/ppermute | solution.py:20
  10.6 0.2 collective-permute-done.2.refs_3_
  10.8 0.0 copy-start
  10.8 2.0 %copy-done = bf16[1,27,512,128]{3,2,1,0:T(8,128)(2,1)S(1)} copy-done((bf16[1,27,512,128]{3,2,1,0:T(8,128)(2,1)S(1)}, bf16[1,27,512,128]{3,2,1,0:T(8,128)(2,1)}, u32[]{:S(2)}) %copy-start) | copy-done | bytes 3538968
  12.8 0.9 %copy-done.2 = bf16[64,3,256]{2,0,1:T(8,128)(2,1)S(1)} copy-done((bf16[64,3,256]{2,0,1:T(8,128)(2,1)S(1)}, bf16[64,3,256]{2,0,1:T(8,128)(2,1)}, u32[]{:S(2)}) %copy-start.2) | copy-done | bytes 98328
  13.7 1.3 %shard_map.37 = (f32[256,128]{1,0:T(8,128)S(1)}, bf16[256,128]{1,0:T(8,128)(2,1)S(1)}) custom-call(s32[1]{0:T(128)} %bitcast.me_ref, bf16[3,64,256]{2,1,0:T(8,128)(2,1)S(1)} %bitcast.10, bf16[3,64,256]{2,1,0:T(8,128)(2,1)S(1)} %collective-permute-done.refs_1_, bf16[3,64,256]{2,1,0:T(8,128)(2,1)S(1)} %collective-permute-done.1.refs_2_, ...), custom_call_target="tpu_custom_call" | custom-call | flops 905969664 | bytes 3538944 | tf_op jit(solution)/shard_map/pallas_call | solution.py:24
  15.0 2.7 %collective-permute-start.7 = (bf16[256,128]{1,0:T(8,128)(2,1)S(1)}, bf16[256,128]{1,0:T(8,128)(2,1)S(1)}, u32[]{:S(2)}, u32[]{:S(2)}) collective-permute-start(bf16[256,128]{1,0:T(8,128)(2,1)S(1)} %get-tuple-element.14), channel_id=1, source_target_pairs={{0,8},{1,9},{2,10},{3,11},{4,12},{5,13},{6,14},{7,15},{8,0},{9,1},... | collective-permute-start | bytes 196616 | tf_op jit(solution)/shard_map/ppermute | solution.py:20
  17.7 0.0 copy-done.1
  17.7 0.3 shard_map.38.refs_2_
  17.9 3.8 %collective-permute-done.7.refs_1_ = bf16[256,128]{1,0:T(8,128)(2,1)S(1)} collective-permute-done((bf16[256,128]{1,0:T(8,128)(2,1)S(1)}, bf16[256,128]{1,0:T(8,128)(2,1)S(1)}, u32[]{:S(2)}, u32[]{:S(2)}) %collective-permute-start.7) | collective-permute-done | bytes 65568 | tf_op jit(solution)/shard_map/ppermute | solution.py:20
  21.7 0.4 %shard_map.39 = (f32[4,1,128,256]{3,2,1,0:T(8,128)S(1)}, bf16[4,1,128,256]{3,2,1,0:T(8,128)(2,1)S(1)}) custom-call(s32[1]{0:T(128)} %bitcast.me_ref, f32[256,128]{1,0:T(8,128)S(1)} %get-tuple-element.13.refs_0_, bf16[256,128]{1,0:T(8,128)(2,1)S(1)} %collective-permute-done.7.refs_1_, bf16[4,512,256]{2,1,0:T(8,128)(2,1)S(1)} %shard_map.38.refs_2_), custom_call_target="tpu_custom_call" | custom-call | flops 268435456 | bytes 1048576 | tf_op jit(solution)/shard_map/pallas_call | solution.py:24
  22.2 0.1 collective-permute-start.8
  22.2 1.5 %collective-permute-done.8.mate_ref = bf16[4,1,128,256]{3,2,1,0:T(8,128)(2,1)S(1)} collective-permute-done((bf16[4,1,128,256]{3,2,1,0:T(8,128)(2,1)S(1)}, bf16[4,1,128,256]{3,2,1,0:T(8,128)(2,1)S(1)}, u32[]{:S(2)}, u32[]{:S(2)}) %collective-permute-start.8) | collective-permute-done | bytes 262176 | tf_op jit(solution)/shard_map/ppermute | solution.py:20
  23.8 1.2 %collective-permute-start.9 = (bf16[1,128,256]{2,1,0:T(8,128)(2,1)S(1)}, bf16[1,128,256]{2,1,0:T(8,128)(2,1)S(1)}, u32[]{:S(2)}, u32[]{:S(2)}) collective-permute-start(bf16[1,128,256]{2,1,0:T(8,128)(2,1)S(1)} %get-tuple-element.18), channel_id=1, source_target_pairs={{0,2},{1,3},{2,0},{3,1},{4,6},{5,7},{6,4},{7,5},{8,10},{9,11},{10,... | collective-permute-start | bytes 196616 | tf_op jit(solution)/shard_map/ppermute | solution.py:20
  25.0 0.6 %collective-permute-start.10 = (bf16[1,128,256]{2,1,0:T(8,128)(2,1)S(1)}, bf16[1,128,256]{2,1,0:T(8,128)(2,1)S(1)}, u32[]{:S(2)}, u32[]{:S(2)}) collective-permute-start(bf16[1,128,256]{2,1,0:T(8,128)(2,1)S(1)} %get-tuple-element.19), channel_id=1, source_target_pairs={{0,4},{1,5},{2,6},{3,7},{4,0},{5,1},{6,2},{7,3},{8,12},{9,13},{10,... | collective-permute-start | bytes 196616 | tf_op jit(solution)/shard_map/ppermute | solution.py:20
  25.6 1.8 %collective-permute-start.11 = (bf16[1,128,256]{2,1,0:T(8,128)(2,1)S(1)}, bf16[1,128,256]{2,1,0:T(8,128)(2,1)S(1)}, u32[]{:S(2)}, u32[]{:S(2)}) collective-permute-start(bf16[1,128,256]{2,1,0:T(8,128)(2,1)S(1)} %get-tuple-element.20), channel_id=1, source_target_pairs={{0,6},{1,7},{2,4},{3,5},{4,2},{5,3},{6,0},{7,1},{8,14},{9,15},{10,... | collective-permute-start | bytes 196616 | tf_op jit(solution)/shard_map/ppermute | solution.py:20
  27.4 0.8 %collective-permute-done.9.refs_0_ = bf16[1,128,256]{2,1,0:T(8,128)(2,1)S(1)} collective-permute-done((bf16[1,128,256]{2,1,0:T(8,128)(2,1)S(1)}, bf16[1,128,256]{2,1,0:T(8,128)(2,1)S(1)}, u32[]{:S(2)}, u32[]{:S(2)}) %collective-permute-start.9) | collective-permute-done | bytes 65568 | tf_op jit(solution)/shard_map/ppermute | solution.py:20
  28.1 1.5 %collective-permute-done.10.refs_1_ = bf16[1,128,256]{2,1,0:T(8,128)(2,1)S(1)} collective-permute-done((bf16[1,128,256]{2,1,0:T(8,128)(2,1)S(1)}, bf16[1,128,256]{2,1,0:T(8,128)(2,1)S(1)}, u32[]{:S(2)}, u32[]{:S(2)}) %collective-permute-start.10) | collective-permute-done | bytes 65568 | tf_op jit(solution)/shard_map/ppermute | solution.py:20
  29.6 1.1 %collective-permute-done.11.refs_2_ = bf16[1,128,256]{2,1,0:T(8,128)(2,1)S(1)} collective-permute-done((bf16[1,128,256]{2,1,0:T(8,128)(2,1)S(1)}, bf16[1,128,256]{2,1,0:T(8,128)(2,1)S(1)}, u32[]{:S(2)}, u32[]{:S(2)}) %collective-permute-start.11) | collective-permute-done | bytes 65568 | tf_op jit(solution)/shard_map/ppermute | solution.py:20
  30.7 0.8 %shard_map.41 = bf16[1,256,128]{2,1,0:T(8,128)(2,1)} custom-call(s32[1]{0:T(128)} %bitcast.me_ref, f32[1,128,256]{2,1,0:T(8,128)S(1)} %get-tuple-element.17.own_ref, bf16[1,128,256]{2,1,0:T(8,128)(2,1)S(1)} %collective-permute-done.9.refs_0_, bf16[1,128,256]{2,1,0:T(8,128)(2,1)S(1)} %collective-permute-done.10.refs_1_, ...), custom_call_target="tpu_custom_call" | custom-call | flops 32768 | bytes 393216 | tf_op jit(solution)/shard_map/pallas_call | solution.py:24
  (3 shorter events, 0.0 us)
Async XLA Ops:
  0.0 7.7 %collective-permute-start.5 = (bf16[3,64,256]{2,1,0:T(8,128)(2,1)}, bf16[3,64,256]{2,1,0:T(8,128)(2,1)S(1)}, u32[]{:S(2)}, u32[]{:S(2)}) collective-permute-start(bf16[3,64,256]{2,1,0:T(8,128)(2,1)} %bitcast.6), channel_id=1, source_target_pairs={{0,6},{1,7},{2,4},{3,5},{4,2},{5,3},{6,0},{7,1},{8,14},{9,15},{10,... | collective-permute-start | bytes 294920 | tf_op jit(solution)/shard_map/ppermute | solution.py:20
  4.0 5.4 %collective-permute-start.3 = (bf16[3,64,256]{2,1,0:T(8,128)(2,1)}, bf16[3,64,256]{2,1,0:T(8,128)(2,1)S(1)}, u32[]{:S(2)}, u32[]{:S(2)}) collective-permute-start(bf16[3,64,256]{2,1,0:T(8,128)(2,1)} %bitcast.7), channel_id=1, source_target_pairs={{0,4},{1,5},{2,6},{3,7},{4,0},{5,1},{6,2},{7,3},{8,12},{9,13},{10,... | collective-permute-start | bytes 294920 | tf_op jit(solution)/shard_map/ppermute | solution.py:20
  4.4 4.9 %collective-permute-start.1 = (bf16[3,64,256]{2,1,0:T(8,128)(2,1)}, bf16[3,64,256]{2,1,0:T(8,128)(2,1)S(1)}, u32[]{:S(2)}, u32[]{:S(2)}) collective-permute-start(bf16[3,64,256]{2,1,0:T(8,128)(2,1)} %bitcast.8), channel_id=1, source_target_pairs={{0,2},{1,3},{2,0},{3,1},{4,6},{5,7},{6,4},{7,5},{8,10},{9,11},{10,... | collective-permute-start | bytes 294920 | tf_op jit(solution)/shard_map/ppermute | solution.py:20
  4.5 5.3 %collective-permute-start = (bf16[3,64,256]{2,1,0:T(8,128)(2,1)}, bf16[3,64,256]{2,1,0:T(8,128)(2,1)S(1)}, u32[]{:S(2)}, u32[]{:S(2)}) collective-permute-start(bf16[3,64,256]{2,1,0:T(8,128)(2,1)} %bitcast.9), channel_id=1, source_target_pairs={{0,1},{1,0},{2,3},{3,2},{4,5},{5,4},{6,7},{7,6},{8,9},{9,8},{10,11... | collective-permute-start | bytes 294920 | tf_op jit(solution)/shard_map/ppermute | solution.py:20
  7.7 2.1 %collective-permute-start.6 = (bf16[3,64,256]{2,1,0:T(8,128)(2,1)S(1)}, bf16[3,64,256]{2,1,0:T(8,128)(2,1)S(1)}, u32[]{:S(2)}, u32[]{:S(2)}) collective-permute-start(bf16[3,64,256]{2,1,0:T(8,128)(2,1)S(1)} %collective-permute-done.5.refs_6_), channel_id=1, source_target_pairs={{0,1},{1,0},{2,3},{3,2},{4,5},{5,4},{6,7},{7,6},{8,9},{9,8},{10,11... | collective-permute-start | bytes 294920 | tf_op jit(solution)/shard_map/ppermute | solution.py:20
  9.3 1.3 %collective-permute-start.4 = (bf16[3,64,256]{2,1,0:T(8,128)(2,1)S(1)}, bf16[3,64,256]{2,1,0:T(8,128)(2,1)S(1)}, u32[]{:S(2)}, u32[]{:S(2)}) collective-permute-start(bf16[3,64,256]{2,1,0:T(8,128)(2,1)S(1)} %collective-permute-done.3.refs_4_), channel_id=1, source_target_pairs={{0,1},{1,0},{2,3},{3,2},{4,5},{5,4},{6,7},{7,6},{8,9},{9,8},{10,11... | collective-permute-start | bytes 294920 | tf_op jit(solution)/shard_map/ppermute | solution.py:20
  9.3 1.5 %collective-permute-start.2 = (bf16[3,64,256]{2,1,0:T(8,128)(2,1)S(1)}, bf16[3,64,256]{2,1,0:T(8,128)(2,1)S(1)}, u32[]{:S(2)}, u32[]{:S(2)}) collective-permute-start(bf16[3,64,256]{2,1,0:T(8,128)(2,1)S(1)} %collective-permute-done.1.refs_2_), channel_id=1, source_target_pairs={{0,1},{1,0},{2,3},{3,2},{4,5},{5,4},{6,7},{7,6},{8,9},{9,8},{10,11... | collective-permute-start | bytes 294920 | tf_op jit(solution)/shard_map/ppermute | solution.py:20
  10.8 2.0 %copy-start = (bf16[1,27,512,128]{3,2,1,0:T(8,128)(2,1)S(1)}, bf16[1,27,512,128]{3,2,1,0:T(8,128)(2,1)}, u32[]{:S(2)}) copy-start(bf16[1,27,512,128]{3,2,1,0:T(8,128)(2,1)} %param.4) | copy-start | bytes 10616836
  12.8 0.9 %copy-start.2 = (bf16[64,3,256]{2,0,1:T(8,128)(2,1)S(1)}, bf16[64,3,256]{2,0,1:T(8,128)(2,1)}, u32[]{:S(2)}) copy-start(bf16[64,3,256]{2,0,1:T(8,128)(2,1)} %param.3) | copy-start | bytes 294916
  13.7 4.0 %copy-start.1 = (bf16[1,9,256,128]{3,2,1,0:T(8,128)(2,1)S(1)}, bf16[1,9,256,128]{3,2,1,0:T(8,128)(2,1)}, u32[]{:S(2)}) copy-start(bf16[1,9,256,128]{3,2,1,0:T(8,128)(2,1)} %param.5) | copy-start | bytes 1769476
  15.0 6.7 %collective-permute-start.7 = (bf16[256,128]{1,0:T(8,128)(2,1)S(1)}, bf16[256,128]{1,0:T(8,128)(2,1)S(1)}, u32[]{:S(2)}, u32[]{:S(2)}) collective-permute-start(bf16[256,128]{1,0:T(8,128)(2,1)S(1)} %get-tuple-element.14), channel_id=1, source_target_pairs={{0,8},{1,9},{2,10},{3,11},{4,12},{5,13},{6,14},{7,15},{8,0},{9,1},... | collective-permute-start | bytes 196616 | tf_op jit(solution)/shard_map/ppermute | solution.py:20
  22.2 1.6 %collective-permute-start.8 = (bf16[4,1,128,256]{3,2,1,0:T(8,128)(2,1)S(1)}, bf16[4,1,128,256]{3,2,1,0:T(8,128)(2,1)S(1)}, u32[]{:S(2)}, u32[]{:S(2)}) collective-permute-start(bf16[4,1,128,256]{3,2,1,0:T(8,128)(2,1)S(1)} %get-tuple-element.16), channel_id=1, source_target_pairs={{0,1},{1,0},{2,3},{3,2},{4,5},{5,4},{6,7},{7,6},{8,9},{9,8},{10,11... | collective-permute-start | bytes 786440 | tf_op jit(solution)/shard_map/ppermute | solution.py:20
  23.8 4.3 %collective-permute-start.9 = (bf16[1,128,256]{2,1,0:T(8,128)(2,1)S(1)}, bf16[1,128,256]{2,1,0:T(8,128)(2,1)S(1)}, u32[]{:S(2)}, u32[]{:S(2)}) collective-permute-start(bf16[1,128,256]{2,1,0:T(8,128)(2,1)S(1)} %get-tuple-element.18), channel_id=1, source_target_pairs={{0,2},{1,3},{2,0},{3,1},{4,6},{5,7},{6,4},{7,5},{8,10},{9,11},{10,... | collective-permute-start | bytes 196616 | tf_op jit(solution)/shard_map/ppermute | solution.py:20
  25.0 4.6 %collective-permute-start.10 = (bf16[1,128,256]{2,1,0:T(8,128)(2,1)S(1)}, bf16[1,128,256]{2,1,0:T(8,128)(2,1)S(1)}, u32[]{:S(2)}, u32[]{:S(2)}) collective-permute-start(bf16[1,128,256]{2,1,0:T(8,128)(2,1)S(1)} %get-tuple-element.19), channel_id=1, source_target_pairs={{0,4},{1,5},{2,6},{3,7},{4,0},{5,1},{6,2},{7,3},{8,12},{9,13},{10,... | collective-permute-start | bytes 196616 | tf_op jit(solution)/shard_map/ppermute | solution.py:20
  25.6 5.2 %collective-permute-start.11 = (bf16[1,128,256]{2,1,0:T(8,128)(2,1)S(1)}, bf16[1,128,256]{2,1,0:T(8,128)(2,1)S(1)}, u32[]{:S(2)}, u32[]{:S(2)}) collective-permute-start(bf16[1,128,256]{2,1,0:T(8,128)(2,1)S(1)} %get-tuple-element.20), channel_id=1, source_target_pairs={{0,6},{1,7},{2,4},{3,5},{4,2},{5,3},{6,0},{7,1},{8,14},{9,15},{10,... | collective-permute-start | bytes 196616 | tf_op jit(solution)/shard_map/ppermute | solution.py:20

commit v2 on v1

v2 whole, which is shorter than its diff:
```python
import functools

import jax
import jax.numpy as jnp
from jax import lax
from jax.experimental import pallas as pl
from jax.experimental.pallas import tpu as pltpu
from jax.sharding import PartitionSpec as P

W = 64
BF = jnp.bfloat16
F32 = jnp.float32
VMEM = pl.BlockSpec(memory_space=pltpu.VMEM)
SMEM = pl.BlockSpec(memory_space=pltpu.SMEM)
LIMIT = 32 * 2**20


def swap(block, mask):
    count = lax.axis_size("rows")
    return lax.ppermute(block, "rows", [(i, i ^ mask) for i in range(count)])


def local(body, outs, scratch, flops, moved, me, *args, ):
    return pl.pallas_call(
        body,
        out_shape=outs,
        in_specs=[SMEM] + [VMEM] * len(args),
        out_specs=jax.tree.map(lambda _: VMEM, outs),
        scratch_shapes=scratch,
        compiler_params=pltpu.CompilerParams(vmem_limit_bytes=LIMIT),
        cost_estimate=pl.CostEstimate(flops=flops, bytes_accessed=moved, transcendentals=0),
    )(me, *args)


def phase_groups(phase):
    if phase == 0:
        return [(-1, (0,)), (0, (1, 2))]
    return [(0, (0, 1)), (1, (2,))]


def shift_cols(plane, step):
    if step == 0:
        return plane
    voxels = plane.shape[0]
    col = lax.broadcasted_iota(jnp.int32, plane.shape, 0) % W
    rolled = pltpu.roll(plane, (-step) % voxels, 0)
    return jnp.where((col + step >= 0) & (col + step < W), rolled, 0)


def shift_rows(plane, step):
    if step == 0:
        return plane
    zeros = jnp.zeros((W,) + plane.shape[1:], plane.dtype)
    if step > 0:
        return jnp.concatenate([plane[W:], zeros], 0)
    return jnp.concatenate([zeros, plane[:-W]], 0)


def phase_body(me_ref, *refs):
    pairs = len(refs) // 2
    upper = me_ref[0] % 2 == 1
    for tiles_ref, out_ref in zip(refs[:pairs], refs[pairs:], strict=True):
        taps = [tiles_ref[t].astype(F32).T for t in range(9)]
        depth = taps[0].shape[0]
        for q in range(2):
            place = 0
            for u in range(2):
                for _, col_taps in phase_groups(q):
                    rows = slice(place * depth, (place + 1) * depth)
                    place += 1
                    totals = []
                    for p in range(2):
                        total = None
                        for b in phase_groups(p)[u][1]:
                            for e in col_taps:
                                tap = taps[3 * b + e]
                                total = tap if total is None else total + tap
                        totals.append(total)
                    if out_ref.shape[0] == 1:
                        totals = [jnp.where(upper, totals[1], totals[0])]
                    for p, total in enumerate(totals):
                        out_ref[p, q, rows, :] = total.astype(BF)


def conv_body(share, masks, first, last, me_ref, *refs):
    refs = list(refs)
    before_ref = None if first else refs.pop(0)
    weight_ref = refs.pop(0)
    pieces = [refs.pop(0) for _ in masks or (0,)]
    *out_refs, order_ref, columns_ref = refs
    frames_of, channels, voxels = order_ref.shape
    if masks:
        part = weight_ref.shape[1] // share
        me = me_ref[0] % share
        spans = []
        for i, mask in enumerate(masks):
            order_ref[:, i * part : (i + 1) * part, :] = pieces[i][...]
            spans.append(pl.ds(pl.multiple_of((me ^ mask) * part, part), part))
    else:
        order_ref[...] = pieces[0][...]
        spans = [slice(None)]
    for a in range(frames_of):
        columns_ref[:, a * channels : (a + 1) * channels] = order_ref[a].T
    products = [None] * 9
    for low in range(0, 9, 2):
        pair = range(low, min(low + 2, 9))
        weights = jnp.concatenate(
            [
                jnp.concatenate(
                    [weight_ref[9 * a + t, span, :] for a in range(frames_of) for span in spans], 0
                )
                for t in pair
            ],
            1,
        )
        product = jnp.dot(columns_ref[...], weights, preferred_element_type=F32)
        filters = product.shape[1] // len(pair)
        for i, t in enumerate(pair):
            own = product[:, i * filters : (i + 1) * filters]
            products[t] = own if first else before_ref[t] + own
    if not last:
        for t in range(9):
            out_refs[0][t] = products[t]
        return
    total = None
    for e in range(3):
        rows = sum(shift_rows(products[3 * b + e], b - 1) for b in range(3))
        moved = shift_cols(rows, e - 1)
        total = moved if total is None else total + moved
    out_refs[0][...] = total
    out_refs[1][...] = total.astype(BF)


def silu_body(me_ref, *refs):
    *sum_refs, hidden_ref = refs
    pre = sum_refs[0][...]
    for other_ref in sum_refs[1:]:
        pre = pre + other_ref[...].astype(F32)
    hidden_ref[...] = (pre / (1 + jnp.exp(-pre))).astype(BF)


def up_products(me_ref, hidden_ref, weight_ref, padded_ref, halves, lines):
    hidden = hidden_ref[...].astype(F32)
    voxels = hidden.shape[0]
    for i, v in enumerate((-1, 0, 1)):
        edge = jnp.zeros((W, hidden.shape[1]), BF)
        padded_ref[i, :W, :] = edge
        padded_ref[i, W + voxels :, :] = edge
        padded_ref[i, W : W + voxels, :] = shift_cols(hidden, v).astype(BF)
    upper = me_ref[0] % 2
    if lines == 1:
        blocks = [(0, halves, upper, [(half, 0) for half in range(halves)])]
    else:
        blocks = [
            (
                p,
                lines // 2,
                half * lines + upper * (lines // 2) + p,
                [(half, 2 * i + p) for i in range(lines // 2)],
            )
            for half in range(halves)
            for p in range(2)
        ]
    for p, count, base, places in blocks:
        for q in range(2):
            columns = []
            for u in range(2):
                start = pl.multiple_of((base + u) * W, W)
                for v, _ in phase_groups(q):
                    columns.append(padded_ref[v + 1, pl.ds(start, count * W), :])
            product = jnp.dot(
                jnp.concatenate(columns, 1), weight_ref[p, q], preferred_element_type=F32
            )
            for i, (half, k) in enumerate(places):
                yield half, k, slice(q * W, (q + 1) * W), product[i * W : (i + 1) * W]


def up_first_body(me_ref, hidden_ref, weight_ref, out_ref, padded_ref):
    halves, lines = out_ref.shape[:2]
    for half, k, cells, value in up_products(
        me_ref, hidden_ref, weight_ref, padded_ref, halves, lines
    ):
        out_ref[half, k, cells, :] = value


def up_second_body(me_ref, before_ref, hidden_ref, weight_ref, *refs):
    *out_refs, total_ref, padded_ref = refs
    halves, lines = before_ref.shape[:2]
    for half, k, cells, value in up_products(
        me_ref, hidden_ref, weight_ref, padded_ref, halves, lines
    ):
        total_ref[half, k, cells, :] = before_ref[half, k, cells, :] + value
    chip = me_ref[0] // 2 % halves
    for mask, out_ref in enumerate(out_refs):
        out_ref[...] = total_ref[chip ^ mask].astype(out_ref.dtype)


def final_body(me_ref, own_ref, *refs):
    *other_refs, out_ref = refs
    total = own_ref[...]
    for other_ref in other_refs:
        total = total + other_ref[...].astype(F32)
    total = total.astype(BF)
    cell = lax.broadcasted_iota(jnp.int32, (2 * W, 2 * W), 0)
    place = lax.broadcasted_iota(jnp.int32, (2 * W, 2 * W), 1)
    spread = (place == 2 * (cell % W) + cell // W).astype(BF)
    for k in range(total.shape[0]):
        woven = lax.dot_general(
            total[k], spread, (((0,), (0,)), ((), ())), preferred_element_type=F32
        )
        out_ref[0, :, k * 2 * W : (k + 1) * 2 * W] = woven.astype(BF)


def on_device(frames, conv_tiles, up_tiles):
    index = lax.axis_index("rows")
    me = index.reshape(1).astype(jnp.int32)
    count = lax.axis_size("rows")
    part, frames_of, voxels = frames.shape
    taps, channels, filters = conv_tiles.shape[1:]
    outputs = up_tiles.shape[2]
    share = channels // part
    blocks = count // share
    halves = share // 2
    lines = 2 * (voxels // W) // share
    shape = jax.ShapeDtypeStruct

    mine = frames.transpose(1, 0, 2)
    pieces = [mine, swap(mine, 1)] + [None] * (share - 2)
    for mask in range(2, share, 2):
        pieces[mask] = swap(mine, mask)
    tiles = up_tiles[0]
    weights = conv_tiles[0]
    if part % 16:
        for mask in range(2, share, 2):
            pieces[mask + 1] = swap(pieces[mask], 1)
        for mask in [1 << level for level in range(share.bit_length() - 1)]:
            pieces = [
                jnp.where(index & mask != 0, pieces[j ^ mask], pieces[j]) for j in range(share)
            ]
        steps = [()]
        pieces = [jnp.concatenate(pieces, 1)]
    else:
        far = share - 2
        near = list(range(2, far, 2))
        steps = [(0,), (1, far, far + 1, *near), tuple(mask + 1 for mask in near)]

    before = []
    for i, masks in enumerate(steps):
        first, last = i == 0, i == len(steps) - 1
        parts = [pieces[mask] for mask in masks] or pieces
        depth = sum(block.shape[1] for block in parts)
        outs = [shape((voxels, filters), F32), shape((voxels, filters), BF)]
        if not last:
            outs = [shape((9, voxels, filters), F32)]
        scratch = [
            pltpu.VMEM((frames_of, depth, voxels), BF),
            pltpu.VMEM((voxels, frames_of * depth), BF),
        ]
        done = local(
            functools.partial(conv_body, share, masks, first, last),
            tuple(outs),
            scratch,
            2 * taps * depth * filters * voxels,
            2 * taps * depth * filters,
            me,
            *before,
            weights,
            *parts,
        )
        before = done[:1]
        if first and not last:
            pieces[far], *before = lax.optimization_barrier((pieces[far], *before))
            for mask in range(2, share, 2):
                pieces[mask + 1] = swap(pieces[mask], 1)
    partial, sent = done
    partial, tiles = lax.optimization_barrier((partial, tiles))
    mate_tiles = swap(tiles, 1)
    others = [swap(sent, share * block) for block in range(1, blocks)]
    some = (min(lines, 2), 2, 4 * filters, outputs)
    keep, mate_phases = local(
        phase_body,
        (shape(some, BF), shape(some, BF)),
        [],
        64 * filters * outputs,
        68 * filters * outputs,
        me,
        up_tiles[0],
        mate_tiles,
    )
    hidden = local(
        silu_body,
        shape((voxels, filters), BF),
        [],
        8 * voxels * filters,
        8 * voxels * filters,
        me,
        partial,
        *others,
    )
    mate_hidden = swap(hidden, 1)
    one = (lines, 2 * W, outputs)
    padded = pltpu.VMEM((3, voxels + 2 * W, filters), BF)
    work = 16 * filters * outputs * voxels
    first = local(
        up_first_body,
        shape((halves, *one), F32),
        [padded],
        work,
        16 * filters * outputs,
        me,
        hidden,
        keep,
    )
    own, *leaving = local(
        up_second_body,
        (shape(one, F32),) + (shape(one, BF),) * (halves - 1),
        [pltpu.VMEM((halves, *one), F32), padded],
        work,
        16 * filters * outputs,
        me,
        first,
        mate_hidden,
        mate_phases,
    )
    arrived = [swap(block, 2 * (mask + 1)) for mask, block in enumerate(leaving)]
    return local(
        final_body,
        shape((1, outputs, lines * 2 * W), BF),
        [],
        own.size,
        12 * own.size,
        me,
        own,
        *arrived,
    )


def solution(mesh):
    return jax.shard_map(
        on_device,
        mesh=mesh,
        in_specs=(
            P(("groups", "rows"), None, None),
            P("rows", None, None, None),
            P("rows", None, None, None),
        ),
        out_specs=P(("groups", "rows"), None, None),
        check_vma=False,
    )
```

time: 31.8 us -> 29 us (0.912)
  waiting for transfers between devices: 14.4 us -> 8.92 us
  Pallas kernels: 2.88 us -> 4.2 us
  starting transfers between devices: 11.4 us -> 12.2 us
  local copies, waits for them, and re-layouts: 2.9 us -> 3.38 us
    ppermute x12 -> x13, waiting for transfers between devices: 14.4 us -> 8.92 us  [swap(): return lax.ppermute(block, 'rows', [(i, i ^ mask) for i in range(count)])]
    pallas_call x5 -> x8, Pallas kernels: 2.88 us -> 4.2 us  [local(): pl.pallas_call(body, out_shape=outs, in_specs=[SMEM] + [VMEM] * len(args)...]
    ppermute x12 -> x13, starting transfers between devices: 11.4 us -> 12.2 us  [swap(): return lax.ppermute(block, 'rows', [(i, i ^ mask) for i in range(count)])]
    unnamed x6, local copies, waits for them, and re-layouts: 2.9 us -> 3.38 us
  transfers between devices with their start and end apart: 12 -> 13, of which waited for: 9 -> 7; matrix products, arithmetic and copies ran while one was open for 0% -> 0% of each run, Pallas kernels for 1% -> 9%
where the time goes in v2:
time: 29 us; the launch traced here: 28.8 us
  starting transfers between devices  12.2 us (42%)
  waiting for transfers between devices  8.92 us (31%)
  Pallas kernels  4.2 us (14%)
  local copies, waits for them, and re-layouts  3.38 us (12%)
    ppermute x13, starting transfers between devices, swap(): return lax.ppermute(block, 'rows', [(i, i ^ mask) for i in range(count)])  12.2 us
    ppermute x13, waiting for transfers between devices, swap(): return lax.ppermute(block, 'rows', [(i, i ^ mask) for i in range(count)])  8.92 us
    pallas_call x8, Pallas kernels, local(): pl.pallas_call(body, out_shape=outs, in_specs=[SMEM] + [VMEM] * len(args)...  4.2 us
    unnamed x6, local copies, waits for them, and re-layouts  3.38 us
  transfers between devices with their start and end apart: 13, of which 7 were waited for; matrix products, arithmetic and copies ran while one was open for 0% of the time, Pallas kernels for 9%

profile of v2, /device:TPU:0, one launch (start us, length us, event | category | flops | bytes accessed | tf_op | source)
XLA Modules:
  0.0 28.8 jit_solution(2084096004662168553)
XLA Ops:
  0.0 4.0 %collective-permute-start = (bf16[3,64,256]{2,1,0:T(8,128)(2,1)}, bf16[3,64,256]{2,1,0:T(8,128)(2,1)S(1)}, u32[]{:S(2)}, u32[]{:S(2)}) collective-permute-start(bf16[3,64,256]{2,1,0:T(8,128)(2,1)} %bitcast.9), channel_id=1, source_target_pairs={{0,6},{1,7},{2,4},{3,5},{4,2},{5,3},{6,0},{7,1},{8,14},{9,15},{10,... | collective-permute-start | bytes 294920 | tf_op jit(solution)/shard_map/ppermute | solution.py:20
  4.0 0.5 %collective-permute-start.3 = (bf16[3,64,256]{2,1,0:T(8,128)(2,1)}, bf16[3,64,256]{2,1,0:T(8,128)(2,1)S(1)}, u32[]{:S(2)}, u32[]{:S(2)}) collective-permute-start(bf16[3,64,256]{2,1,0:T(8,128)(2,1)} %bitcast.10), channel_id=1, source_target_pairs={{0,2},{1,3},{2,0},{3,1},{4,6},{5,7},{6,4},{7,5},{8,10},{9,11},{10,... | collective-permute-start | bytes 294920 | tf_op jit(solution)/shard_map/ppermute | solution.py:20
  4.5 0.1 collective-permute-start.4
  4.5 0.0 collective-permute-start.1
  4.6 2.0 %copy-done = bf16[1,27,512,128]{3,2,1,0:T(8,128)(2,1)S(1)} copy-done((bf16[1,27,512,128]{3,2,1,0:T(8,128)(2,1)S(1)}, bf16[1,27,512,128]{3,2,1,0:T(8,128)(2,1)}, u32[]{:S(2)}) %copy-start) | copy-done | bytes 3538968
  6.6 0.9 %copy-done.2 = bf16[64,3,256]{2,0,1:T(8,128)(2,1)S(1)} copy-done((bf16[64,3,256]{2,0,1:T(8,128)(2,1)S(1)}, bf16[64,3,256]{2,0,1:T(8,128)(2,1)}, u32[]{:S(2)}) %copy-start.2) | copy-done | bytes 98328
  7.4 0.5 %shard_map.37.refs_0_ = f32[9,256,128]{2,1,0:T(8,128)S(1)} custom-call(s32[1]{0:T(128)} %bitcast.me_ref, bf16[27,512,128]{2,1,0:T(8,128)(2,1)S(1)} %bitcast.4, bf16[3,64,256]{2,1,0:T(8,128)(2,1)S(1)} %bitcast.13), custom_call_target="tpu_custom_call" | custom-call | flops 113246208 | bytes 442368 | tf_op jit(solution)/shard_map/pallas_call | solution.py:24
  7.9 0.6 %collective-permute-start.2 = (bf16[3,64,256]{2,1,0:T(8,128)(2,1)S(1)}, bf16[3,64,256]{2,1,0:T(8,128)(2,1)S(1)}, u32[]{:S(2)}, u32[]{:S(2)}) collective-permute-start(bf16[3,64,256]{2,1,0:T(8,128)(2,1)S(1)} %collective-permute-done.refs_3_), channel_id=1, source_target_pairs={{0,1},{1,0},{2,3},{3,2},{4,5},{5,4},{6,7},{7,6},{8,9},{9,8},{10,11... | collective-permute-start | bytes 294920 | tf_op jit(solution)/shard_map/ppermute | solution.py:20
  8.5 0.6 %collective-permute-done.3.refs_5_ = bf16[3,64,256]{2,1,0:T(8,128)(2,1)S(1)} collective-permute-done((bf16[3,64,256]{2,1,0:T(8,128)(2,1)}, bf16[3,64,256]{2,1,0:T(8,128)(2,1)S(1)}, u32[]{:S(2)}, u32[]{:S(2)}) %collective-permute-start.3) | collective-permute-done | bytes 98336 | tf_op jit(solution)/shard_map/ppermute | solution.py:20
  9.1 0.0 collective-permute-start.5
  9.1 0.2 collective-permute-done.4.refs_6_
  9.3 0.3 collective-permute-start.6
  9.6 1.1 %shard_map.38.refs_0_ = f32[9,256,128]{2,1,0:T(8,128)S(1)} custom-call(s32[1]{0:T(128)} %bitcast.me_ref, f32[9,256,128]{2,1,0:T(8,128)S(1)} %shard_map.37.refs_0_, bf16[27,512,128]{2,1,0:T(8,128)(2,1)S(1)} %bitcast.5, bf16[3,64,256]{2,1,0:T(8,128)(2,1)S(1)} %collective-permute-done.1.refs_2_, bf16[3,64,256]{2,1,0:T(8,128)(2,1)S(1)} %collective-permute-done.refs_3_, ...), custom_call_target="tpu_custom_call" | custom-call | flops 566231040 | bytes 2211840 | tf_op jit(solution)/shard_map/pallas_call | solution.py:24
  10.7 0.0 copy-start.1
  10.7 0.0 collective-permute-done.5.refs_2_
  10.7 0.5 %shard_map.39 = (f32[256,128]{1,0:T(8,128)S(1)}, bf16[256,128]{1,0:T(8,128)(2,1)S(1)}) custom-call(s32[1]{0:T(128)} %bitcast.me_ref, f32[9,256,128]{2,1,0:T(8,128)S(1)} %shard_map.38.refs_0_, bf16[27,512,128]{2,1,0:T(8,128)(2,1)S(1)} %bitcast.6, bf16[3,64,256]{2,1,0:T(8,128)(2,1)S(1)} %collective-permute-done.5.refs_2_, ...), custom_call_target="tpu_custom_call" | custom-call | flops 226492416 | bytes 884736 | tf_op jit(solution)/shard_map/pallas_call | solution.py:24
  11.3 0.5 %copy-done.1 = bf16[1,9,256,128]{3,2,1,0:T(8,128)(2,1)S(1)} copy-done((bf16[1,9,256,128]{3,2,1,0:T(8,128)(2,1)S(1)}, bf16[1,9,256,128]{3,2,1,0:T(8,128)(2,1)}, u32[]{:S(2)}) %copy-start.1) | copy-done | bytes 589848
  11.8 0.3 collective-permute-start.8
  12.0 2.9 %collective-permute-start.7 = (bf16[256,128]{1,0:T(8,128)(2,1)S(1)}, bf16[256,128]{1,0:T(8,128)(2,1)S(1)}, u32[]{:S(2)}, u32[]{:S(2)}) collective-permute-start(bf16[256,128]{1,0:T(8,128)(2,1)S(1)} %get-tuple-element.21), channel_id=1, source_target_pairs={{0,8},{1,9},{2,10},{3,11},{4,12},{5,13},{6,14},{7,15},{8,0},{9,1},... | collective-permute-start | bytes 196616 | tf_op jit(solution)/shard_map/ppermute | solution.py:20
  14.9 3.8 %collective-permute-done.7.refs_1_ = bf16[256,128]{1,0:T(8,128)(2,1)S(1)} collective-permute-done((bf16[256,128]{1,0:T(8,128)(2,1)S(1)}, bf16[256,128]{1,0:T(8,128)(2,1)S(1)}, u32[]{:S(2)}, u32[]{:S(2)}) %collective-permute-start.7) | collective-permute-done | bytes 65568 | tf_op jit(solution)/shard_map/ppermute | solution.py:20
  18.8 0.1 collective-permute-start.9
  18.9 0.5 %shard_map.41 = (bf16[1,2,512,256]{3,2,1,0:T(8,128)(2,1)S(1)}, bf16[1,2,512,256]{3,2,1,0:T(8,128)(2,1)S(1)}) custom-call(s32[1]{0:T(128)} %bitcast.me_ref, bf16[9,256,128]{2,1,0:T(8,128)(2,1)S(1)} %bitcast.8, bf16[9,256,128]{2,1,0:T(8,128)(2,1)S(1)} %collective-permute-done.8.refs_1_), custom_call_target="tpu_custom_call" | custom-call | flops 2097152 | bytes 2228224 | tf_op jit(solution)/shard_map/pallas_call | solution.py:24
  19.4 0.3 %shard_map.42.before_ref = f32[4,1,128,256]{3,2,1,0:T(8,128)S(1)} custom-call(s32[1]{0:T(128)} %bitcast.me_ref, bf16[256,128]{1,0:T(8,128)(2,1)S(1)} %shard_map.40.hidden_ref, bf16[1,2,512,256]{3,2,1,0:T(8,128)(2,1)S(1)} %get-tuple-element.23.weight_ref), custom_call_target="tpu_custom_call" | custom-call | flops 134217728 | bytes 524288 | tf_op jit(solution)/shard_map/pallas_call | solution.py:24
  19.8 0.4 %collective-permute-done.9.hidden_ref = bf16[256,128]{1,0:T(8,128)(2,1)S(1)} collective-permute-done((bf16[256,128]{1,0:T(8,128)(2,1)S(1)}, bf16[256,128]{1,0:T(8,128)(2,1)S(1)}, u32[]{:S(2)}, u32[]{:S(2)}) %collective-permute-start.9) | collective-permute-done | bytes 65568 | tf_op jit(solution)/shard_map/ppermute | solution.py:20
  20.1 0.4 %shard_map.43 = (f32[1,128,256]{2,1,0:T(8,128)S(1)}, bf16[1,128,256]{2,1,0:T(8,128)(2,1)S(1)}, bf16[1,128,256]{2,1,0:T(8,128)(2,1)S(1)}, bf16[1,128,256]{2,1,0:T(8,128)(2,1)S(1)}) custom-call(s32[1]{0:T(128)} %bitcast.me_ref, f32[4,1,128,256]{3,2,1,0:T(8,128)S(1)} %shard_map.42.before_ref, bf16[256,128]{1,0:T(8,128)(2,1)S(1)} %collective-permute-done.9.hidden_ref, ...), custom_call_target="tpu_custom_call" | custom-call | flops 134217728 | bytes 524288 | tf_op jit(solution)/shard_map/pallas_call | solution.py:24
  20.5 1.8 %collective-permute-start.10 = (bf16[1,128,256]{2,1,0:T(8,128)(2,1)S(1)}, bf16[1,128,256]{2,1,0:T(8,128)(2,1)S(1)}, u32[]{:S(2)}, u32[]{:S(2)}) collective-permute-start(bf16[1,128,256]{2,1,0:T(8,128)(2,1)S(1)} %get-tuple-element.26), channel_id=1, source_target_pairs={{0,2},{1,3},{2,0},{3,1},{4,6},{5,7},{6,4},{7,5},{8,10},{9,11},{10,... | collective-permute-start | bytes 196616 | tf_op jit(solution)/shard_map/ppermute | solution.py:20
  22.2 0.6 %collective-permute-start.11 = (bf16[1,128,256]{2,1,0:T(8,128)(2,1)S(1)}, bf16[1,128,256]{2,1,0:T(8,128)(2,1)S(1)}, u32[]{:S(2)}, u32[]{:S(2)}) collective-permute-start(bf16[1,128,256]{2,1,0:T(8,128)(2,1)S(1)} %get-tuple-element.27), channel_id=1, source_target_pairs={{0,4},{1,5},{2,6},{3,7},{4,0},{5,1},{6,2},{7,3},{8,12},{9,13},{10,... | collective-permute-start | bytes 196616 | tf_op jit(solution)/shard_map/ppermute | solution.py:20
  22.8 1.2 %collective-permute-start.12 = (bf16[1,128,256]{2,1,0:T(8,128)(2,1)S(1)}, bf16[1,128,256]{2,1,0:T(8,128)(2,1)S(1)}, u32[]{:S(2)}, u32[]{:S(2)}) collective-permute-start(bf16[1,128,256]{2,1,0:T(8,128)(2,1)S(1)} %get-tuple-element.28), channel_id=1, source_target_pairs={{0,6},{1,7},{2,4},{3,5},{4,2},{5,3},{6,0},{7,1},{8,14},{9,15},{10,... | collective-permute-start | bytes 196616 | tf_op jit(solution)/shard_map/ppermute | solution.py:20
  24.1 0.8 %collective-permute-done.10.refs_0_ = bf16[1,128,256]{2,1,0:T(8,128)(2,1)S(1)} collective-permute-done((bf16[1,128,256]{2,1,0:T(8,128)(2,1)S(1)}, bf16[1,128,256]{2,1,0:T(8,128)(2,1)S(1)}, u32[]{:S(2)}, u32[]{:S(2)}) %collective-permute-start.10) | collective-permute-done | bytes 65568 | tf_op jit(solution)/shard_map/ppermute | solution.py:20
  24.8 2.0 %collective-permute-done.11.refs_1_ = bf16[1,128,256]{2,1,0:T(8,128)(2,1)S(1)} collective-permute-done((bf16[1,128,256]{2,1,0:T(8,128)(2,1)S(1)}, bf16[1,128,256]{2,1,0:T(8,128)(2,1)S(1)}, u32[]{:S(2)}, u32[]{:S(2)}) %collective-permute-start.11) | collective-permute-done | bytes 65568 | tf_op jit(solution)/shard_map/ppermute | solution.py:20
  26.8 1.1 %collective-permute-done.12.refs_2_ = bf16[1,128,256]{2,1,0:T(8,128)(2,1)S(1)} collective-permute-done((bf16[1,128,256]{2,1,0:T(8,128)(2,1)S(1)}, bf16[1,128,256]{2,1,0:T(8,128)(2,1)S(1)}, u32[]{:S(2)}, u32[]{:S(2)}) %collective-permute-start.12) | collective-permute-done | bytes 65568 | tf_op jit(solution)/shard_map/ppermute | solution.py:20
  28.0 0.8 %shard_map.44 = bf16[1,256,128]{2,1,0:T(8,128)(2,1)} custom-call(s32[1]{0:T(128)} %bitcast.me_ref, f32[1,128,256]{2,1,0:T(8,128)S(1)} %get-tuple-element.25.own_ref, bf16[1,128,256]{2,1,0:T(8,128)(2,1)S(1)} %collective-permute-done.10.refs_0_, bf16[1,128,256]{2,1,0:T(8,128)(2,1)S(1)} %collective-permute-done.11.refs_1_, ...), custom_call_target="tpu_custom_call" | custom-call | flops 32768 | bytes 393216 | tf_op jit(solution)/shard_map/pallas_call | solution.py:24
  (8 shorter events, 0.1 us)
Async XLA Ops:
  0.0 7.9 %collective-permute-start = (bf16[3,64,256]{2,1,0:T(8,128)(2,1)}, bf16[3,64,256]{2,1,0:T(8,128)(2,1)S(1)}, u32[]{:S(2)}, u32[]{:S(2)}) collective-permute-start(bf16[3,64,256]{2,1,0:T(8,128)(2,1)} %bitcast.9), channel_id=1, source_target_pairs={{0,6},{1,7},{2,4},{3,5},{4,2},{5,3},{6,0},{7,1},{8,14},{9,15},{10,... | collective-permute-start | bytes 294920 | tf_op jit(solution)/shard_map/ppermute | solution.py:20
  4.0 5.1 %collective-permute-start.3 = (bf16[3,64,256]{2,1,0:T(8,128)(2,1)}, bf16[3,64,256]{2,1,0:T(8,128)(2,1)S(1)}, u32[]{:S(2)}, u32[]{:S(2)}) collective-permute-start(bf16[3,64,256]{2,1,0:T(8,128)(2,1)} %bitcast.10), channel_id=1, source_target_pairs={{0,2},{1,3},{2,0},{3,1},{4,6},{5,7},{6,4},{7,5},{8,10},{9,11},{10,... | collective-permute-start | bytes 294920 | tf_op jit(solution)/shard_map/ppermute | solution.py:20
  4.5 4.8 %collective-permute-start.4 = (bf16[3,64,256]{2,1,0:T(8,128)(2,1)}, bf16[3,64,256]{2,1,0:T(8,128)(2,1)S(1)}, u32[]{:S(2)}, u32[]{:S(2)}) collective-permute-start(bf16[3,64,256]{2,1,0:T(8,128)(2,1)} %bitcast.11), channel_id=1, source_target_pairs={{0,4},{1,5},{2,6},{3,7},{4,0},{5,1},{6,2},{7,3},{8,12},{9,13},{10,... | collective-permute-start | bytes 294920 | tf_op jit(solution)/shard_map/ppermute | solution.py:20
  4.5 5.1 %collective-permute-start.1 = (bf16[3,64,256]{2,1,0:T(8,128)(2,1)}, bf16[3,64,256]{2,1,0:T(8,128)(2,1)S(1)}, u32[]{:S(2)}, u32[]{:S(2)}) collective-permute-start(bf16[3,64,256]{2,1,0:T(8,128)(2,1)} %bitcast.12), channel_id=1, source_target_pairs={{0,1},{1,0},{2,3},{3,2},{4,5},{5,4},{6,7},{7,6},{8,9},{9,8},{10,11... | collective-permute-start | bytes 294920 | tf_op jit(solution)/shard_map/ppermute | solution.py:20
  4.6 2.0 %copy-start = (bf16[1,27,512,128]{3,2,1,0:T(8,128)(2,1)S(1)}, bf16[1,27,512,128]{3,2,1,0:T(8,128)(2,1)}, u32[]{:S(2)}) copy-start(bf16[1,27,512,128]{3,2,1,0:T(8,128)(2,1)} %param.4) | copy-start | bytes 10616836
  6.6 0.9 %copy-start.2 = (bf16[64,3,256]{2,0,1:T(8,128)(2,1)S(1)}, bf16[64,3,256]{2,0,1:T(8,128)(2,1)}, u32[]{:S(2)}) copy-start(bf16[64,3,256]{2,0,1:T(8,128)(2,1)} %param.3) | copy-start | bytes 294916
  7.9 1.7 %collective-permute-start.2 = (bf16[3,64,256]{2,1,0:T(8,128)(2,1)S(1)}, bf16[3,64,256]{2,1,0:T(8,128)(2,1)S(1)}, u32[]{:S(2)}, u32[]{:S(2)}) collective-permute-start(bf16[3,64,256]{2,1,0:T(8,128)(2,1)S(1)} %collective-permute-done.refs_3_), channel_id=1, source_target_pairs={{0,1},{1,0},{2,3},{3,2},{4,5},{5,4},{6,7},{7,6},{8,9},{9,8},{10,11... | collective-permute-start | bytes 294920 | tf_op jit(solution)/shard_map/ppermute | solution.py:20
  9.1 1.6 %collective-permute-start.5 = (bf16[3,64,256]{2,1,0:T(8,128)(2,1)S(1)}, bf16[3,64,256]{2,1,0:T(8,128)(2,1)S(1)}, u32[]{:S(2)}, u32[]{:S(2)}) collective-permute-start(bf16[3,64,256]{2,1,0:T(8,128)(2,1)S(1)} %collective-permute-done.3.refs_5_), channel_id=1, source_target_pairs={{0,1},{1,0},{2,3},{3,2},{4,5},{5,4},{6,7},{7,6},{8,9},{9,8},{10,11... | collective-permute-start | bytes 294920 | tf_op jit(solution)/shard_map/ppermute | solution.py:20
  9.3 1.4 %collective-permute-start.6 = (bf16[3,64,256]{2,1,0:T(8,128)(2,1)S(1)}, bf16[3,64,256]{2,1,0:T(8,128)(2,1)S(1)}, u32[]{:S(2)}, u32[]{:S(2)}) collective-permute-start(bf16[3,64,256]{2,1,0:T(8,128)(2,1)S(1)} %collective-permute-done.4.refs_6_), channel_id=1, source_target_pairs={{0,1},{1,0},{2,3},{3,2},{4,5},{5,4},{6,7},{7,6},{8,9},{9,8},{10,11... | collective-permute-start | bytes 294920 | tf_op jit(solution)/shard_map/ppermute | solution.py:20
  10.7 1.1 %copy-start.1 = (bf16[1,9,256,128]{3,2,1,0:T(8,128)(2,1)S(1)}, bf16[1,9,256,128]{3,2,1,0:T(8,128)(2,1)}, u32[]{:S(2)}) copy-start(bf16[1,9,256,128]{3,2,1,0:T(8,128)(2,1)} %param.5) | copy-start | bytes 1769476
  11.8 7.1 %collective-permute-start.8 = (bf16[9,256,128]{2,1,0:T(8,128)(2,1)S(1)}, bf16[9,256,128]{2,1,0:T(8,128)(2,1)S(1)}, u32[]{:S(2)}, u32[]{:S(2)}) collective-permute-start(bf16[9,256,128]{2,1,0:T(8,128)(2,1)S(1)} %bitcast.7), channel_id=1, source_target_pairs={{0,1},{1,0},{2,3},{3,2},{4,5},{5,4},{6,7},{7,6},{8,9},{9,8},{10,11... | collective-permute-start | bytes 1769480 | tf_op jit(solution)/shard_map/ppermute | solution.py:20
  12.0 6.8 %collective-permute-start.7 = (bf16[256,128]{1,0:T(8,128)(2,1)S(1)}, bf16[256,128]{1,0:T(8,128)(2,1)S(1)}, u32[]{:S(2)}, u32[]{:S(2)}) collective-permute-start(bf16[256,128]{1,0:T(8,128)(2,1)S(1)} %get-tuple-element.21), channel_id=1, source_target_pairs={{0,8},{1,9},{2,10},{3,11},{4,12},{5,13},{6,14},{7,15},{8,0},{9,1},... | collective-permute-start | bytes 196616 | tf_op jit(solution)/shard_map/ppermute | solution.py:20
  18.8 1.3 %collective-permute-start.9 = (bf16[256,128]{1,0:T(8,128)(2,1)S(1)}, bf16[256,128]{1,0:T(8,128)(2,1)S(1)}, u32[]{:S(2)}, u32[]{:S(2)}) collective-permute-start(bf16[256,128]{1,0:T(8,128)(2,1)S(1)} %shard_map.40.hidden_ref), channel_id=1, source_target_pairs={{0,1},{1,0},{2,3},{3,2},{4,5},{5,4},{6,7},{7,6},{8,9},{9,8},{10,11... | collective-permute-start | bytes 196616 | tf_op jit(solution)/shard_map/ppermute | solution.py:20
  20.5 4.3 %collective-permute-start.10 = (bf16[1,128,256]{2,1,0:T(8,128)(2,1)S(1)}, bf16[1,128,256]{2,1,0:T(8,128)(2,1)S(1)}, u32[]{:S(2)}, u32[]{:S(2)}) collective-permute-start(bf16[1,128,256]{2,1,0:T(8,128)(2,1)S(1)} %get-tuple-element.26), channel_id=1, source_target_pairs={{0,2},{1,3},{2,0},{3,1},{4,6},{5,7},{6,4},{7,5},{8,10},{9,11},{10,... | collective-permute-start | bytes 196616 | tf_op jit(solution)/shard_map/ppermute | solution.py:20
  22.2 4.6 %collective-permute-start.11 = (bf16[1,128,256]{2,1,0:T(8,128)(2,1)S(1)}, bf16[1,128,256]{2,1,0:T(8,128)(2,1)S(1)}, u32[]{:S(2)}, u32[]{:S(2)}) collective-permute-start(bf16[1,128,256]{2,1,0:T(8,128)(2,1)S(1)} %get-tuple-element.27), channel_id=1, source_target_pairs={{0,4},{1,5},{2,6},{3,7},{4,0},{5,1},{6,2},{7,3},{8,12},{9,13},{10,... | collective-permute-start | bytes 196616 | tf_op jit(solution)/shard_map/ppermute | solution.py:20
  22.8 5.2 %collective-permute-start.12 = (bf16[1,128,256]{2,1,0:T(8,128)(2,1)S(1)}, bf16[1,128,256]{2,1,0:T(8,128)(2,1)S(1)}, u32[]{:S(2)}, u32[]{:S(2)}) collective-permute-start(bf16[1,128,256]{2,1,0:T(8,128)(2,1)S(1)} %get-tuple-element.28), channel_id=1, source_target_pairs={{0,6},{1,7},{2,4},{3,5},{4,2},{5,3},{6,0},{7,1},{8,14},{9,15},{10,... | collective-permute-start | bytes 196616 | tf_op jit(solution)/shard_map/ppermute | solution.py:20

commit v3 on v2

--- a/solution.py
+++ b/solution.py
@@ -12,6 +12,7 @@
 F32 = jnp.float32
 VMEM = pl.BlockSpec(memory_space=pltpu.VMEM)
 SMEM = pl.BlockSpec(memory_space=pltpu.SMEM)
+HBM = pl.BlockSpec(memory_space=pltpu.HBM)
 LIMIT = 32 * 2**20
 
 
@@ -20,11 +21,11 @@
     return lax.ppermute(block, "rows", [(i, i ^ mask) for i in range(count)])
 
 
-def local(body, outs, scratch, flops, moved, me, *args, ):
+def local(body, outs, scratch, flops, moved, me, *args, in_hbm=()):
     return pl.pallas_call(
         body,
         out_shape=outs,
-        in_specs=[SMEM] + [VMEM] * len(args),
+        in_specs=[SMEM] + [HBM if i in in_hbm else VMEM for i in range(len(args))],
         out_specs=jax.tree.map(lambda _: VMEM, outs),
         scratch_shapes=scratch,
         compiler_params=pltpu.CompilerParams(vmem_limit_bytes=LIMIT),
@@ -56,30 +57,28 @@
     return jnp.concatenate([zeros, plane[:-W]], 0)
 
 
-def phase_body(me_ref, *refs):
-    pairs = len(refs) // 2
+def phase_body(me_ref, tiles_ref, out_ref):
     upper = me_ref[0] % 2 == 1
-    for tiles_ref, out_ref in zip(refs[:pairs], refs[pairs:], strict=True):
-        taps = [tiles_ref[t].astype(F32).T for t in range(9)]
-        depth = taps[0].shape[0]
-        for q in range(2):
-            place = 0
-            for u in range(2):
-                for _, col_taps in phase_groups(q):
-                    rows = slice(place * depth, (place + 1) * depth)
-                    place += 1
-                    totals = []
-                    for p in range(2):
-                        total = None
-                        for b in phase_groups(p)[u][1]:
-                            for e in col_taps:
-                                tap = taps[3 * b + e]
-                                total = tap if total is None else total + tap
-                        totals.append(total)
-                    if out_ref.shape[0] == 1:
-                        totals = [jnp.where(upper, totals[1], totals[0])]
-                    for p, total in enumerate(totals):
-                        out_ref[p, q, rows, :] = total.astype(BF)
+    taps = [tiles_ref[t].astype(F32).T for t in range(9)]
+    depth = taps[0].shape[0]
+    for q in range(2):
+        place = 0
+        for u in range(2):
+            for _, col_taps in phase_groups(q):
+                rows = slice(place * depth, (place + 1) * depth)
+                place += 1
+                totals = []
+                for p in range(2):
+                    total = None
+                    for b in phase_groups(p)[u][1]:
+                        for e in col_taps:
+                            tap = taps[3 * b + e]
+                            total = tap if total is None else total + tap
+                    totals.append(total)
+                if out_ref.shape[0] == 1:
+                    totals = [jnp.where(upper, totals[1], totals[0])]
+                for p, total in enumerate(totals):
+                    out_ref[p, q, rows, :] = total.astype(BF)
 
 
 def conv_body(share, masks, first, last, me_ref, *refs):
@@ -195,18 +194,21 @@
         out_ref[...] = total_ref[chip ^ mask].astype(out_ref.dtype)
 
 
-def final_body(me_ref, own_ref, *refs):
+def spread_body(me_ref, out_ref):
+    cell = lax.broadcasted_iota(jnp.int32, out_ref.shape, 0)
+    place = lax.broadcasted_iota(jnp.int32, out_ref.shape, 1)
+    out_ref[...] = (place == 2 * (cell % W) + cell // W).astype(BF)
+
+
+def final_body(me_ref, spread_ref, own_ref, *refs):
     *other_refs, out_ref = refs
     total = own_ref[...]
     for other_ref in other_refs:
         total = total + other_ref[...].astype(F32)
     total = total.astype(BF)
-    cell = lax.broadcasted_iota(jnp.int32, (2 * W, 2 * W), 0)
-    place = lax.broadcasted_iota(jnp.int32, (2 * W, 2 * W), 1)
-    spread = (place == 2 * (cell % W) + cell // W).astype(BF)
     for k in range(total.shape[0]):
         woven = lax.dot_general(
-            total[k], spread, (((0,), (0,)), ((), ())), preferred_element_type=F32
+            total[k], spread_ref[...], (((0,), (0,)), ((), ())), preferred_element_type=F32
         )
         out_ref[0, :, k * 2 * W : (k + 1) * 2 * W] = woven.astype(BF)
 
@@ -225,14 +227,21 @@
     shape = jax.ShapeDtypeStruct
 
     mine = frames.transpose(1, 0, 2)
-    pieces = [mine, swap(mine, 1)] + [None] * (share - 2)
+    pieces = [mine] + [None] * (share - 1)
+    far = share - 2
+    near = list(range(2, far, 2))
     for mask in range(2, share, 2):
         pieces[mask] = swap(mine, mask)
-    tiles = up_tiles[0]
+    spread = local(spread_body, shape((2 * W, 2 * W), BF), [], 2**33, 2**25, me)
+    mate_tiles = swap(up_tiles[0], 1)
+    pieces[far], spread, mate_tiles = lax.optimization_barrier(
+        (pieces[far], spread, mate_tiles)
+    )
+    pieces[0], spread = lax.optimization_barrier((mine, spread))
+    for mask in range(0, share, 2):
+        pieces[mask + 1] = swap(pieces[mask], 1)
     weights = conv_tiles[0]
     if part % 16:
-        for mask in range(2, share, 2):
-            pieces[mask + 1] = swap(pieces[mask], 1)
         for mask in [1 << level for level in range(share.bit_length() - 1)]:
             pieces = [
                 jnp.where(index & mask != 0, pieces[j ^ mask], pieces[j]) for j in range(share)
@@ -240,9 +249,7 @@
         steps = [()]
         pieces = [jnp.concatenate(pieces, 1)]
     else:
-        far = share - 2
-        near = list(range(2, far, 2))
-        steps = [(0,), (1, far, far + 1, *near), tuple(mask + 1 for mask in near)]
+        steps = [(0, 1, far, far + 1, *near), tuple(mask + 1 for mask in near)]
 
     before = []
     for i, masks in enumerate(steps):
@@ -268,25 +275,20 @@
             *parts,
         )
         before = done[:1]
-        if first and not last:
-            pieces[far], *before = lax.optimization_barrier((pieces[far], *before))
-            for mask in range(2, share, 2):
-                pieces[mask + 1] = swap(pieces[mask], 1)
     partial, sent = done
-    partial, tiles = lax.optimization_barrier((partial, tiles))
-    mate_tiles = swap(tiles, 1)
     others = [swap(sent, share * block) for block in range(1, blocks)]
-    some = (min(lines, 2), 2, 4 * filters, outputs)
-    keep, mate_phases = local(
+    phases = functools.partial(
+        local,
         phase_body,
-        (shape(some, BF), shape(some, BF)),
+        shape((min(lines, 2), 2, 4 * filters, outputs), BF),
         [],
-        64 * filters * outputs,
-        68 * filters * outputs,
-        me,
-        up_tiles[0],
-        mate_tiles,
-    )
+        32 * filters * outputs,
+        34 * filters * outputs,
+        me,
+    )
+    partial, tiles, mate_tiles = lax.optimization_barrier((partial, up_tiles[0], mate_tiles))
+    keep, mate_phases = phases(tiles), phases(mate_tiles)
+    others[0], keep, mate_phases = lax.optimization_barrier((others[0], keep, mate_phases))
     hidden = local(
         silu_body,
         shape((voxels, filters), BF),
@@ -330,6 +332,7 @@
         own.size,
         12 * own.size,
         me,
+        spread,
         own,
         *arrived,
     )

time: 29 us -> 28.1 us (0.969)
  waiting for transfers between devices: 8.92 us -> 12.3 us
  local copies, waits for them, and re-layouts: 3.38 us -> 0.01 us
  Pallas kernels: 4.2 us -> 3.77 us
  starting transfers between devices: 12.2 us -> 11.8 us
    unnamed x6, local copies, waits for them, and re-layouts: 3.38 us -> 0.01 us
    ppermute x13, waiting for transfers between devices: 8.92 us -> 12.3 us  [swap(): return lax.ppermute(block, 'rows', [(i, i ^ mask) for i in range(count)])]
    pallas_call x8 -> x9, Pallas kernels: 4.2 us -> 3.77 us  [local(): pl.pallas_call(body, out_shape=outs, in_specs=[SMEM] + [HBM if i in in_hb...]
    ppermute x13, starting transfers between devices: 12.2 us -> 11.8 us  [swap(): return lax.ppermute(block, 'rows', [(i, i ^ mask) for i in range(count)])]
  transfers between devices with their start and end apart: 13 -> 13, of which waited for: 7 -> 8; matrix products, arithmetic and copies ran while one was open for 0% -> 0% of each run, Pallas kernels for 9% -> 7%
where the time goes in v3:
time: 28.1 us; the launch traced here: 27.9 us
  waiting for transfers between devices  12.3 us (44%)
  starting transfers between devices  11.8 us (42%)
  Pallas kernels  3.77 us (13%)
    ppermute x13, waiting for transfers between devices, swap(): return lax.ppermute(block, 'rows', [(i, i ^ mask) for i in range(count)])  12.3 us
    ppermute x13, starting transfers between devices, swap(): return lax.ppermute(block, 'rows', [(i, i ^ mask) for i in range(count)])  11.8 us
    pallas_call x9, Pallas kernels, local(): pl.pallas_call(body, out_shape=outs, in_specs=[SMEM] + [HBM if i in in_hb...  3.77 us
  transfers between devices with their start and end apart: 13, of which 8 were waited for; matrix products, arithmetic and copies ran while one was open for 0% of the time, Pallas kernels for 7%

profile of v3, /device:TPU:0, one launch (start us, length us, event | category | flops | bytes accessed | tf_op | source)
XLA Modules:
  0.0 27.9 jit_solution(13716419292716881475)
XLA Ops:
  0.0 4.0 %collective-permute-start = (bf16[3,64,256]{2,1,0:T(8,128)(2,1)}, bf16[3,64,256]{2,1,0:T(8,128)(2,1)S(1)}, u32[]{:S(2)}, u32[]{:S(2)}) collective-permute-start(bf16[3,64,256]{2,1,0:T(8,128)(2,1)} %bitcast.8), channel_id=1, source_target_pairs={{0,6},{1,7},{2,4},{3,5},{4,2},{5,3},{6,0},{7,1},{8,14},{9,15},{10,... | collective-permute-start | bytes 294920 | tf_op jit(solution)/shard_map/ppermute | solution.py:21
  4.0 0.5 %collective-permute-start.4 = (bf16[3,64,256]{2,1,0:T(8,128)(2,1)}, bf16[3,64,256]{2,1,0:T(8,128)(2,1)S(1)}, u32[]{:S(2)}, u32[]{:S(2)}) collective-permute-start(bf16[3,64,256]{2,1,0:T(8,128)(2,1)} %bitcast.9), channel_id=1, source_target_pairs={{0,2},{1,3},{2,0},{3,1},{4,6},{5,7},{6,4},{7,5},{8,10},{9,11},{10,... | collective-permute-start | bytes 294920 | tf_op jit(solution)/shard_map/ppermute | solution.py:21
  4.5 0.1 collective-permute-start.5
  4.5 0.0 collective-permute-start.1
  4.6 2.9 %collective-permute-done.refs_3_ = bf16[3,64,256]{2,1,0:T(8,128)(2,1)S(1)} collective-permute-done((bf16[3,64,256]{2,1,0:T(8,128)(2,1)}, bf16[3,64,256]{2,1,0:T(8,128)(2,1)S(1)}, u32[]{:S(2)}, u32[]{:S(2)}) %collective-permute-start) | collective-permute-done | bytes 98336 | tf_op jit(solution)/shard_map/ppermute | solution.py:21
  7.5 0.0 collective-permute-done.1.tiles_ref
  7.5 0.0 collective-permute-start.2
  7.5 0.5 %collective-permute-start.3 = (bf16[3,64,256]{2,1,0:T(8,128)(2,1)S(1)}, bf16[3,64,256]{2,1,0:T(8,128)(2,1)S(1)}, u32[]{:S(2)}, u32[]{:S(2)}) collective-permute-start(bf16[3,64,256]{2,1,0:T(8,128)(2,1)S(1)} %collective-permute-done.refs_3_), channel_id=1, source_target_pairs={{0,1},{1,0},{2,3},{3,2},{4,5},{5,4},{6,7},{7,6},{8,9},{9,8},{10,11... | collective-permute-start | bytes 294920 | tf_op jit(solution)/shard_map/ppermute | solution.py:21
  8.0 1.1 %collective-permute-done.4.refs_5_ = bf16[3,64,256]{2,1,0:T(8,128)(2,1)S(1)} collective-permute-done((bf16[3,64,256]{2,1,0:T(8,128)(2,1)}, bf16[3,64,256]{2,1,0:T(8,128)(2,1)S(1)}, u32[]{:S(2)}, u32[]{:S(2)}) %collective-permute-start.4) | collective-permute-done | bytes 98336 | tf_op jit(solution)/shard_map/ppermute | solution.py:21
  9.1 0.0 collective-permute-start.6
  9.1 0.2 collective-permute-done.5.refs_6_
  9.3 0.3 collective-permute-start.7
  9.6 0.0 collective-permute-done.2.refs_2_
  9.6 0.0 collective-permute-done.3.refs_4_
  9.6 1.1 %shard_map.38.refs_0_ = f32[9,256,128]{2,1,0:T(8,128)S(1)} custom-call(s32[1]{0:T(128)} %bitcast.me_ref, bf16[27,512,128]{2,1,0:T(8,128)(2,1)S(1)} %bitcast.4, bf16[3,64,256]{2,1,0:T(8,128)(2,1)S(1)} %bitcast.12, bf16[3,64,256]{2,1,0:T(8,128)(2,1)S(1)} %collective-permute-done.2.refs_2_, bf16[3,64,256]{2,1,0:T(8,128)(2,1)S(1)} %collective-permute-done.refs_3_, ...), custom_call_target="tpu_custom_call" | custom-call | flops 679477248 | bytes 2654208 | tf_op jit(solution)/shard_map/pallas_call | solution.py:25
  10.7 0.0 copy-start.1
  10.7 0.5 %shard_map.39 = (f32[256,128]{1,0:T(8,128)S(1)}, bf16[256,128]{1,0:T(8,128)(2,1)S(1)}) custom-call(s32[1]{0:T(128)} %bitcast.me_ref, f32[9,256,128]{2,1,0:T(8,128)S(1)} %shard_map.38.refs_0_, bf16[27,512,128]{2,1,0:T(8,128)(2,1)S(1)} %bitcast.5, bf16[3,64,256]{2,1,0:T(8,128)(2,1)S(1)} %collective-permute-done.6.refs_2_, ...), custom_call_target="tpu_custom_call" | custom-call | flops 226492416 | bytes 884736 | tf_op jit(solution)/shard_map/pallas_call | solution.py:25
  11.3 2.8 %collective-permute-start.8 = (bf16[256,128]{1,0:T(8,128)(2,1)S(1)}, bf16[256,128]{1,0:T(8,128)(2,1)S(1)}, u32[]{:S(2)}, u32[]{:S(2)}) collective-permute-start(bf16[256,128]{1,0:T(8,128)(2,1)S(1)} %get-tuple-element.29), channel_id=1, source_target_pairs={{0,8},{1,9},{2,10},{3,11},{4,12},{5,13},{6,14},{7,15},{8,0},{9,1},... | collective-permute-start | bytes 196616 | tf_op jit(solution)/shard_map/ppermute | solution.py:21
  14.1 0.3 shard_map.40.weight_ref
  14.4 0.3 shard_map.41.weight_ref
  14.7 3.3 %collective-permute-done.8.refs_1_ = bf16[256,128]{1,0:T(8,128)(2,1)S(1)} collective-permute-done((bf16[256,128]{1,0:T(8,128)(2,1)S(1)}, bf16[256,128]{1,0:T(8,128)(2,1)S(1)}, u32[]{:S(2)}, u32[]{:S(2)}) %collective-permute-start.8) | collective-permute-done | bytes 65568 | tf_op jit(solution)/shard_map/ppermute | solution.py:21
  18.0 0.1 collective-permute-start.9
  18.1 0.3 %shard_map.43.before_ref = f32[4,1,128,256]{3,2,1,0:T(8,128)S(1)} custom-call(s32[1]{0:T(128)} %bitcast.me_ref, bf16[256,128]{1,0:T(8,128)(2,1)S(1)} %shard_map.42.hidden_ref, bf16[1,2,512,256]{3,2,1,0:T(8,128)(2,1)S(1)} %shard_map.40.weight_ref), custom_call_target="tpu_custom_call" | custom-call | flops 134217728 | bytes 524288 | tf_op jit(solution)/shard_map/pallas_call | solution.py:25
  18.4 0.9 %collective-permute-done.9.hidden_ref = bf16[256,128]{1,0:T(8,128)(2,1)S(1)} collective-permute-done((bf16[256,128]{1,0:T(8,128)(2,1)S(1)}, bf16[256,128]{1,0:T(8,128)(2,1)S(1)}, u32[]{:S(2)}, u32[]{:S(2)}) %collective-permute-start.9) | collective-permute-done | bytes 65568 | tf_op jit(solution)/shard_map/ppermute | solution.py:21
  19.3 0.4 %shard_map.44 = (f32[1,128,256]{2,1,0:T(8,128)S(1)}, bf16[1,128,256]{2,1,0:T(8,128)(2,1)S(1)}, bf16[1,128,256]{2,1,0:T(8,128)(2,1)S(1)}, bf16[1,128,256]{2,1,0:T(8,128)(2,1)S(1)}) custom-call(s32[1]{0:T(128)} %bitcast.me_ref, f32[4,1,128,256]{3,2,1,0:T(8,128)S(1)} %shard_map.43.before_ref, bf16[256,128]{1,0:T(8,128)(2,1)S(1)} %collective-permute-done.9.hidden_ref, ...), custom_call_target="tpu_custom_call" | custom-call | flops 134217728 | bytes 524288 | tf_op jit(solution)/shard_map/pallas_call | solution.py:25
  19.7 1.6 %collective-permute-start.10 = (bf16[1,128,256]{2,1,0:T(8,128)(2,1)S(1)}, bf16[1,128,256]{2,1,0:T(8,128)(2,1)S(1)}, u32[]{:S(2)}, u32[]{:S(2)}) collective-permute-start(bf16[1,128,256]{2,1,0:T(8,128)(2,1)S(1)} %get-tuple-element.36), channel_id=1, source_target_pairs={{0,2},{1,3},{2,0},{3,1},{4,6},{5,7},{6,4},{7,5},{8,10},{9,11},{10,... | collective-permute-start | bytes 196616 | tf_op jit(solution)/shard_map/ppermute | solution.py:21
  21.3 0.6 %collective-permute-start.11 = (bf16[1,128,256]{2,1,0:T(8,128)(2,1)S(1)}, bf16[1,128,256]{2,1,0:T(8,128)(2,1)S(1)}, u32[]{:S(2)}, u32[]{:S(2)}) collective-permute-start(bf16[1,128,256]{2,1,0:T(8,128)(2,1)S(1)} %get-tuple-element.37), channel_id=1, source_target_pairs={{0,4},{1,5},{2,6},{3,7},{4,0},{5,1},{6,2},{7,3},{8,12},{9,13},{10,... | collective-permute-start | bytes 196616 | tf_op jit(solution)/shard_map/ppermute | solution.py:21
  21.9 1.3 %collective-permute-start.12 = (bf16[1,128,256]{2,1,0:T(8,128)(2,1)S(1)}, bf16[1,128,256]{2,1,0:T(8,128)(2,1)S(1)}, u32[]{:S(2)}, u32[]{:S(2)}) collective-permute-start(bf16[1,128,256]{2,1,0:T(8,128)(2,1)S(1)} %get-tuple-element.38), channel_id=1, source_target_pairs={{0,6},{1,7},{2,4},{3,5},{4,2},{5,3},{6,0},{7,1},{8,14},{9,15},{10,... | collective-permute-start | bytes 196616 | tf_op jit(solution)/shard_map/ppermute | solution.py:21
  23.3 0.8 %collective-permute-done.10.refs_0_ = bf16[1,128,256]{2,1,0:T(8,128)(2,1)S(1)} collective-permute-done((bf16[1,128,256]{2,1,0:T(8,128)(2,1)S(1)}, bf16[1,128,256]{2,1,0:T(8,128)(2,1)S(1)}, u32[]{:S(2)}, u32[]{:S(2)}) %collective-permute-start.10) | collective-permute-done | bytes 65568 | tf_op jit(solution)/shard_map/ppermute | solution.py:21
  24.0 1.9 %collective-permute-done.11.refs_1_ = bf16[1,128,256]{2,1,0:T(8,128)(2,1)S(1)} collective-permute-done((bf16[1,128,256]{2,1,0:T(8,128)(2,1)S(1)}, bf16[1,128,256]{2,1,0:T(8,128)(2,1)S(1)}, u32[]{:S(2)}, u32[]{:S(2)}) %collective-permute-start.11) | collective-permute-done | bytes 65568 | tf_op jit(solution)/shard_map/ppermute | solution.py:21
  25.9 1.2 %collective-permute-done.12.refs_2_ = bf16[1,128,256]{2,1,0:T(8,128)(2,1)S(1)} collective-permute-done((bf16[1,128,256]{2,1,0:T(8,128)(2,1)S(1)}, bf16[1,128,256]{2,1,0:T(8,128)(2,1)S(1)}, u32[]{:S(2)}, u32[]{:S(2)}) %collective-permute-start.12) | collective-permute-done | bytes 65568 | tf_op jit(solution)/shard_map/ppermute | solution.py:21
  27.1 0.8 %shard_map.45 = bf16[1,256,128]{2,1,0:T(8,128)(2,1)} custom-call(s32[1]{0:T(128)} %bitcast.me_ref, bf16[128,128]{1,0:T(8,128)(2,1)S(1)} %shard_map.37.spread_ref, f32[1,128,256]{2,1,0:T(8,128)S(1)} %get-tuple-element.35.own_ref, bf16[1,128,256]{2,1,0:T(8,128)(2,1)S(1)} %collective-permute-done.10.refs_0_, ...), custom_call_target="tpu_custom_call" | custom-call | flops 32768 | bytes 393216 | tf_op jit(solution)/shard_map/pallas_call | solution.py:25
  (9 shorter events, 0.1 us)
Async XLA Ops:
  0.0 7.4 %collective-permute-start = (bf16[3,64,256]{2,1,0:T(8,128)(2,1)}, bf16[3,64,256]{2,1,0:T(8,128)(2,1)S(1)}, u32[]{:S(2)}, u32[]{:S(2)}) collective-permute-start(bf16[3,64,256]{2,1,0:T(8,128)(2,1)} %bitcast.8), channel_id=1, source_target_pairs={{0,6},{1,7},{2,4},{3,5},{4,2},{5,3},{6,0},{7,1},{8,14},{9,15},{10,... | collective-permute-start | bytes 294920 | tf_op jit(solution)/shard_map/ppermute | solution.py:21
  4.0 5.1 %collective-permute-start.4 = (bf16[3,64,256]{2,1,0:T(8,128)(2,1)}, bf16[3,64,256]{2,1,0:T(8,128)(2,1)S(1)}, u32[]{:S(2)}, u32[]{:S(2)}) collective-permute-start(bf16[3,64,256]{2,1,0:T(8,128)(2,1)} %bitcast.9), channel_id=1, source_target_pairs={{0,2},{1,3},{2,0},{3,1},{4,6},{5,7},{6,4},{7,5},{8,10},{9,11},{10,... | collective-permute-start | bytes 294920 | tf_op jit(solution)/shard_map/ppermute | solution.py:21
  4.5 4.8 %collective-permute-start.5 = (bf16[3,64,256]{2,1,0:T(8,128)(2,1)}, bf16[3,64,256]{2,1,0:T(8,128)(2,1)S(1)}, u32[]{:S(2)}, u32[]{:S(2)}) collective-permute-start(bf16[3,64,256]{2,1,0:T(8,128)(2,1)} %bitcast.10), channel_id=1, source_target_pairs={{0,4},{1,5},{2,6},{3,7},{4,0},{5,1},{6,2},{7,3},{8,12},{9,13},{10,... | collective-permute-start | bytes 294920 | tf_op jit(solution)/shard_map/ppermute | solution.py:21
  4.5 2.9 %collective-permute-start.1 = (bf16[9,256,128]{2,1,0:T(8,128)(2,1)}, bf16[9,256,128]{2,1,0:T(8,128)(2,1)S(1)}, u32[]{:S(2)}, u32[]{:S(2)}) collective-permute-start(bf16[9,256,128]{2,1,0:T(8,128)(2,1)} %bitcast.6), channel_id=1, source_target_pairs={{0,1},{1,0},{2,3},{3,2},{4,5},{5,4},{6,7},{7,6},{8,9},{9,8},{10,11... | collective-permute-start | bytes 1769480 | tf_op jit(solution)/shard_map/ppermute | solution.py:21
  4.6 2.9 %copy-start.2 = (bf16[64,3,256]{2,0,1:T(8,128)(2,1)S(1)}, bf16[64,3,256]{2,0,1:T(8,128)(2,1)}, u32[]{:S(2)}) copy-start(bf16[64,3,256]{2,0,1:T(8,128)(2,1)} %param.3) | copy-start | bytes 294916
  4.6 5.1 %copy-start = (bf16[1,27,512,128]{3,2,1,0:T(8,128)(2,1)S(1)}, bf16[1,27,512,128]{3,2,1,0:T(8,128)(2,1)}, u32[]{:S(2)}) copy-start(bf16[1,27,512,128]{3,2,1,0:T(8,128)(2,1)} %param.4) | copy-start | bytes 10616836
  7.5 2.2 %collective-permute-start.2 = (bf16[3,64,256]{2,1,0:T(8,128)(2,1)S(1)}, bf16[3,64,256]{2,1,0:T(8,128)(2,1)S(1)}, u32[]{:S(2)}, u32[]{:S(2)}) collective-permute-start(bf16[3,64,256]{2,1,0:T(8,128)(2,1)S(1)} %bitcast.11), channel_id=1, source_target_pairs={{0,1},{1,0},{2,3},{3,2},{4,5},{5,4},{6,7},{7,6},{8,9},{9,8},{10,11... | collective-permute-start | bytes 294920 | tf_op jit(solution)/shard_map/ppermute | solution.py:21
  7.5 2.1 %collective-permute-start.3 = (bf16[3,64,256]{2,1,0:T(8,128)(2,1)S(1)}, bf16[3,64,256]{2,1,0:T(8,128)(2,1)S(1)}, u32[]{:S(2)}, u32[]{:S(2)}) collective-permute-start(bf16[3,64,256]{2,1,0:T(8,128)(2,1)S(1)} %collective-permute-done.refs_3_), channel_id=1, source_target_pairs={{0,1},{1,0},{2,3},{3,2},{4,5},{5,4},{6,7},{7,6},{8,9},{9,8},{10,11... | collective-permute-start | bytes 294920 | tf_op jit(solution)/shard_map/ppermute | solution.py:21
  9.1 1.6 %collective-permute-start.6 = (bf16[3,64,256]{2,1,0:T(8,128)(2,1)S(1)}, bf16[3,64,256]{2,1,0:T(8,128)(2,1)S(1)}, u32[]{:S(2)}, u32[]{:S(2)}) collective-permute-start(bf16[3,64,256]{2,1,0:T(8,128)(2,1)S(1)} %collective-permute-done.4.refs_5_), channel_id=1, source_target_pairs={{0,1},{1,0},{2,3},{3,2},{4,5},{5,4},{6,7},{7,6},{8,9},{9,8},{10,11... | collective-permute-start | bytes 294920 | tf_op jit(solution)/shard_map/ppermute | solution.py:21
  9.3 1.4 %collective-permute-start.7 = (bf16[3,64,256]{2,1,0:T(8,128)(2,1)S(1)}, bf16[3,64,256]{2,1,0:T(8,128)(2,1)S(1)}, u32[]{:S(2)}, u32[]{:S(2)}) collective-permute-start(bf16[3,64,256]{2,1,0:T(8,128)(2,1)S(1)} %collective-permute-done.5.refs_6_), channel_id=1, source_target_pairs={{0,1},{1,0},{2,3},{3,2},{4,5},{5,4},{6,7},{7,6},{8,9},{9,8},{10,11... | collective-permute-start | bytes 294920 | tf_op jit(solution)/shard_map/ppermute | solution.py:21
  10.7 3.4 %copy-start.1 = (bf16[1,9,256,128]{3,2,1,0:T(8,128)(2,1)S(1)}, bf16[1,9,256,128]{3,2,1,0:T(8,128)(2,1)}, u32[]{:S(2)}) copy-start(bf16[1,9,256,128]{3,2,1,0:T(8,128)(2,1)} %param.5) | copy-start | bytes 1769476
  11.3 6.7 %collective-permute-start.8 = (bf16[256,128]{1,0:T(8,128)(2,1)S(1)}, bf16[256,128]{1,0:T(8,128)(2,1)S(1)}, u32[]{:S(2)}, u32[]{:S(2)}) collective-permute-start(bf16[256,128]{1,0:T(8,128)(2,1)S(1)} %get-tuple-element.29), channel_id=1, source_target_pairs={{0,8},{1,9},{2,10},{3,11},{4,12},{5,13},{6,14},{7,15},{8,0},{9,1},... | collective-permute-start | bytes 196616 | tf_op jit(solution)/shard_map/ppermute | solution.py:21
  18.0 1.3 %collective-permute-start.9 = (bf16[256,128]{1,0:T(8,128)(2,1)S(1)}, bf16[256,128]{1,0:T(8,128)(2,1)S(1)}, u32[]{:S(2)}, u32[]{:S(2)}) collective-permute-start(bf16[256,128]{1,0:T(8,128)(2,1)S(1)} %shard_map.42.hidden_ref), channel_id=1, source_target_pairs={{0,1},{1,0},{2,3},{3,2},{4,5},{5,4},{6,7},{7,6},{8,9},{9,8},{10,11... | collective-permute-start | bytes 196616 | tf_op jit(solution)/shard_map/ppermute | solution.py:21
  19.7 4.3 %collective-permute-start.10 = (bf16[1,128,256]{2,1,0:T(8,128)(2,1)S(1)}, bf16[1,128,256]{2,1,0:T(8,128)(2,1)S(1)}, u32[]{:S(2)}, u32[]{:S(2)}) collective-permute-start(bf16[1,128,256]{2,1,0:T(8,128)(2,1)S(1)} %get-tuple-element.36), channel_id=1, source_target_pairs={{0,2},{1,3},{2,0},{3,1},{4,6},{5,7},{6,4},{7,5},{8,10},{9,11},{10,... | collective-permute-start | bytes 196616 | tf_op jit(solution)/shard_map/ppermute | solution.py:21
  21.3 4.6 %collective-permute-start.11 = (bf16[1,128,256]{2,1,0:T(8,128)(2,1)S(1)}, bf16[1,128,256]{2,1,0:T(8,128)(2,1)S(1)}, u32[]{:S(2)}, u32[]{:S(2)}) collective-permute-start(bf16[1,128,256]{2,1,0:T(8,128)(2,1)S(1)} %get-tuple-element.37), channel_id=1, source_target_pairs={{0,4},{1,5},{2,6},{3,7},{4,0},{5,1},{6,2},{7,3},{8,12},{9,13},{10,... | collective-permute-start | bytes 196616 | tf_op jit(solution)/shard_map/ppermute | solution.py:21
  21.9 5.2 %collective-permute-start.12 = (bf16[1,128,256]{2,1,0:T(8,128)(2,1)S(1)}, bf16[1,128,256]{2,1,0:T(8,128)(2,1)S(1)}, u32[]{:S(2)}, u32[]{:S(2)}) collective-permute-start(bf16[1,128,256]{2,1,0:T(8,128)(2,1)S(1)} %get-tuple-element.38), channel_id=1, source_target_pairs={{0,6},{1,7},{2,4},{3,5},{4,2},{5,3},{6,0},{7,1},{8,14},{9,15},{10,... | collective-permute-start | bytes 196616 | tf_op jit(solution)/shard_map/ppermute | solution.py:21

commit v4 on v3

--- a/solution.py
+++ b/solution.py
@@ -12,7 +12,6 @@
 F32 = jnp.float32
 VMEM = pl.BlockSpec(memory_space=pltpu.VMEM)
 SMEM = pl.BlockSpec(memory_space=pltpu.SMEM)
-HBM = pl.BlockSpec(memory_space=pltpu.HBM)
 LIMIT = 32 * 2**20
 
 
@@ -21,16 +20,20 @@
     return lax.ppermute(block, "rows", [(i, i ^ mask) for i in range(count)])
 
 
-def local(body, outs, scratch, flops, moved, me, *args, in_hbm=()):
+def local(body, outs, scratch, flops, moved, me, *args):
     return pl.pallas_call(
         body,
         out_shape=outs,
-        in_specs=[SMEM] + [HBM if i in in_hbm else VMEM for i in range(len(args))],
+        in_specs=[SMEM] + [VMEM] * len(args),
         out_specs=jax.tree.map(lambda _: VMEM, outs),
         scratch_shapes=scratch,
         compiler_params=pltpu.CompilerParams(vmem_limit_bytes=LIMIT),
         cost_estimate=pl.CostEstimate(flops=flops, bytes_accessed=moved, transcendentals=0),
     )(me, *args)
+
+
+def farthest_first(chips):
+    return (chips - 1, *range(1, chips - 1))
 
 
 def phase_groups(phase):
@@ -190,8 +193,10 @@
     ):
         total_ref[half, k, cells, :] = before_ref[half, k, cells, :] + value
     chip = me_ref[0] // 2 % halves
-    for mask, out_ref in enumerate(out_refs):
-        out_ref[...] = total_ref[chip ^ mask].astype(out_ref.dtype)
+    own_ref, *leaving_refs = out_refs
+    own_ref[...] = total_ref[chip]
+    for mask, out_ref in zip(farthest_first(halves), leaving_refs, strict=True):
+        out_ref[...] = total_ref[chip ^ mask].astype(BF)
 
 
 def spread_body(me_ref, out_ref):
@@ -324,7 +329,9 @@
         mate_hidden,
         mate_phases,
     )
-    arrived = [swap(block, 2 * (mask + 1)) for mask, block in enumerate(leaving)]
+    arrived = [
+        swap(block, 2 * mask) for mask, block in zip(farthest_first(halves), leaving, strict=True)
+    ]
     return local(
         final_body,
         shape((1, outputs, lines * 2 * W), BF),

time: 28.1 us -> 27.3 us (0.972)
  waiting for transfers between devices: 12.3 us -> 11.5 us
    ppermute x13, waiting for transfers between devices: 12.3 us -> 11.5 us  [swap(): return lax.ppermute(block, 'rows', [(i, i ^ mask) for i in range(count)])]
where the time goes in v4:
time: 27.3 us; the launch traced here: 27.2 us
  starting transfers between devices  11.8 us (43%)
  waiting for transfers between devices  11.5 us (42%)
  Pallas kernels  3.77 us (14%)
    ppermute x13, starting transfers between devices, swap(): return lax.ppermute(block, 'rows', [(i, i ^ mask) for i in range(count)])  11.8 us
    ppermute x13, waiting for transfers between devices, swap(): return lax.ppermute(block, 'rows', [(i, i ^ mask) for i in range(count)])  11.5 us
    pallas_call x9, Pallas kernels, local(): pl.pallas_call(body, out_shape=outs, in_specs=[SMEM] + [VMEM] * len(args)...  3.77 us
  transfers between devices with their start and end apart: 13, of which 8 were waited for; matrix products, arithmetic and copies ran while one was open for 0% of the time, Pallas kernels for 7%

profile of v4, /device:TPU:0, one launch (start us, length us, event | category | flops | bytes accessed | tf_op | source)
XLA Modules:
  0.0 27.2 jit_solution(17248130748875438330)
XLA Ops:
  0.0 4.0 %collective-permute-start = (bf16[3,64,256]{2,1,0:T(8,128)(2,1)}, bf16[3,64,256]{2,1,0:T(8,128)(2,1)S(1)}, u32[]{:S(2)}, u32[]{:S(2)}) collective-permute-start(bf16[3,64,256]{2,1,0:T(8,128)(2,1)} %bitcast.8), channel_id=1, source_target_pairs={{0,6},{1,7},{2,4},{3,5},{4,2},{5,3},{6,0},{7,1},{8,14},{9,15},{10,... | collective-permute-start | bytes 294920 | tf_op jit(solution)/shard_map/ppermute | solution.py:20
  4.0 0.5 %collective-permute-start.4 = (bf16[3,64,256]{2,1,0:T(8,128)(2,1)}, bf16[3,64,256]{2,1,0:T(8,128)(2,1)S(1)}, u32[]{:S(2)}, u32[]{:S(2)}) collective-permute-start(bf16[3,64,256]{2,1,0:T(8,128)(2,1)} %bitcast.9), channel_id=1, source_target_pairs={{0,2},{1,3},{2,0},{3,1},{4,6},{5,7},{6,4},{7,5},{8,10},{9,11},{10,... | collective-permute-start | bytes 294920 | tf_op jit(solution)/shard_map/ppermute | solution.py:20
  4.5 0.1 collective-permute-start.5
  4.5 0.0 collective-permute-start.1
  4.6 2.9 %collective-permute-done.refs_3_ = bf16[3,64,256]{2,1,0:T(8,128)(2,1)S(1)} collective-permute-done((bf16[3,64,256]{2,1,0:T(8,128)(2,1)}, bf16[3,64,256]{2,1,0:T(8,128)(2,1)S(1)}, u32[]{:S(2)}, u32[]{:S(2)}) %collective-permute-start) | collective-permute-done | bytes 98336 | tf_op jit(solution)/shard_map/ppermute | solution.py:20
  7.5 0.0 collective-permute-done.1.tiles_ref
  7.5 0.0 collective-permute-start.2
  7.5 0.5 %collective-permute-start.3 = (bf16[3,64,256]{2,1,0:T(8,128)(2,1)S(1)}, bf16[3,64,256]{2,1,0:T(8,128)(2,1)S(1)}, u32[]{:S(2)}, u32[]{:S(2)}) collective-permute-start(bf16[3,64,256]{2,1,0:T(8,128)(2,1)S(1)} %collective-permute-done.refs_3_), channel_id=1, source_target_pairs={{0,1},{1,0},{2,3},{3,2},{4,5},{5,4},{6,7},{7,6},{8,9},{9,8},{10,11... | collective-permute-start | bytes 294920 | tf_op jit(solution)/shard_map/ppermute | solution.py:20
  8.0 1.1 %collective-permute-done.4.refs_5_ = bf16[3,64,256]{2,1,0:T(8,128)(2,1)S(1)} collective-permute-done((bf16[3,64,256]{2,1,0:T(8,128)(2,1)}, bf16[3,64,256]{2,1,0:T(8,128)(2,1)S(1)}, u32[]{:S(2)}, u32[]{:S(2)}) %collective-permute-start.4) | collective-permute-done | bytes 98336 | tf_op jit(solution)/shard_map/ppermute | solution.py:20
  9.1 0.0 collective-permute-start.6
  9.1 0.2 collective-permute-done.5.refs_6_
  9.3 0.3 collective-permute-start.7
  9.6 0.0 collective-permute-done.2.refs_2_
  9.6 0.0 collective-permute-done.3.refs_4_
  9.6 1.1 %shard_map.38.refs_0_ = f32[9,256,128]{2,1,0:T(8,128)S(1)} custom-call(s32[1]{0:T(128)} %bitcast.me_ref, bf16[27,512,128]{2,1,0:T(8,128)(2,1)S(1)} %bitcast.4, bf16[3,64,256]{2,1,0:T(8,128)(2,1)S(1)} %bitcast.12, bf16[3,64,256]{2,1,0:T(8,128)(2,1)S(1)} %collective-permute-done.2.refs_2_, bf16[3,64,256]{2,1,0:T(8,128)(2,1)S(1)} %collective-permute-done.refs_3_, ...), custom_call_target="tpu_custom_call" | custom-call | flops 679477248 | bytes 2654208 | tf_op jit(solution)/shard_map/pallas_call | solution.py:24
  10.7 0.0 copy-start.1
  10.7 0.5 %shard_map.39 = (f32[256,128]{1,0:T(8,128)S(1)}, bf16[256,128]{1,0:T(8,128)(2,1)S(1)}) custom-call(s32[1]{0:T(128)} %bitcast.me_ref, f32[9,256,128]{2,1,0:T(8,128)S(1)} %shard_map.38.refs_0_, bf16[27,512,128]{2,1,0:T(8,128)(2,1)S(1)} %bitcast.5, bf16[3,64,256]{2,1,0:T(8,128)(2,1)S(1)} %collective-permute-done.6.refs_2_, ...), custom_call_target="tpu_custom_call" | custom-call | flops 226492416 | bytes 884736 | tf_op jit(solution)/shard_map/pallas_call | solution.py:24
  11.3 2.8 %collective-permute-start.8 = (bf16[256,128]{1,0:T(8,128)(2,1)S(1)}, bf16[256,128]{1,0:T(8,128)(2,1)S(1)}, u32[]{:S(2)}, u32[]{:S(2)}) collective-permute-start(bf16[256,128]{1,0:T(8,128)(2,1)S(1)} %get-tuple-element.29), channel_id=1, source_target_pairs={{0,8},{1,9},{2,10},{3,11},{4,12},{5,13},{6,14},{7,15},{8,0},{9,1},... | collective-permute-start | bytes 196616 | tf_op jit(solution)/shard_map/ppermute | solution.py:20
  14.1 0.3 %shard_map.40.weight_ref = bf16[1,2,512,256]{3,2,1,0:T(8,128)(2,1)S(1)} custom-call(s32[1]{0:T(128)} %bitcast.me_ref, bf16[9,256,128]{2,1,0:T(8,128)(2,1)S(1)} %bitcast.7), custom_call_target="tpu_custom_call" | custom-call | flops 1048576 | bytes 1114112 | tf_op jit(solution)/shard_map/pallas_call | solution.py:24
  14.4 0.3 %shard_map.41.weight_ref = bf16[1,2,512,256]{3,2,1,0:T(8,128)(2,1)S(1)} custom-call(s32[1]{0:T(128)} %bitcast.me_ref, bf16[9,256,128]{2,1,0:T(8,128)(2,1)S(1)} %collective-permute-done.1.tiles_ref), custom_call_target="tpu_custom_call" | custom-call | flops 1048576 | bytes 1114112 | tf_op jit(solution)/shard_map/pallas_call | solution.py:24
  14.7 3.3 %collective-permute-done.8.refs_1_ = bf16[256,128]{1,0:T(8,128)(2,1)S(1)} collective-permute-done((bf16[256,128]{1,0:T(8,128)(2,1)S(1)}, bf16[256,128]{1,0:T(8,128)(2,1)S(1)}, u32[]{:S(2)}, u32[]{:S(2)}) %collective-permute-start.8) | collective-permute-done | bytes 65568 | tf_op jit(solution)/shard_map/ppermute | solution.py:20
  18.0 0.1 collective-permute-start.9
  18.1 0.3 %shard_map.43.before_ref = f32[4,1,128,256]{3,2,1,0:T(8,128)S(1)} custom-call(s32[1]{0:T(128)} %bitcast.me_ref, bf16[256,128]{1,0:T(8,128)(2,1)S(1)} %shard_map.42.hidden_ref, bf16[1,2,512,256]{3,2,1,0:T(8,128)(2,1)S(1)} %shard_map.40.weight_ref), custom_call_target="tpu_custom_call" | custom-call | flops 134217728 | bytes 524288 | tf_op jit(solution)/shard_map/pallas_call | solution.py:24
  18.4 0.9 %collective-permute-done.9.hidden_ref = bf16[256,128]{1,0:T(8,128)(2,1)S(1)} collective-permute-done((bf16[256,128]{1,0:T(8,128)(2,1)S(1)}, bf16[256,128]{1,0:T(8,128)(2,1)S(1)}, u32[]{:S(2)}, u32[]{:S(2)}) %collective-permute-start.9) | collective-permute-done | bytes 65568 | tf_op jit(solution)/shard_map/ppermute | solution.py:20
  19.3 0.4 %shard_map.44 = (f32[1,128,256]{2,1,0:T(8,128)S(1)}, bf16[1,128,256]{2,1,0:T(8,128)(2,1)S(1)}, bf16[1,128,256]{2,1,0:T(8,128)(2,1)S(1)}, bf16[1,128,256]{2,1,0:T(8,128)(2,1)S(1)}) custom-call(s32[1]{0:T(128)} %bitcast.me_ref, f32[4,1,128,256]{3,2,1,0:T(8,128)S(1)} %shard_map.43.before_ref, bf16[256,128]{1,0:T(8,128)(2,1)S(1)} %collective-permute-done.9.hidden_ref, ...), custom_call_target="tpu_custom_call" | custom-call | flops 134217728 | bytes 524288 | tf_op jit(solution)/shard_map/pallas_call | solution.py:24
  19.7 1.7 %collective-permute-start.10 = (bf16[1,128,256]{2,1,0:T(8,128)(2,1)S(1)}, bf16[1,128,256]{2,1,0:T(8,128)(2,1)S(1)}, u32[]{:S(2)}, u32[]{:S(2)}) collective-permute-start(bf16[1,128,256]{2,1,0:T(8,128)(2,1)S(1)} %get-tuple-element.36), channel_id=1, source_target_pairs={{0,6},{1,7},{2,4},{3,5},{4,2},{5,3},{6,0},{7,1},{8,14},{9,15},{10,... | collective-permute-start | bytes 196616 | tf_op jit(solution)/shard_map/ppermute | solution.py:20
  21.4 0.6 %collective-permute-start.11 = (bf16[1,128,256]{2,1,0:T(8,128)(2,1)S(1)}, bf16[1,128,256]{2,1,0:T(8,128)(2,1)S(1)}, u32[]{:S(2)}, u32[]{:S(2)}) collective-permute-start(bf16[1,128,256]{2,1,0:T(8,128)(2,1)S(1)} %get-tuple-element.37), channel_id=1, source_target_pairs={{0,2},{1,3},{2,0},{3,1},{4,6},{5,7},{6,4},{7,5},{8,10},{9,11},{10,... | collective-permute-start | bytes 196616 | tf_op jit(solution)/shard_map/ppermute | solution.py:20
  21.9 1.3 %collective-permute-start.12 = (bf16[1,128,256]{2,1,0:T(8,128)(2,1)S(1)}, bf16[1,128,256]{2,1,0:T(8,128)(2,1)S(1)}, u32[]{:S(2)}, u32[]{:S(2)}) collective-permute-start(bf16[1,128,256]{2,1,0:T(8,128)(2,1)S(1)} %get-tuple-element.38), channel_id=1, source_target_pairs={{0,4},{1,5},{2,6},{3,7},{4,0},{5,1},{6,2},{7,3},{8,12},{9,13},{10,... | collective-permute-start | bytes 196616 | tf_op jit(solution)/shard_map/ppermute | solution.py:20
  23.3 1.7 %collective-permute-done.10.refs_0_ = bf16[1,128,256]{2,1,0:T(8,128)(2,1)S(1)} collective-permute-done((bf16[1,128,256]{2,1,0:T(8,128)(2,1)S(1)}, bf16[1,128,256]{2,1,0:T(8,128)(2,1)S(1)}, u32[]{:S(2)}, u32[]{:S(2)}) %collective-permute-start.10) | collective-permute-done | bytes 65568 | tf_op jit(solution)/shard_map/ppermute | solution.py:20
  25.0 1.2 %collective-permute-done.11.refs_1_ = bf16[1,128,256]{2,1,0:T(8,128)(2,1)S(1)} collective-permute-done((bf16[1,128,256]{2,1,0:T(8,128)(2,1)S(1)}, bf16[1,128,256]{2,1,0:T(8,128)(2,1)S(1)}, u32[]{:S(2)}, u32[]{:S(2)}) %collective-permute-start.11) | collective-permute-done | bytes 65568 | tf_op jit(solution)/shard_map/ppermute | solution.py:20
  26.2 0.1 collective-permute-done.12.refs_2_
  26.3 0.8 %shard_map.45 = bf16[1,256,128]{2,1,0:T(8,128)(2,1)} custom-call(s32[1]{0:T(128)} %bitcast.me_ref, bf16[128,128]{1,0:T(8,128)(2,1)S(1)} %shard_map.37.spread_ref, f32[1,128,256]{2,1,0:T(8,128)S(1)} %get-tuple-element.35.own_ref, bf16[1,128,256]{2,1,0:T(8,128)(2,1)S(1)} %collective-permute-done.10.refs_0_, ...), custom_call_target="tpu_custom_call" | custom-call | flops 32768 | bytes 393216 | tf_op jit(solution)/shard_map/pallas_call | solution.py:24
  (9 shorter events, 0.1 us)
Async XLA Ops:
  0.0 7.4 %collective-permute-start = (bf16[3,64,256]{2,1,0:T(8,128)(2,1)}, bf16[3,64,256]{2,1,0:T(8,128)(2,1)S(1)}, u32[]{:S(2)}, u32[]{:S(2)}) collective-permute-start(bf16[3,64,256]{2,1,0:T(8,128)(2,1)} %bitcast.8), channel_id=1, source_target_pairs={{0,6},{1,7},{2,4},{3,5},{4,2},{5,3},{6,0},{7,1},{8,14},{9,15},{10,... | collective-permute-start | bytes 294920 | tf_op jit(solution)/shard_map/ppermute | solution.py:20
  4.0 5.1 %collective-permute-start.4 = (bf16[3,64,256]{2,1,0:T(8,128)(2,1)}, bf16[3,64,256]{2,1,0:T(8,128)(2,1)S(1)}, u32[]{:S(2)}, u32[]{:S(2)}) collective-permute-start(bf16[3,64,256]{2,1,0:T(8,128)(2,1)} %bitcast.9), channel_id=1, source_target_pairs={{0,2},{1,3},{2,0},{3,1},{4,6},{5,7},{6,4},{7,5},{8,10},{9,11},{10,... | collective-permute-start | bytes 294920 | tf_op jit(solution)/shard_map/ppermute | solution.py:20
  4.5 4.8 %collective-permute-start.5 = (bf16[3,64,256]{2,1,0:T(8,128)(2,1)}, bf16[3,64,256]{2,1,0:T(8,128)(2,1)S(1)}, u32[]{:S(2)}, u32[]{:S(2)}) collective-permute-start(bf16[3,64,256]{2,1,0:T(8,128)(2,1)} %bitcast.10), channel_id=1, source_target_pairs={{0,4},{1,5},{2,6},{3,7},{4,0},{5,1},{6,2},{7,3},{8,12},{9,13},{10,... | collective-permute-start | bytes 294920 | tf_op jit(solution)/shard_map/ppermute | solution.py:20
  4.5 2.9 %collective-permute-start.1 = (bf16[9,256,128]{2,1,0:T(8,128)(2,1)}, bf16[9,256,128]{2,1,0:T(8,128)(2,1)S(1)}, u32[]{:S(2)}, u32[]{:S(2)}) collective-permute-start(bf16[9,256,128]{2,1,0:T(8,128)(2,1)} %bitcast.6), channel_id=1, source_target_pairs={{0,1},{1,0},{2,3},{3,2},{4,5},{5,4},{6,7},{7,6},{8,9},{9,8},{10,11... | collective-permute-start | bytes 1769480 | tf_op jit(solution)/shard_map/ppermute | solution.py:20
  4.6 2.9 %copy-start.2 = (bf16[64,3,256]{2,0,1:T(8,128)(2,1)S(1)}, bf16[64,3,256]{2,0,1:T(8,128)(2,1)}, u32[]{:S(2)}) copy-start(bf16[64,3,256]{2,0,1:T(8,128)(2,1)} %param.3) | copy-start | bytes 294916
  4.6 5.1 %copy-start = (bf16[1,27,512,128]{3,2,1,0:T(8,128)(2,1)S(1)}, bf16[1,27,512,128]{3,2,1,0:T(8,128)(2,1)}, u32[]{:S(2)}) copy-start(bf16[1,27,512,128]{3,2,1,0:T(8,128)(2,1)} %param.4) | copy-start | bytes 10616836
  7.5 2.2 %collective-permute-start.2 = (bf16[3,64,256]{2,1,0:T(8,128)(2,1)S(1)}, bf16[3,64,256]{2,1,0:T(8,128)(2,1)S(1)}, u32[]{:S(2)}, u32[]{:S(2)}) collective-permute-start(bf16[3,64,256]{2,1,0:T(8,128)(2,1)S(1)} %bitcast.11), channel_id=1, source_target_pairs={{0,1},{1,0},{2,3},{3,2},{4,5},{5,4},{6,7},{7,6},{8,9},{9,8},{10,11... | collective-permute-start | bytes 294920 | tf_op jit(solution)/shard_map/ppermute | solution.py:20
  7.5 2.1 %collective-permute-start.3 = (bf16[3,64,256]{2,1,0:T(8,128)(2,1)S(1)}, bf16[3,64,256]{2,1,0:T(8,128)(2,1)S(1)}, u32[]{:S(2)}, u32[]{:S(2)}) collective-permute-start(bf16[3,64,256]{2,1,0:T(8,128)(2,1)S(1)} %collective-permute-done.refs_3_), channel_id=1, source_target_pairs={{0,1},{1,0},{2,3},{3,2},{4,5},{5,4},{6,7},{7,6},{8,9},{9,8},{10,11... | collective-permute-start | bytes 294920 | tf_op jit(solution)/shard_map/ppermute | solution.py:20
  9.1 1.6 %collective-permute-start.6 = (bf16[3,64,256]{2,1,0:T(8,128)(2,1)S(1)}, bf16[3,64,256]{2,1,0:T(8,128)(2,1)S(1)}, u32[]{:S(2)}, u32[]{:S(2)}) collective-permute-start(bf16[3,64,256]{2,1,0:T(8,128)(2,1)S(1)} %collective-permute-done.4.refs_5_), channel_id=1, source_target_pairs={{0,1},{1,0},{2,3},{3,2},{4,5},{5,4},{6,7},{7,6},{8,9},{9,8},{10,11... | collective-permute-start | bytes 294920 | tf_op jit(solution)/shard_map/ppermute | solution.py:20
  9.3 1.4 %collective-permute-start.7 = (bf16[3,64,256]{2,1,0:T(8,128)(2,1)S(1)}, bf16[3,64,256]{2,1,0:T(8,128)(2,1)S(1)}, u32[]{:S(2)}, u32[]{:S(2)}) collective-permute-start(bf16[3,64,256]{2,1,0:T(8,128)(2,1)S(1)} %collective-permute-done.5.refs_6_), channel_id=1, source_target_pairs={{0,1},{1,0},{2,3},{3,2},{4,5},{5,4},{6,7},{7,6},{8,9},{9,8},{10,11... | collective-permute-start | bytes 294920 | tf_op jit(solution)/shard_map/ppermute | solution.py:20
  10.7 3.4 %copy-start.1 = (bf16[1,9,256,128]{3,2,1,0:T(8,128)(2,1)S(1)}, bf16[1,9,256,128]{3,2,1,0:T(8,128)(2,1)}, u32[]{:S(2)}) copy-start(bf16[1,9,256,128]{3,2,1,0:T(8,128)(2,1)} %param.5) | copy-start | bytes 1769476
  11.3 6.7 %collective-permute-start.8 = (bf16[256,128]{1,0:T(8,128)(2,1)S(1)}, bf16[256,128]{1,0:T(8,128)(2,1)S(1)}, u32[]{:S(2)}, u32[]{:S(2)}) collective-permute-start(bf16[256,128]{1,0:T(8,128)(2,1)S(1)} %get-tuple-element.29), channel_id=1, source_target_pairs={{0,8},{1,9},{2,10},{3,11},{4,12},{5,13},{6,14},{7,15},{8,0},{9,1},... | collective-permute-start | bytes 196616 | tf_op jit(solution)/shard_map/ppermute | solution.py:20
  18.0 1.3 %collective-permute-start.9 = (bf16[256,128]{1,0:T(8,128)(2,1)S(1)}, bf16[256,128]{1,0:T(8,128)(2,1)S(1)}, u32[]{:S(2)}, u32[]{:S(2)}) collective-permute-start(bf16[256,128]{1,0:T(8,128)(2,1)S(1)} %shard_map.42.hidden_ref), channel_id=1, source_target_pairs={{0,1},{1,0},{2,3},{3,2},{4,5},{5,4},{6,7},{7,6},{8,9},{9,8},{10,11... | collective-permute-start | bytes 196616 | tf_op jit(solution)/shard_map/ppermute | solution.py:20
  19.7 5.3 %collective-permute-start.10 = (bf16[1,128,256]{2,1,0:T(8,128)(2,1)S(1)}, bf16[1,128,256]{2,1,0:T(8,128)(2,1)S(1)}, u32[]{:S(2)}, u32[]{:S(2)}) collective-permute-start(bf16[1,128,256]{2,1,0:T(8,128)(2,1)S(1)} %get-tuple-element.36), channel_id=1, source_target_pairs={{0,6},{1,7},{2,4},{3,5},{4,2},{5,3},{6,0},{7,1},{8,14},{9,15},{10,... | collective-permute-start | bytes 196616 | tf_op jit(solution)/shard_map/ppermute | solution.py:20
  21.4 4.9 %collective-permute-start.11 = (bf16[1,128,256]{2,1,0:T(8,128)(2,1)S(1)}, bf16[1,128,256]{2,1,0:T(8,128)(2,1)S(1)}, u32[]{:S(2)}, u32[]{:S(2)}) collective-permute-start(bf16[1,128,256]{2,1,0:T(8,128)(2,1)S(1)} %get-tuple-element.37), channel_id=1, source_target_pairs={{0,2},{1,3},{2,0},{3,1},{4,6},{5,7},{6,4},{7,5},{8,10},{9,11},{10,... | collective-permute-start | bytes 196616 | tf_op jit(solution)/shard_map/ppermute | solution.py:20
  21.9 4.4 %collective-permute-start.12 = (bf16[1,128,256]{2,1,0:T(8,128)(2,1)S(1)}, bf16[1,128,256]{2,1,0:T(8,128)(2,1)S(1)}, u32[]{:S(2)}, u32[]{:S(2)}) collective-permute-start(bf16[1,128,256]{2,1,0:T(8,128)(2,1)S(1)} %get-tuple-element.38), channel_id=1, source_target_pairs={{0,4},{1,5},{2,6},{3,7},{4,0},{5,1},{6,2},{7,3},{8,12},{9,13},{10,... | collective-permute-start | bytes 196616 | tf_op jit(solution)/shard_map/ppermute | solution.py:20

commit v5 on v4

--- a/solution.py
+++ b/solution.py
@@ -89,20 +89,20 @@
     before_ref = None if first else refs.pop(0)
     weight_ref = refs.pop(0)
     pieces = [refs.pop(0) for _ in masks or (0,)]
-    *out_refs, order_ref, columns_ref = refs
-    frames_of, channels, voxels = order_ref.shape
+    *out_refs, order_ref = refs
+    frames_of, _, voxels = pieces[0].shape
+    channels = order_ref.shape[0] // frames_of
     if masks:
         part = weight_ref.shape[1] // share
         me = me_ref[0] % share
-        spans = []
-        for i, mask in enumerate(masks):
-            order_ref[:, i * part : (i + 1) * part, :] = pieces[i][...]
-            spans.append(pl.ds(pl.multiple_of((me ^ mask) * part, part), part))
+        spans = [pl.ds(pl.multiple_of((me ^ mask) * part, part), part) for mask in masks]
     else:
-        order_ref[...] = pieces[0][...]
         spans = [slice(None)]
     for a in range(frames_of):
-        columns_ref[:, a * channels : (a + 1) * channels] = order_ref[a].T
+        for i, piece_ref in enumerate(pieces):
+            place = a * channels + i * piece_ref.shape[1]
+            order_ref[place : place + piece_ref.shape[1], :] = piece_ref[a]
+    columns = order_ref[...].T
     products = [None] * 9
     for low in range(0, 9, 2):
         pair = range(low, min(low + 2, 9))
@@ -115,7 +115,7 @@
             ],
             1,
         )
-        product = jnp.dot(columns_ref[...], weights, preferred_element_type=F32)
+        product = jnp.dot(columns, weights, preferred_element_type=F32)
         filters = product.shape[1] // len(pair)
         for i, t in enumerate(pair):
             own = product[:, i * filters : (i + 1) * filters]
@@ -206,16 +206,29 @@
 
 
 def final_body(me_ref, spread_ref, own_ref, *refs):
-    *other_refs, out_ref = refs
+    *other_refs, out_ref, line_ref = refs
     total = own_ref[...]
     for other_ref in other_refs:
         total = total + other_ref[...].astype(F32)
     total = total.astype(BF)
+    outputs = total.shape[2]
     for k in range(total.shape[0]):
-        woven = lax.dot_general(
-            total[k], spread_ref[...], (((0,), (0,)), ((), ())), preferred_element_type=F32
-        )
-        out_ref[0, :, k * 2 * W : (k + 1) * 2 * W] = woven.astype(BF)
+        places = slice(k * 2 * W, (k + 1) * 2 * W)
+        whole = outputs // 128
+        for i in range(whole):
+            block = total[k, :, i * 128 : (i + 1) * 128].astype(F32)
+            for q in range(2):
+                line_ref[k, i, pl.ds(q, W, stride=2), :] = block[q * W : (q + 1) * W]
+        for i in range(whole):
+            out_ref[0, i * 128 : (i + 1) * 128, places] = line_ref[k, i].T.astype(BF)
+        if outputs % 128:
+            woven = lax.dot_general(
+                total[k, :, whole * 128 :],
+                spread_ref[...],
+                (((0,), (0,)), ((), ())),
+                preferred_element_type=F32,
+            )
+            out_ref[0, whole * 128 :, places] = woven.astype(BF)
 
 
 def on_device(frames, conv_tiles, up_tiles):
@@ -264,14 +277,10 @@
         outs = [shape((voxels, filters), F32), shape((voxels, filters), BF)]
         if not last:
             outs = [shape((9, voxels, filters), F32)]
-        scratch = [
-            pltpu.VMEM((frames_of, depth, voxels), BF),
-            pltpu.VMEM((voxels, frames_of * depth), BF),
-        ]
         done = local(
             functools.partial(conv_body, share, masks, first, last),
             tuple(outs),
-            scratch,
+            [pltpu.VMEM((frames_of * depth, voxels), BF)],
             2 * taps * depth * filters * voxels,
             2 * taps * depth * filters,
             me,
@@ -335,7 +344,7 @@
     return local(
         final_body,
         shape((1, outputs, lines * 2 * W), BF),
-        [],
+        [pltpu.VMEM((lines, max(outputs // 128, 1), 2 * W, 128), F32)],
         own.size,
         12 * own.size,
         me,

time: 27.3 us -> 27.2 us (level)
  no operation moved by 1% of the time
where the time goes in v5:
time: 27.2 us; the launch traced here: 27.1 us
  starting transfers between devices  11.8 us (43%)
  waiting for transfers between devices  11.5 us (42%)
  Pallas kernels  3.65 us (13%)
    ppermute x13, starting transfers between devices, swap(): return lax.ppermute(block, 'rows', [(i, i ^ mask) for i in range(count)])  11.8 us
    ppermute x13, waiting for transfers between devices, swap(): return lax.ppermute(block, 'rows', [(i, i ^ mask) for i in range(count)])  11.5 us
    pallas_call x9, Pallas kernels, local(): pl.pallas_call(body, out_shape=outs, in_specs=[SMEM] + [VMEM] * len(args)...  3.65 us
  transfers between devices with their start and end apart: 13, of which 8 were waited for; matrix products, arithmetic and copies ran while one was open for 0% of the time, Pallas kernels for 7%

profile of v5, /device:TPU:0, one launch (start us, length us, event | category | flops | bytes accessed | tf_op | source)
XLA Modules:
  0.0 27.1 jit_solution(8596096246442385902)
XLA Ops:
  0.0 4.0 %collective-permute-start = (bf16[3,64,256]{2,1,0:T(8,128)(2,1)}, bf16[3,64,256]{2,1,0:T(8,128)(2,1)S(1)}, u32[]{:S(2)}, u32[]{:S(2)}) collective-permute-start(bf16[3,64,256]{2,1,0:T(8,128)(2,1)} %bitcast.8), channel_id=1, source_target_pairs={{0,6},{1,7},{2,4},{3,5},{4,2},{5,3},{6,0},{7,1},{8,14},{9,15},{10,... | collective-permute-start | bytes 294920 | tf_op jit(solution)/shard_map/ppermute | solution.py:20
  4.0 0.5 %collective-permute-start.4 = (bf16[3,64,256]{2,1,0:T(8,128)(2,1)}, bf16[3,64,256]{2,1,0:T(8,128)(2,1)S(1)}, u32[]{:S(2)}, u32[]{:S(2)}) collective-permute-start(bf16[3,64,256]{2,1,0:T(8,128)(2,1)} %bitcast.9), channel_id=1, source_target_pairs={{0,2},{1,3},{2,0},{3,1},{4,6},{5,7},{6,4},{7,5},{8,10},{9,11},{10,... | collective-permute-start | bytes 294920 | tf_op jit(solution)/shard_map/ppermute | solution.py:20
  4.5 0.1 collective-permute-start.5
  4.5 0.0 collective-permute-start.1
  4.6 2.9 %collective-permute-done.refs_3_ = bf16[3,64,256]{2,1,0:T(8,128)(2,1)S(1)} collective-permute-done((bf16[3,64,256]{2,1,0:T(8,128)(2,1)}, bf16[3,64,256]{2,1,0:T(8,128)(2,1)S(1)}, u32[]{:S(2)}, u32[]{:S(2)}) %collective-permute-start) | collective-permute-done | bytes 98336 | tf_op jit(solution)/shard_map/ppermute | solution.py:20
  7.5 0.0 collective-permute-done.1.tiles_ref
  7.5 0.0 collective-permute-start.2
  7.5 0.5 %collective-permute-start.3 = (bf16[3,64,256]{2,1,0:T(8,128)(2,1)S(1)}, bf16[3,64,256]{2,1,0:T(8,128)(2,1)S(1)}, u32[]{:S(2)}, u32[]{:S(2)}) collective-permute-start(bf16[3,64,256]{2,1,0:T(8,128)(2,1)S(1)} %collective-permute-done.refs_3_), channel_id=1, source_target_pairs={{0,1},{1,0},{2,3},{3,2},{4,5},{5,4},{6,7},{7,6},{8,9},{9,8},{10,11... | collective-permute-start | bytes 294920 | tf_op jit(solution)/shard_map/ppermute | solution.py:20
  8.0 1.1 %collective-permute-done.4.refs_5_ = bf16[3,64,256]{2,1,0:T(8,128)(2,1)S(1)} collective-permute-done((bf16[3,64,256]{2,1,0:T(8,128)(2,1)}, bf16[3,64,256]{2,1,0:T(8,128)(2,1)S(1)}, u32[]{:S(2)}, u32[]{:S(2)}) %collective-permute-start.4) | collective-permute-done | bytes 98336 | tf_op jit(solution)/shard_map/ppermute | solution.py:20
  9.1 0.0 collective-permute-start.6
  9.1 0.2 collective-permute-done.5.refs_6_
  9.3 0.3 collective-permute-start.7
  9.6 0.0 collective-permute-done.2.refs_2_
  9.6 0.0 collective-permute-done.3.refs_4_
  9.6 1.0 %shard_map.38.refs_0_ = f32[9,256,128]{2,1,0:T(8,128)S(1)} custom-call(s32[1]{0:T(128)} %bitcast.me_ref, bf16[27,512,128]{2,1,0:T(8,128)(2,1)S(1)} %bitcast.4, bf16[3,64,256]{2,1,0:T(8,128)(2,1)S(1)} %bitcast.12, bf16[3,64,256]{2,1,0:T(8,128)(2,1)S(1)} %collective-permute-done.2.refs_2_, bf16[3,64,256]{2,1,0:T(8,128)(2,1)S(1)} %collective-permute-done.refs_3_, ...), custom_call_target="tpu_custom_call" | custom-call | flops 679477248 | bytes 2654208 | tf_op jit(solution)/shard_map/pallas_call | solution.py:24
  10.7 0.0 copy-start.1
  10.7 0.5 %shard_map.39 = (f32[256,128]{1,0:T(8,128)S(1)}, bf16[256,128]{1,0:T(8,128)(2,1)S(1)}) custom-call(s32[1]{0:T(128)} %bitcast.me_ref, f32[9,256,128]{2,1,0:T(8,128)S(1)} %shard_map.38.refs_0_, bf16[27,512,128]{2,1,0:T(8,128)(2,1)S(1)} %bitcast.5, bf16[3,64,256]{2,1,0:T(8,128)(2,1)S(1)} %collective-permute-done.6.refs_2_, ...), custom_call_target="tpu_custom_call" | custom-call | flops 226492416 | bytes 884736 | tf_op jit(solution)/shard_map/pallas_call | solution.py:24
  11.2 2.8 %collective-permute-start.8 = (bf16[256,128]{1,0:T(8,128)(2,1)S(1)}, bf16[256,128]{1,0:T(8,128)(2,1)S(1)}, u32[]{:S(2)}, u32[]{:S(2)}) collective-permute-start(bf16[256,128]{1,0:T(8,128)(2,1)S(1)} %get-tuple-element.29), channel_id=1, source_target_pairs={{0,8},{1,9},{2,10},{3,11},{4,12},{5,13},{6,14},{7,15},{8,0},{9,1},... | collective-permute-start | bytes 196616 | tf_op jit(solution)/shard_map/ppermute | solution.py:20
  14.1 0.3 %shard_map.40.weight_ref = bf16[1,2,512,256]{3,2,1,0:T(8,128)(2,1)S(1)} custom-call(s32[1]{0:T(128)} %bitcast.me_ref, bf16[9,256,128]{2,1,0:T(8,128)(2,1)S(1)} %bitcast.7), custom_call_target="tpu_custom_call" | custom-call | flops 1048576 | bytes 1114112 | tf_op jit(solution)/shard_map/pallas_call | solution.py:24
  14.4 0.3 %shard_map.41.weight_ref = bf16[1,2,512,256]{3,2,1,0:T(8,128)(2,1)S(1)} custom-call(s32[1]{0:T(128)} %bitcast.me_ref, bf16[9,256,128]{2,1,0:T(8,128)(2,1)S(1)} %collective-permute-done.1.tiles_ref), custom_call_target="tpu_custom_call" | custom-call | flops 1048576 | bytes 1114112 | tf_op jit(solution)/shard_map/pallas_call | solution.py:24
  14.7 3.3 %collective-permute-done.8.refs_1_ = bf16[256,128]{1,0:T(8,128)(2,1)S(1)} collective-permute-done((bf16[256,128]{1,0:T(8,128)(2,1)S(1)}, bf16[256,128]{1,0:T(8,128)(2,1)S(1)}, u32[]{:S(2)}, u32[]{:S(2)}) %collective-permute-start.8) | collective-permute-done | bytes 65568 | tf_op jit(solution)/shard_map/ppermute | solution.py:20
  18.0 0.1 collective-permute-start.9
  18.1 0.3 %shard_map.43.before_ref = f32[4,1,128,256]{3,2,1,0:T(8,128)S(1)} custom-call(s32[1]{0:T(128)} %bitcast.me_ref, bf16[256,128]{1,0:T(8,128)(2,1)S(1)} %shard_map.42.hidden_ref, bf16[1,2,512,256]{3,2,1,0:T(8,128)(2,1)S(1)} %shard_map.40.weight_ref), custom_call_target="tpu_custom_call" | custom-call | flops 134217728 | bytes 524288 | tf_op jit(solution)/shard_map/pallas_call | solution.py:24
  18.4 0.9 %collective-permute-done.9.hidden_ref = bf16[256,128]{1,0:T(8,128)(2,1)S(1)} collective-permute-done((bf16[256,128]{1,0:T(8,128)(2,1)S(1)}, bf16[256,128]{1,0:T(8,128)(2,1)S(1)}, u32[]{:S(2)}, u32[]{:S(2)}) %collective-permute-start.9) | collective-permute-done | bytes 65568 | tf_op jit(solution)/shard_map/ppermute | solution.py:20
  19.3 0.4 %shard_map.44 = (f32[1,128,256]{2,1,0:T(8,128)S(1)}, bf16[1,128,256]{2,1,0:T(8,128)(2,1)S(1)}, bf16[1,128,256]{2,1,0:T(8,128)(2,1)S(1)}, bf16[1,128,256]{2,1,0:T(8,128)(2,1)S(1)}) custom-call(s32[1]{0:T(128)} %bitcast.me_ref, f32[4,1,128,256]{3,2,1,0:T(8,128)S(1)} %shard_map.43.before_ref, bf16[256,128]{1,0:T(8,128)(2,1)S(1)} %collective-permute-done.9.hidden_ref, ...), custom_call_target="tpu_custom_call" | custom-call | flops 134217728 | bytes 524288 | tf_op jit(solution)/shard_map/pallas_call | solution.py:24
  19.7 1.7 %collective-permute-start.10 = (bf16[1,128,256]{2,1,0:T(8,128)(2,1)S(1)}, bf16[1,128,256]{2,1,0:T(8,128)(2,1)S(1)}, u32[]{:S(2)}, u32[]{:S(2)}) collective-permute-start(bf16[1,128,256]{2,1,0:T(8,128)(2,1)S(1)} %get-tuple-element.36), channel_id=1, source_target_pairs={{0,6},{1,7},{2,4},{3,5},{4,2},{5,3},{6,0},{7,1},{8,14},{9,15},{10,... | collective-permute-start | bytes 196616 | tf_op jit(solution)/shard_map/ppermute | solution.py:20
  21.3 0.6 %collective-permute-start.11 = (bf16[1,128,256]{2,1,0:T(8,128)(2,1)S(1)}, bf16[1,128,256]{2,1,0:T(8,128)(2,1)S(1)}, u32[]{:S(2)}, u32[]{:S(2)}) collective-permute-start(bf16[1,128,256]{2,1,0:T(8,128)(2,1)S(1)} %get-tuple-element.37), channel_id=1, source_target_pairs={{0,2},{1,3},{2,0},{3,1},{4,6},{5,7},{6,4},{7,5},{8,10},{9,11},{10,... | collective-permute-start | bytes 196616 | tf_op jit(solution)/shard_map/ppermute | solution.py:20
  21.9 1.3 %collective-permute-start.12 = (bf16[1,128,256]{2,1,0:T(8,128)(2,1)S(1)}, bf16[1,128,256]{2,1,0:T(8,128)(2,1)S(1)}, u32[]{:S(2)}, u32[]{:S(2)}) collective-permute-start(bf16[1,128,256]{2,1,0:T(8,128)(2,1)S(1)} %get-tuple-element.38), channel_id=1, source_target_pairs={{0,4},{1,5},{2,6},{3,7},{4,0},{5,1},{6,2},{7,3},{8,12},{9,13},{10,... | collective-permute-start | bytes 196616 | tf_op jit(solution)/shard_map/ppermute | solution.py:20
  23.2 1.7 %collective-permute-done.10.refs_0_ = bf16[1,128,256]{2,1,0:T(8,128)(2,1)S(1)} collective-permute-done((bf16[1,128,256]{2,1,0:T(8,128)(2,1)S(1)}, bf16[1,128,256]{2,1,0:T(8,128)(2,1)S(1)}, u32[]{:S(2)}, u32[]{:S(2)}) %collective-permute-start.10) | collective-permute-done | bytes 65568 | tf_op jit(solution)/shard_map/ppermute | solution.py:20
  25.0 1.2 %collective-permute-done.11.refs_1_ = bf16[1,128,256]{2,1,0:T(8,128)(2,1)S(1)} collective-permute-done((bf16[1,128,256]{2,1,0:T(8,128)(2,1)S(1)}, bf16[1,128,256]{2,1,0:T(8,128)(2,1)S(1)}, u32[]{:S(2)}, u32[]{:S(2)}) %collective-permute-start.11) | collective-permute-done | bytes 65568 | tf_op jit(solution)/shard_map/ppermute | solution.py:20
  26.2 0.1 collective-permute-done.12.refs_2_
  26.3 0.8 %shard_map.45 = bf16[1,256,128]{2,1,0:T(8,128)(2,1)} custom-call(s32[1]{0:T(128)} %bitcast.me_ref, bf16[128,128]{1,0:T(8,128)(2,1)S(1)} %shard_map.37.spread_ref, f32[1,128,256]{2,1,0:T(8,128)S(1)} %get-tuple-element.35.own_ref, bf16[1,128,256]{2,1,0:T(8,128)(2,1)S(1)} %collective-permute-done.10.refs_0_, ...), custom_call_target="tpu_custom_call" | custom-call | flops 32768 | bytes 393216 | tf_op jit(solution)/shard_map/pallas_call | solution.py:24
  (9 shorter events, 0.1 us)
Async XLA Ops:
  0.0 7.4 %collective-permute-start = (bf16[3,64,256]{2,1,0:T(8,128)(2,1)}, bf16[3,64,256]{2,1,0:T(8,128)(2,1)S(1)}, u32[]{:S(2)}, u32[]{:S(2)}) collective-permute-start(bf16[3,64,256]{2,1,0:T(8,128)(2,1)} %bitcast.8), channel_id=1, source_target_pairs={{0,6},{1,7},{2,4},{3,5},{4,2},{5,3},{6,0},{7,1},{8,14},{9,15},{10,... | collective-permute-start | bytes 294920 | tf_op jit(solution)/shard_map/ppermute | solution.py:20
  4.0 5.1 %collective-permute-start.4 = (bf16[3,64,256]{2,1,0:T(8,128)(2,1)}, bf16[3,64,256]{2,1,0:T(8,128)(2,1)S(1)}, u32[]{:S(2)}, u32[]{:S(2)}) collective-permute-start(bf16[3,64,256]{2,1,0:T(8,128)(2,1)} %bitcast.9), channel_id=1, source_target_pairs={{0,2},{1,3},{2,0},{3,1},{4,6},{5,7},{6,4},{7,5},{8,10},{9,11},{10,... | collective-permute-start | bytes 294920 | tf_op jit(solution)/shard_map/ppermute | solution.py:20
  4.5 4.8 %collective-permute-start.5 = (bf16[3,64,256]{2,1,0:T(8,128)(2,1)}, bf16[3,64,256]{2,1,0:T(8,128)(2,1)S(1)}, u32[]{:S(2)}, u32[]{:S(2)}) collective-permute-start(bf16[3,64,256]{2,1,0:T(8,128)(2,1)} %bitcast.10), channel_id=1, source_target_pairs={{0,4},{1,5},{2,6},{3,7},{4,0},{5,1},{6,2},{7,3},{8,12},{9,13},{10,... | collective-permute-start | bytes 294920 | tf_op jit(solution)/shard_map/ppermute | solution.py:20
  4.5 2.9 %collective-permute-start.1 = (bf16[9,256,128]{2,1,0:T(8,128)(2,1)}, bf16[9,256,128]{2,1,0:T(8,128)(2,1)S(1)}, u32[]{:S(2)}, u32[]{:S(2)}) collective-permute-start(bf16[9,256,128]{2,1,0:T(8,128)(2,1)} %bitcast.6), channel_id=1, source_target_pairs={{0,1},{1,0},{2,3},{3,2},{4,5},{5,4},{6,7},{7,6},{8,9},{9,8},{10,11... | collective-permute-start | bytes 1769480 | tf_op jit(solution)/shard_map/ppermute | solution.py:20
  4.6 2.9 %copy-start.2 = (bf16[64,3,256]{2,0,1:T(8,128)(2,1)S(1)}, bf16[64,3,256]{2,0,1:T(8,128)(2,1)}, u32[]{:S(2)}) copy-start(bf16[64,3,256]{2,0,1:T(8,128)(2,1)} %param.3) | copy-start | bytes 294916
  4.6 5.1 %copy-start = (bf16[1,27,512,128]{3,2,1,0:T(8,128)(2,1)S(1)}, bf16[1,27,512,128]{3,2,1,0:T(8,128)(2,1)}, u32[]{:S(2)}) copy-start(bf16[1,27,512,128]{3,2,1,0:T(8,128)(2,1)} %param.4) | copy-start | bytes 10616836
  7.5 2.2 %collective-permute-start.2 = (bf16[3,64,256]{2,1,0:T(8,128)(2,1)S(1)}, bf16[3,64,256]{2,1,0:T(8,128)(2,1)S(1)}, u32[]{:S(2)}, u32[]{:S(2)}) collective-permute-start(bf16[3,64,256]{2,1,0:T(8,128)(2,1)S(1)} %bitcast.11), channel_id=1, source_target_pairs={{0,1},{1,0},{2,3},{3,2},{4,5},{5,4},{6,7},{7,6},{8,9},{9,8},{10,11... | collective-permute-start | bytes 294920 | tf_op jit(solution)/shard_map/ppermute | solution.py:20
  7.5 2.1 %collective-permute-start.3 = (bf16[3,64,256]{2,1,0:T(8,128)(2,1)S(1)}, bf16[3,64,256]{2,1,0:T(8,128)(2,1)S(1)}, u32[]{:S(2)}, u32[]{:S(2)}) collective-permute-start(bf16[3,64,256]{2,1,0:T(8,128)(2,1)S(1)} %collective-permute-done.refs_3_), channel_id=1, source_target_pairs={{0,1},{1,0},{2,3},{3,2},{4,5},{5,4},{6,7},{7,6},{8,9},{9,8},{10,11... | collective-permute-start | bytes 294920 | tf_op jit(solution)/shard_map/ppermute | solution.py:20
  9.1 1.6 %collective-permute-start.6 = (bf16[3,64,256]{2,1,0:T(8,128)(2,1)S(1)}, bf16[3,64,256]{2,1,0:T(8,128)(2,1)S(1)}, u32[]{:S(2)}, u32[]{:S(2)}) collective-permute-start(bf16[3,64,256]{2,1,0:T(8,128)(2,1)S(1)} %collective-permute-done.4.refs_5_), channel_id=1, source_target_pairs={{0,1},{1,0},{2,3},{3,2},{4,5},{5,4},{6,7},{7,6},{8,9},{9,8},{10,11... | collective-permute-start | bytes 294920 | tf_op jit(solution)/shard_map/ppermute | solution.py:20
  9.3 1.4 %collective-permute-start.7 = (bf16[3,64,256]{2,1,0:T(8,128)(2,1)S(1)}, bf16[3,64,256]{2,1,0:T(8,128)(2,1)S(1)}, u32[]{:S(2)}, u32[]{:S(2)}) collective-permute-start(bf16[3,64,256]{2,1,0:T(8,128)(2,1)S(1)} %collective-permute-done.5.refs_6_), channel_id=1, source_target_pairs={{0,1},{1,0},{2,3},{3,2},{4,5},{5,4},{6,7},{7,6},{8,9},{9,8},{10,11... | collective-permute-start | bytes 294920 | tf_op jit(solution)/shard_map/ppermute | solution.py:20
  10.7 3.4 %copy-start.1 = (bf16[1,9,256,128]{3,2,1,0:T(8,128)(2,1)S(1)}, bf16[1,9,256,128]{3,2,1,0:T(8,128)(2,1)}, u32[]{:S(2)}) copy-start(bf16[1,9,256,128]{3,2,1,0:T(8,128)(2,1)} %param.5) | copy-start | bytes 1769476
  11.2 6.7 %collective-permute-start.8 = (bf16[256,128]{1,0:T(8,128)(2,1)S(1)}, bf16[256,128]{1,0:T(8,128)(2,1)S(1)}, u32[]{:S(2)}, u32[]{:S(2)}) collective-permute-start(bf16[256,128]{1,0:T(8,128)(2,1)S(1)} %get-tuple-element.29), channel_id=1, source_target_pairs={{0,8},{1,9},{2,10},{3,11},{4,12},{5,13},{6,14},{7,15},{8,0},{9,1},... | collective-permute-start | bytes 196616 | tf_op jit(solution)/shard_map/ppermute | solution.py:20
  18.0 1.3 %collective-permute-start.9 = (bf16[256,128]{1,0:T(8,128)(2,1)S(1)}, bf16[256,128]{1,0:T(8,128)(2,1)S(1)}, u32[]{:S(2)}, u32[]{:S(2)}) collective-permute-start(bf16[256,128]{1,0:T(8,128)(2,1)S(1)} %shard_map.42.hidden_ref), channel_id=1, source_target_pairs={{0,1},{1,0},{2,3},{3,2},{4,5},{5,4},{6,7},{7,6},{8,9},{9,8},{10,11... | collective-permute-start | bytes 196616 | tf_op jit(solution)/shard_map/ppermute | solution.py:20
  19.7 5.3 %collective-permute-start.10 = (bf16[1,128,256]{2,1,0:T(8,128)(2,1)S(1)}, bf16[1,128,256]{2,1,0:T(8,128)(2,1)S(1)}, u32[]{:S(2)}, u32[]{:S(2)}) collective-permute-start(bf16[1,128,256]{2,1,0:T(8,128)(2,1)S(1)} %get-tuple-element.36), channel_id=1, source_target_pairs={{0,6},{1,7},{2,4},{3,5},{4,2},{5,3},{6,0},{7,1},{8,14},{9,15},{10,... | collective-permute-start | bytes 196616 | tf_op jit(solution)/shard_map/ppermute | solution.py:20
  21.3 4.9 %collective-permute-start.11 = (bf16[1,128,256]{2,1,0:T(8,128)(2,1)S(1)}, bf16[1,128,256]{2,1,0:T(8,128)(2,1)S(1)}, u32[]{:S(2)}, u32[]{:S(2)}) collective-permute-start(bf16[1,128,256]{2,1,0:T(8,128)(2,1)S(1)} %get-tuple-element.37), channel_id=1, source_target_pairs={{0,2},{1,3},{2,0},{3,1},{4,6},{5,7},{6,4},{7,5},{8,10},{9,11},{10,... | collective-permute-start | bytes 196616 | tf_op jit(solution)/shard_map/ppermute | solution.py:20
  21.9 4.4 %collective-permute-start.12 = (bf16[1,128,256]{2,1,0:T(8,128)(2,1)S(1)}, bf16[1,128,256]{2,1,0:T(8,128)(2,1)S(1)}, u32[]{:S(2)}, u32[]{:S(2)}) collective-permute-start(bf16[1,128,256]{2,1,0:T(8,128)(2,1)S(1)} %get-tuple-element.38), channel_id=1, source_target_pairs={{0,4},{1,5},{2,6},{3,7},{4,0},{5,1},{6,2},{7,3},{8,12},{9,13},{10,... | collective-permute-start | bytes 196616 | tf_op jit(solution)/shard_map/ppermute | solution.py:20

commit v6 on v5

--- a/solution.py
+++ b/solution.py
@@ -88,7 +88,10 @@
     refs = list(refs)
     before_ref = None if first else refs.pop(0)
     weight_ref = refs.pop(0)
-    pieces = [refs.pop(0) for _ in masks or (0,)]
+    pieces = []
+    while len(pieces) < max(len(masks), 1):
+        ref = refs.pop(0)
+        pieces += [ref] if len(ref.shape) == 3 else [ref.at[i] for i in range(ref.shape[0])]
     *out_refs, order_ref = refs
     frames_of, _, voxels = pieces[0].shape
     channels = order_ref.shape[0] // frames_of
@@ -133,6 +136,12 @@
     out_refs[1][...] = total.astype(BF)
 
 
+def pack_body(me_ref, *refs):
+    *block_refs, out_ref = refs
+    for i, block_ref in enumerate(block_refs):
+        out_ref[i] = block_ref[...]
+
+
 def silu_body(me_ref, *refs):
     *sum_refs, hidden_ref = refs
     pre = sum_refs[0][...]
@@ -256,24 +265,33 @@
         (pieces[far], spread, mate_tiles)
     )
     pieces[0], spread = lax.optimization_barrier((mine, spread))
-    for mask in range(0, share, 2):
-        pieces[mask + 1] = swap(pieces[mask], 1)
     weights = conv_tiles[0]
     if part % 16:
+        for mask in range(0, share, 2):
+            pieces[mask + 1] = swap(pieces[mask], 1)
         for mask in [1 << level for level in range(share.bit_length() - 1)]:
             pieces = [
                 jnp.where(index & mask != 0, pieces[j ^ mask], pieces[j]) for j in range(share)
             ]
-        steps = [()]
-        pieces = [jnp.concatenate(pieces, 1)]
+        steps = [((), [jnp.concatenate(pieces, 1)])]
     else:
-        steps = [(0, 1, far, far + 1, *near), tuple(mask + 1 for mask in near)]
+
+        def mates(masks):
+            blocks = [pieces[mask] for mask in masks]
+            packed = shape((len(blocks), *mine.shape), BF)
+            return swap(local(pack_body, packed, [], 0, 2 * packed.size, me, *blocks), 1)
+
+        near_mates, far_mates = mates(near), mates((0, far))
+        direct = (0, far, *near)
+        steps = [
+            ((*direct, 1, far + 1), [pieces[mask] for mask in direct] + [far_mates]),
+            (tuple(mask + 1 for mask in near), [near_mates]),
+        ]
 
     before = []
-    for i, masks in enumerate(steps):
+    for i, (masks, parts) in enumerate(steps):
         first, last = i == 0, i == len(steps) - 1
-        parts = [pieces[mask] for mask in masks] or pieces
-        depth = sum(block.shape[1] for block in parts)
+        depth = part * len(masks) or channels
         outs = [shape((voxels, filters), F32), shape((voxels, filters), BF)]
         if not last:
             outs = [shape((9, voxels, filters), F32)]

time: 27.2 us -> 27.2 us (level)
  starting transfers between devices: 11.8 us -> 11 us
  waiting for transfers between devices: 11.5 us -> 12.3 us
    ppermute x13 -> x11, starting transfers between devices: 11.8 us -> 11 us  [swap(): return lax.ppermute(block, 'rows', [(i, i ^ mask) for i in range(count)])]
    ppermute x13 -> x11, waiting for transfers between devices: 11.5 us -> 12.3 us  [swap(): return lax.ppermute(block, 'rows', [(i, i ^ mask) for i in range(count)])]
    pallas_call x9 -> x11, Pallas kernels: 3.65 us -> 3.68 us  [local(): pl.pallas_call(body, out_shape=outs, in_specs=[SMEM] + [VMEM] * len(args)...]
  transfers between devices with their start and end apart: 13 -> 11, of which waited for: 8 -> 8; matrix products, arithmetic and copies ran while one was open for 0% -> 0% of each run, Pallas kernels for 7% -> 7%
where the time goes in v6:
time: 27.2 us; the launch traced here: 27.1 us
  waiting for transfers between devices  12.3 us (45%)
  starting transfers between devices  11 us (40%)
  Pallas kernels  3.68 us (14%)
    ppermute x11, waiting for transfers between devices, swap(): return lax.ppermute(block, 'rows', [(i, i ^ mask) for i in range(count)])  12.3 us
    ppermute x11, starting transfers between devices, swap(): return lax.ppermute(block, 'rows', [(i, i ^ mask) for i in range(count)])  11 us
    pallas_call x11, Pallas kernels, local(): pl.pallas_call(body, out_shape=outs, in_specs=[SMEM] + [VMEM] * len(args)...  3.68 us
  transfers between devices with their start and end apart: 11, of which 8 were waited for; matrix products, arithmetic and copies ran while one was open for 0% of the time, Pallas kernels for 7%

profile of v6, /device:TPU:0, one launch (start us, length us, event | category | flops | bytes accessed | tf_op | source)
XLA Modules:
  0.0 27.1 jit_solution(11746740874623781352)
XLA Ops:
  0.0 4.0 %collective-permute-start = (bf16[3,64,256]{2,1,0:T(8,128)(2,1)}, bf16[3,64,256]{2,1,0:T(8,128)(2,1)S(1)}, u32[]{:S(2)}, u32[]{:S(2)}) collective-permute-start(bf16[3,64,256]{2,1,0:T(8,128)(2,1)} %bitcast.8), channel_id=1, source_target_pairs={{0,6},{1,7},{2,4},{3,5},{4,2},{5,3},{6,0},{7,1},{8,14},{9,15},{10,... | collective-permute-start | bytes 294920 | tf_op jit(solution)/shard_map/ppermute | solution.py:20
  4.0 0.5 %collective-permute-start.2 = (bf16[3,64,256]{2,1,0:T(8,128)(2,1)}, bf16[3,64,256]{2,1,0:T(8,128)(2,1)S(1)}, u32[]{:S(2)}, u32[]{:S(2)}) collective-permute-start(bf16[3,64,256]{2,1,0:T(8,128)(2,1)} %bitcast.9), channel_id=1, source_target_pairs={{0,2},{1,3},{2,0},{3,1},{4,6},{5,7},{6,4},{7,5},{8,10},{9,11},{10,... | collective-permute-start | bytes 294920 | tf_op jit(solution)/shard_map/ppermute | solution.py:20
  4.5 0.1 collective-permute-start.3
  4.5 0.0 collective-permute-start.1
  4.6 2.9 %collective-permute-done.refs_1_.refs_2_ = bf16[3,64,256]{2,1,0:T(8,128)(2,1)S(1)} collective-permute-done((bf16[3,64,256]{2,1,0:T(8,128)(2,1)}, bf16[3,64,256]{2,1,0:T(8,128)(2,1)S(1)}, u32[]{:S(2)}, u32[]{:S(2)}) %collective-permute-start) | collective-permute-done | bytes 98336 | tf_op jit(solution)/shard_map/ppermute | solution.py:20
  7.5 0.0 collective-permute-done.1.tiles_ref
  7.5 0.0 copy-done.2
  7.5 0.1 collective-permute-start.4
  7.6 1.5 %collective-permute-done.2.refs_3_.refs_0_ = bf16[3,64,256]{2,1,0:T(8,128)(2,1)S(1)} collective-permute-done((bf16[3,64,256]{2,1,0:T(8,128)(2,1)}, bf16[3,64,256]{2,1,0:T(8,128)(2,1)S(1)}, u32[]{:S(2)}, u32[]{:S(2)}) %collective-permute-start.2) | collective-permute-done | bytes 98336 | tf_op jit(solution)/shard_map/ppermute | solution.py:20
  9.1 0.2 collective-permute-done.3.refs_4_.refs_1_
  9.4 0.1 collective-permute-start.5
  9.4 0.0 collective-permute-done.4.refs_5_
  9.4 0.0 copy-done
  9.5 1.1 %shard_map.39.refs_0_ = f32[9,256,128]{2,1,0:T(8,128)S(1)} custom-call(s32[1]{0:T(128)} %bitcast.me_ref, bf16[27,512,128]{2,1,0:T(8,128)(2,1)S(1)} %bitcast.4, bf16[3,64,256]{2,1,0:T(8,128)(2,1)S(1)} %bitcast.12, bf16[3,64,256]{2,1,0:T(8,128)(2,1)S(1)} %collective-permute-done.refs_1_.refs_2_, ...), custom_call_target="tpu_custom_call" | custom-call | flops 679477248 | bytes 2654208 | tf_op jit(solution)/shard_map/pallas_call | solution.py:24
  10.5 0.0 copy-start.1
  10.5 0.3 %collective-permute-done.5.refs_2_ = bf16[2,3,64,256]{3,2,1,0:T(8,128)(2,1)S(1)} collective-permute-done((bf16[2,3,64,256]{3,2,1,0:T(8,128)(2,1)S(1)}, bf16[2,3,64,256]{3,2,1,0:T(8,128)(2,1)S(1)}, u32[]{:S(2)}, u32[]{:S(2)}) %collective-permute-start.5) | collective-permute-done | bytes 196640 | tf_op jit(solution)/shard_map/ppermute | solution.py:20
  10.9 0.5 %shard_map.41 = (f32[256,128]{1,0:T(8,128)S(1)}, bf16[256,128]{1,0:T(8,128)(2,1)S(1)}) custom-call(s32[1]{0:T(128)} %bitcast.me_ref, f32[9,256,128]{2,1,0:T(8,128)S(1)} %shard_map.39.refs_0_, bf16[27,512,128]{2,1,0:T(8,128)(2,1)S(1)} %bitcast.5, bf16[2,3,64,256]{3,2,1,0:T(8,128)(2,1)S(1)} %collective-permute-done.5.refs_2_), custom_call_target="tpu_custom_call" | custom-call | flops 226492416 | bytes 884736 | tf_op jit(solution)/shard_map/pallas_call | solution.py:24
  11.4 2.7 %collective-permute-start.6 = (bf16[256,128]{1,0:T(8,128)(2,1)S(1)}, bf16[256,128]{1,0:T(8,128)(2,1)S(1)}, u32[]{:S(2)}, u32[]{:S(2)}) collective-permute-start(bf16[256,128]{1,0:T(8,128)(2,1)S(1)} %get-tuple-element.29), channel_id=1, source_target_pairs={{0,8},{1,9},{2,10},{3,11},{4,12},{5,13},{6,14},{7,15},{8,0},{9,1},... | collective-permute-start | bytes 196616 | tf_op jit(solution)/shard_map/ppermute | solution.py:20
  14.1 0.3 %shard_map.42.weight_ref = bf16[1,2,512,256]{3,2,1,0:T(8,128)(2,1)S(1)} custom-call(s32[1]{0:T(128)} %bitcast.me_ref, bf16[9,256,128]{2,1,0:T(8,128)(2,1)S(1)} %bitcast.7), custom_call_target="tpu_custom_call" | custom-call | flops 1048576 | bytes 1114112 | tf_op jit(solution)/shard_map/pallas_call | solution.py:24
  14.3 0.3 %shard_map.43.weight_ref = bf16[1,2,512,256]{3,2,1,0:T(8,128)(2,1)S(1)} custom-call(s32[1]{0:T(128)} %bitcast.me_ref, bf16[9,256,128]{2,1,0:T(8,128)(2,1)S(1)} %collective-permute-done.1.tiles_ref), custom_call_target="tpu_custom_call" | custom-call | flops 1048576 | bytes 1114112 | tf_op jit(solution)/shard_map/pallas_call | solution.py:24
  14.6 3.4 %collective-permute-done.6.refs_1_ = bf16[256,128]{1,0:T(8,128)(2,1)S(1)} collective-permute-done((bf16[256,128]{1,0:T(8,128)(2,1)S(1)}, bf16[256,128]{1,0:T(8,128)(2,1)S(1)}, u32[]{:S(2)}, u32[]{:S(2)}) %collective-permute-start.6) | collective-permute-done | bytes 65568 | tf_op jit(solution)/shard_map/ppermute | solution.py:20
  18.1 0.1 collective-permute-start.7
  18.2 0.3 %shard_map.45.before_ref = f32[4,1,128,256]{3,2,1,0:T(8,128)S(1)} custom-call(s32[1]{0:T(128)} %bitcast.me_ref, bf16[256,128]{1,0:T(8,128)(2,1)S(1)} %shard_map.44.hidden_ref, bf16[1,2,512,256]{3,2,1,0:T(8,128)(2,1)S(1)} %shard_map.42.weight_ref), custom_call_target="tpu_custom_call" | custom-call | flops 134217728 | bytes 524288 | tf_op jit(solution)/shard_map/pallas_call | solution.py:24
  18.5 0.9 %collective-permute-done.7.hidden_ref = bf16[256,128]{1,0:T(8,128)(2,1)S(1)} collective-permute-done((bf16[256,128]{1,0:T(8,128)(2,1)S(1)}, bf16[256,128]{1,0:T(8,128)(2,1)S(1)}, u32[]{:S(2)}, u32[]{:S(2)}) %collective-permute-start.7) | collective-permute-done | bytes 65568 | tf_op jit(solution)/shard_map/ppermute | solution.py:20
  19.4 0.4 %shard_map.46 = (f32[1,128,256]{2,1,0:T(8,128)S(1)}, bf16[1,128,256]{2,1,0:T(8,128)(2,1)S(1)}, bf16[1,128,256]{2,1,0:T(8,128)(2,1)S(1)}, bf16[1,128,256]{2,1,0:T(8,128)(2,1)S(1)}) custom-call(s32[1]{0:T(128)} %bitcast.me_ref, f32[4,1,128,256]{3,2,1,0:T(8,128)S(1)} %shard_map.45.before_ref, bf16[256,128]{1,0:T(8,128)(2,1)S(1)} %collective-permute-done.7.hidden_ref, ...), custom_call_target="tpu_custom_call" | custom-call | flops 134217728 | bytes 524288 | tf_op jit(solution)/shard_map/pallas_call | solution.py:24
  19.8 1.6 %collective-permute-start.8 = (bf16[1,128,256]{2,1,0:T(8,128)(2,1)S(1)}, bf16[1,128,256]{2,1,0:T(8,128)(2,1)S(1)}, u32[]{:S(2)}, u32[]{:S(2)}) collective-permute-start(bf16[1,128,256]{2,1,0:T(8,128)(2,1)S(1)} %get-tuple-element.36), channel_id=1, source_target_pairs={{0,6},{1,7},{2,4},{3,5},{4,2},{5,3},{6,0},{7,1},{8,14},{9,15},{10,... | collective-permute-start | bytes 196616 | tf_op jit(solution)/shard_map/ppermute | solution.py:20
  21.3 0.5 %collective-permute-start.9 = (bf16[1,128,256]{2,1,0:T(8,128)(2,1)S(1)}, bf16[1,128,256]{2,1,0:T(8,128)(2,1)S(1)}, u32[]{:S(2)}, u32[]{:S(2)}) collective-permute-start(bf16[1,128,256]{2,1,0:T(8,128)(2,1)S(1)} %get-tuple-element.37), channel_id=1, source_target_pairs={{0,2},{1,3},{2,0},{3,1},{4,6},{5,7},{6,4},{7,5},{8,10},{9,11},{10,... | collective-permute-start | bytes 196616 | tf_op jit(solution)/shard_map/ppermute | solution.py:20
  21.8 1.5 %collective-permute-start.10 = (bf16[1,128,256]{2,1,0:T(8,128)(2,1)S(1)}, bf16[1,128,256]{2,1,0:T(8,128)(2,1)S(1)}, u32[]{:S(2)}, u32[]{:S(2)}) collective-permute-start(bf16[1,128,256]{2,1,0:T(8,128)(2,1)S(1)} %get-tuple-element.38), channel_id=1, source_target_pairs={{0,4},{1,5},{2,6},{3,7},{4,0},{5,1},{6,2},{7,3},{8,12},{9,13},{10,... | collective-permute-start | bytes 196616 | tf_op jit(solution)/shard_map/ppermute | solution.py:20
  23.3 1.7 %collective-permute-done.8.refs_0_ = bf16[1,128,256]{2,1,0:T(8,128)(2,1)S(1)} collective-permute-done((bf16[1,128,256]{2,1,0:T(8,128)(2,1)S(1)}, bf16[1,128,256]{2,1,0:T(8,128)(2,1)S(1)}, u32[]{:S(2)}, u32[]{:S(2)}) %collective-permute-start.8) | collective-permute-done | bytes 65568 | tf_op jit(solution)/shard_map/ppermute | solution.py:20
  25.1 1.2 %collective-permute-done.9.refs_1_ = bf16[1,128,256]{2,1,0:T(8,128)(2,1)S(1)} collective-permute-done((bf16[1,128,256]{2,1,0:T(8,128)(2,1)S(1)}, bf16[1,128,256]{2,1,0:T(8,128)(2,1)S(1)}, u32[]{:S(2)}, u32[]{:S(2)}) %collective-permute-start.9) | collective-permute-done | bytes 65568 | tf_op jit(solution)/shard_map/ppermute | solution.py:20
  26.3 0.0 collective-permute-done.10.refs_2_
  26.3 0.8 %shard_map.47 = bf16[1,256,128]{2,1,0:T(8,128)(2,1)} custom-call(s32[1]{0:T(128)} %bitcast.me_ref, bf16[128,128]{1,0:T(8,128)(2,1)S(1)} %shard_map.37.spread_ref, f32[1,128,256]{2,1,0:T(8,128)S(1)} %get-tuple-element.35.own_ref, bf16[1,128,256]{2,1,0:T(8,128)(2,1)S(1)} %collective-permute-done.8.refs_0_, ...), custom_call_target="tpu_custom_call" | custom-call | flops 32768 | bytes 393216 | tf_op jit(solution)/shard_map/pallas_call | solution.py:24
  (7 shorter events, 0.1 us)
Async XLA Ops:
  0.0 7.4 %collective-permute-start = (bf16[3,64,256]{2,1,0:T(8,128)(2,1)}, bf16[3,64,256]{2,1,0:T(8,128)(2,1)S(1)}, u32[]{:S(2)}, u32[]{:S(2)}) collective-permute-start(bf16[3,64,256]{2,1,0:T(8,128)(2,1)} %bitcast.8), channel_id=1, source_target_pairs={{0,6},{1,7},{2,4},{3,5},{4,2},{5,3},{6,0},{7,1},{8,14},{9,15},{10,... | collective-permute-start | bytes 294920 | tf_op jit(solution)/shard_map/ppermute | solution.py:20
  4.0 5.1 %collective-permute-start.2 = (bf16[3,64,256]{2,1,0:T(8,128)(2,1)}, bf16[3,64,256]{2,1,0:T(8,128)(2,1)S(1)}, u32[]{:S(2)}, u32[]{:S(2)}) collective-permute-start(bf16[3,64,256]{2,1,0:T(8,128)(2,1)} %bitcast.9), channel_id=1, source_target_pairs={{0,2},{1,3},{2,0},{3,1},{4,6},{5,7},{6,4},{7,5},{8,10},{9,11},{10,... | collective-permute-start | bytes 294920 | tf_op jit(solution)/shard_map/ppermute | solution.py:20
  4.5 4.8 %collective-permute-start.3 = (bf16[3,64,256]{2,1,0:T(8,128)(2,1)}, bf16[3,64,256]{2,1,0:T(8,128)(2,1)S(1)}, u32[]{:S(2)}, u32[]{:S(2)}) collective-permute-start(bf16[3,64,256]{2,1,0:T(8,128)(2,1)} %bitcast.10), channel_id=1, source_target_pairs={{0,4},{1,5},{2,6},{3,7},{4,0},{5,1},{6,2},{7,3},{8,12},{9,13},{10,... | collective-permute-start | bytes 294920 | tf_op jit(solution)/shard_map/ppermute | solution.py:20
  4.5 2.9 %collective-permute-start.1 = (bf16[9,256,128]{2,1,0:T(8,128)(2,1)}, bf16[9,256,128]{2,1,0:T(8,128)(2,1)S(1)}, u32[]{:S(2)}, u32[]{:S(2)}) collective-permute-start(bf16[9,256,128]{2,1,0:T(8,128)(2,1)} %bitcast.6), channel_id=1, source_target_pairs={{0,1},{1,0},{2,3},{3,2},{4,5},{5,4},{6,7},{7,6},{8,9},{9,8},{10,11... | collective-permute-start | bytes 1769480 | tf_op jit(solution)/shard_map/ppermute | solution.py:20
  4.6 2.9 %copy-start.2 = (bf16[64,3,256]{2,0,1:T(8,128)(2,1)S(1)}, bf16[64,3,256]{2,0,1:T(8,128)(2,1)}, u32[]{:S(2)}) copy-start(bf16[64,3,256]{2,0,1:T(8,128)(2,1)} %param.3) | copy-start | bytes 294916
  4.6 4.9 %copy-start = (bf16[1,27,512,128]{3,2,1,0:T(8,128)(2,1)S(1)}, bf16[1,27,512,128]{3,2,1,0:T(8,128)(2,1)}, u32[]{:S(2)}) copy-start(bf16[1,27,512,128]{3,2,1,0:T(8,128)(2,1)} %param.4) | copy-start | bytes 10616836
  7.5 2.0 %collective-permute-start.4 = (bf16[2,3,64,256]{3,2,1,0:T(8,128)(2,1)S(1)}, bf16[2,3,64,256]{3,2,1,0:T(8,128)(2,1)S(1)}, u32[]{:S(2)}, u32[]{:S(2)}) collective-permute-start(bf16[2,3,64,256]{3,2,1,0:T(8,128)(2,1)S(1)} %shard_map.38), channel_id=1, source_target_pairs={{0,1},{1,0},{2,3},{3,2},{4,5},{5,4},{6,7},{7,6},{8,9},{9,8},{10,11... | collective-permute-start | bytes 589832 | tf_op jit(solution)/shard_map/ppermute | solution.py:20
  9.4 1.5 %collective-permute-start.5 = (bf16[2,3,64,256]{3,2,1,0:T(8,128)(2,1)S(1)}, bf16[2,3,64,256]{3,2,1,0:T(8,128)(2,1)S(1)}, u32[]{:S(2)}, u32[]{:S(2)}) collective-permute-start(bf16[2,3,64,256]{3,2,1,0:T(8,128)(2,1)S(1)} %shard_map.40), channel_id=1, source_target_pairs={{0,1},{1,0},{2,3},{3,2},{4,5},{5,4},{6,7},{7,6},{8,9},{9,8},{10,11... | collective-permute-start | bytes 589832 | tf_op jit(solution)/shard_map/ppermute | solution.py:20
  10.5 3.5 %copy-start.1 = (bf16[1,9,256,128]{3,2,1,0:T(8,128)(2,1)S(1)}, bf16[1,9,256,128]{3,2,1,0:T(8,128)(2,1)}, u32[]{:S(2)}) copy-start(bf16[1,9,256,128]{3,2,1,0:T(8,128)(2,1)} %param.5) | copy-start | bytes 1769476
  11.4 6.6 %collective-permute-start.6 = (bf16[256,128]{1,0:T(8,128)(2,1)S(1)}, bf16[256,128]{1,0:T(8,128)(2,1)S(1)}, u32[]{:S(2)}, u32[]{:S(2)}) collective-permute-start(bf16[256,128]{1,0:T(8,128)(2,1)S(1)} %get-tuple-element.29), channel_id=1, source_target_pairs={{0,8},{1,9},{2,10},{3,11},{4,12},{5,13},{6,14},{7,15},{8,0},{9,1},... | collective-permute-start | bytes 196616 | tf_op jit(solution)/shard_map/ppermute | solution.py:20
  18.1 1.3 %collective-permute-start.7 = (bf16[256,128]{1,0:T(8,128)(2,1)S(1)}, bf16[256,128]{1,0:T(8,128)(2,1)S(1)}, u32[]{:S(2)}, u32[]{:S(2)}) collective-permute-start(bf16[256,128]{1,0:T(8,128)(2,1)S(1)} %shard_map.44.hidden_ref), channel_id=1, source_target_pairs={{0,1},{1,0},{2,3},{3,2},{4,5},{5,4},{6,7},{7,6},{8,9},{9,8},{10,11... | collective-permute-start | bytes 196616 | tf_op jit(solution)/shard_map/ppermute | solution.py:20
  19.8 5.3 %collective-permute-start.8 = (bf16[1,128,256]{2,1,0:T(8,128)(2,1)S(1)}, bf16[1,128,256]{2,1,0:T(8,128)(2,1)S(1)}, u32[]{:S(2)}, u32[]{:S(2)}) collective-permute-start(bf16[1,128,256]{2,1,0:T(8,128)(2,1)S(1)} %get-tuple-element.36), channel_id=1, source_target_pairs={{0,6},{1,7},{2,4},{3,5},{4,2},{5,3},{6,0},{7,1},{8,14},{9,15},{10,... | collective-permute-start | bytes 196616 | tf_op jit(solution)/shard_map/ppermute | solution.py:20
  21.3 5.0 %collective-permute-start.9 = (bf16[1,128,256]{2,1,0:T(8,128)(2,1)S(1)}, bf16[1,128,256]{2,1,0:T(8,128)(2,1)S(1)}, u32[]{:S(2)}, u32[]{:S(2)}) collective-permute-start(bf16[1,128,256]{2,1,0:T(8,128)(2,1)S(1)} %get-tuple-element.37), channel_id=1, source_target_pairs={{0,2},{1,3},{2,0},{3,1},{4,6},{5,7},{6,4},{7,5},{8,10},{9,11},{10,... | collective-permute-start | bytes 196616 | tf_op jit(solution)/shard_map/ppermute | solution.py:20
  21.8 4.5 %collective-permute-start.10 = (bf16[1,128,256]{2,1,0:T(8,128)(2,1)S(1)}, bf16[1,128,256]{2,1,0:T(8,128)(2,1)S(1)}, u32[]{:S(2)}, u32[]{:S(2)}) collective-permute-start(bf16[1,128,256]{2,1,0:T(8,128)(2,1)S(1)} %get-tuple-element.38), channel_id=1, source_target_pairs={{0,4},{1,5},{2,6},{3,7},{4,0},{5,1},{6,2},{7,3},{8,12},{9,13},{10,... | collective-permute-start | bytes 196616 | tf_op jit(solution)/shard_map/ppermute | solution.py:20

commit v7 on v5

--- a/solution.py
+++ b/solution.py
@@ -148,7 +148,8 @@
         edge = jnp.zeros((W, hidden.shape[1]), BF)
         padded_ref[i, :W, :] = edge
         padded_ref[i, W + voxels :, :] = edge
-        padded_ref[i, W : W + voxels, :] = shift_cols(hidden, v).astype(BF)
+        plane = shift_cols(hidden, v).astype(BF) if v else hidden_ref[...]
+        padded_ref[i, W : W + voxels, :] = plane
     upper = me_ref[0] % 2
     if lines == 1:
         blocks = [(0, halves, upper, [(half, 0) for half in range(halves)])]

time: 27.2 us -> 27.2 us (level)
  no operation moved by 1% of the time
where the time goes in v7:
time: 27.2 us; the launch traced here: 27 us
  starting transfers between devices  11.8 us (43%)
  waiting for transfers between devices  11.5 us (42%)
  Pallas kernels  3.61 us (13%)
    ppermute x13, starting transfers between devices, swap(): return lax.ppermute(block, 'rows', [(i, i ^ mask) for i in range(count)])  11.8 us
    ppermute x13, waiting for transfers between devices, swap(): return lax.ppermute(block, 'rows', [(i, i ^ mask) for i in range(count)])  11.5 us
    pallas_call x9, Pallas kernels, local(): pl.pallas_call(body, out_shape=outs, in_specs=[SMEM] + [VMEM] * len(args)...  3.61 us
  transfers between devices with their start and end apart: 13, of which 8 were waited for; matrix products, arithmetic and copies ran while one was open for 0% of the time, Pallas kernels for 7%

profile of v7, /device:TPU:0, one launch (start us, length us, event | category | flops | bytes accessed | tf_op | source)
XLA Modules:
  0.0 27.0 jit_solution(9720796977699243305)
XLA Ops:
  0.0 4.0 %collective-permute-start = (bf16[3,64,256]{2,1,0:T(8,128)(2,1)}, bf16[3,64,256]{2,1,0:T(8,128)(2,1)S(1)}, u32[]{:S(2)}, u32[]{:S(2)}) collective-permute-start(bf16[3,64,256]{2,1,0:T(8,128)(2,1)} %bitcast.8), channel_id=1, source_target_pairs={{0,6},{1,7},{2,4},{3,5},{4,2},{5,3},{6,0},{7,1},{8,14},{9,15},{10,... | collective-permute-start | bytes 294920 | tf_op jit(solution)/shard_map/ppermute | solution.py:20
  4.0 0.5 %collective-permute-start.4 = (bf16[3,64,256]{2,1,0:T(8,128)(2,1)}, bf16[3,64,256]{2,1,0:T(8,128)(2,1)S(1)}, u32[]{:S(2)}, u32[]{:S(2)}) collective-permute-start(bf16[3,64,256]{2,1,0:T(8,128)(2,1)} %bitcast.9), channel_id=1, source_target_pairs={{0,2},{1,3},{2,0},{3,1},{4,6},{5,7},{6,4},{7,5},{8,10},{9,11},{10,... | collective-permute-start | bytes 294920 | tf_op jit(solution)/shard_map/ppermute | solution.py:20
  4.5 0.1 collective-permute-start.5
  4.5 0.0 collective-permute-start.1
  4.6 2.9 %collective-permute-done.refs_3_ = bf16[3,64,256]{2,1,0:T(8,128)(2,1)S(1)} collective-permute-done((bf16[3,64,256]{2,1,0:T(8,128)(2,1)}, bf16[3,64,256]{2,1,0:T(8,128)(2,1)S(1)}, u32[]{:S(2)}, u32[]{:S(2)}) %collective-permute-start) | collective-permute-done | bytes 98336 | tf_op jit(solution)/shard_map/ppermute | solution.py:20
  7.5 0.0 collective-permute-done.1.tiles_ref
  7.5 0.5 %collective-permute-start.3 = (bf16[3,64,256]{2,1,0:T(8,128)(2,1)S(1)}, bf16[3,64,256]{2,1,0:T(8,128)(2,1)S(1)}, u32[]{:S(2)}, u32[]{:S(2)}) collective-permute-start(bf16[3,64,256]{2,1,0:T(8,128)(2,1)S(1)} %collective-permute-done.refs_3_), channel_id=1, source_target_pairs={{0,1},{1,0},{2,3},{3,2},{4,5},{5,4},{6,7},{7,6},{8,9},{9,8},{10,11... | collective-permute-start | bytes 294920 | tf_op jit(solution)/shard_map/ppermute | solution.py:20
  8.0 1.1 %collective-permute-done.4.refs_5_ = bf16[3,64,256]{2,1,0:T(8,128)(2,1)S(1)} collective-permute-done((bf16[3,64,256]{2,1,0:T(8,128)(2,1)}, bf16[3,64,256]{2,1,0:T(8,128)(2,1)S(1)}, u32[]{:S(2)}, u32[]{:S(2)}) %collective-permute-start.4) | collective-permute-done | bytes 98336 | tf_op jit(solution)/shard_map/ppermute | solution.py:20
  9.1 0.0 collective-permute-start.6
  9.1 0.2 collective-permute-done.5.refs_6_
  9.3 0.3 collective-permute-start.7
  9.6 0.0 collective-permute-done.2.refs_2_
  9.6 0.0 collective-permute-done.3.refs_4_
  9.6 1.0 %shard_map.38.refs_0_ = f32[9,256,128]{2,1,0:T(8,128)S(1)} custom-call(s32[1]{0:T(128)} %bitcast.me_ref, bf16[27,512,128]{2,1,0:T(8,128)(2,1)S(1)} %bitcast.4, bf16[3,64,256]{2,1,0:T(8,128)(2,1)S(1)} %bitcast.12, bf16[3,64,256]{2,1,0:T(8,128)(2,1)S(1)} %collective-permute-done.2.refs_2_, bf16[3,64,256]{2,1,0:T(8,128)(2,1)S(1)} %collective-permute-done.refs_3_, ...), custom_call_target="tpu_custom_call" | custom-call | flops 679477248 | bytes 2654208 | tf_op jit(solution)/shard_map/pallas_call | solution.py:24
  10.7 0.0 copy-start.1
  10.7 0.0 collective-permute-done.6.refs_2_
  10.7 0.5 %shard_map.39 = (f32[256,128]{1,0:T(8,128)S(1)}, bf16[256,128]{1,0:T(8,128)(2,1)S(1)}) custom-call(s32[1]{0:T(128)} %bitcast.me_ref, f32[9,256,128]{2,1,0:T(8,128)S(1)} %shard_map.38.refs_0_, bf16[27,512,128]{2,1,0:T(8,128)(2,1)S(1)} %bitcast.5, bf16[3,64,256]{2,1,0:T(8,128)(2,1)S(1)} %collective-permute-done.6.refs_2_, ...), custom_call_target="tpu_custom_call" | custom-call | flops 226492416 | bytes 884736 | tf_op jit(solution)/shard_map/pallas_call | solution.py:24
  11.2 2.8 %collective-permute-start.8 = (bf16[256,128]{1,0:T(8,128)(2,1)S(1)}, bf16[256,128]{1,0:T(8,128)(2,1)S(1)}, u32[]{:S(2)}, u32[]{:S(2)}) collective-permute-start(bf16[256,128]{1,0:T(8,128)(2,1)S(1)} %get-tuple-element.29), channel_id=1, source_target_pairs={{0,8},{1,9},{2,10},{3,11},{4,12},{5,13},{6,14},{7,15},{8,0},{9,1},... | collective-permute-start | bytes 196616 | tf_op jit(solution)/shard_map/ppermute | solution.py:20
  14.1 0.3 %shard_map.40.weight_ref = bf16[1,2,512,256]{3,2,1,0:T(8,128)(2,1)S(1)} custom-call(s32[1]{0:T(128)} %bitcast.me_ref, bf16[9,256,128]{2,1,0:T(8,128)(2,1)S(1)} %bitcast.7), custom_call_target="tpu_custom_call" | custom-call | flops 1048576 | bytes 1114112 | tf_op jit(solution)/shard_map/pallas_call | solution.py:24
  14.4 0.3 %shard_map.41.weight_ref = bf16[1,2,512,256]{3,2,1,0:T(8,128)(2,1)S(1)} custom-call(s32[1]{0:T(128)} %bitcast.me_ref, bf16[9,256,128]{2,1,0:T(8,128)(2,1)S(1)} %collective-permute-done.1.tiles_ref), custom_call_target="tpu_custom_call" | custom-call | flops 1048576 | bytes 1114112 | tf_op jit(solution)/shard_map/pallas_call | solution.py:24
  14.7 3.3 %collective-permute-done.8.refs_1_ = bf16[256,128]{1,0:T(8,128)(2,1)S(1)} collective-permute-done((bf16[256,128]{1,0:T(8,128)(2,1)S(1)}, bf16[256,128]{1,0:T(8,128)(2,1)S(1)}, u32[]{:S(2)}, u32[]{:S(2)}) %collective-permute-start.8) | collective-permute-done | bytes 65568 | tf_op jit(solution)/shard_map/ppermute | solution.py:20
  18.0 0.1 collective-permute-start.9
  18.1 0.3 %shard_map.43.before_ref = f32[4,1,128,256]{3,2,1,0:T(8,128)S(1)} custom-call(s32[1]{0:T(128)} %bitcast.me_ref, bf16[256,128]{1,0:T(8,128)(2,1)S(1)} %shard_map.42.hidden_ref, bf16[1,2,512,256]{3,2,1,0:T(8,128)(2,1)S(1)} %shard_map.40.weight_ref), custom_call_target="tpu_custom_call" | custom-call | flops 134217728 | bytes 524288 | tf_op jit(solution)/shard_map/pallas_call | solution.py:24
  18.4 0.9 %collective-permute-done.9.hidden_ref = bf16[256,128]{1,0:T(8,128)(2,1)S(1)} collective-permute-done((bf16[256,128]{1,0:T(8,128)(2,1)S(1)}, bf16[256,128]{1,0:T(8,128)(2,1)S(1)}, u32[]{:S(2)}, u32[]{:S(2)}) %collective-permute-start.9) | collective-permute-done | bytes 65568 | tf_op jit(solution)/shard_map/ppermute | solution.py:20
  19.3 0.3 %shard_map.44 = (f32[1,128,256]{2,1,0:T(8,128)S(1)}, bf16[1,128,256]{2,1,0:T(8,128)(2,1)S(1)}, bf16[1,128,256]{2,1,0:T(8,128)(2,1)S(1)}, bf16[1,128,256]{2,1,0:T(8,128)(2,1)S(1)}) custom-call(s32[1]{0:T(128)} %bitcast.me_ref, f32[4,1,128,256]{3,2,1,0:T(8,128)S(1)} %shard_map.43.before_ref, bf16[256,128]{1,0:T(8,128)(2,1)S(1)} %collective-permute-done.9.hidden_ref, ...), custom_call_target="tpu_custom_call" | custom-call | flops 134217728 | bytes 524288 | tf_op jit(solution)/shard_map/pallas_call | solution.py:24
  19.7 1.7 %collective-permute-start.10 = (bf16[1,128,256]{2,1,0:T(8,128)(2,1)S(1)}, bf16[1,128,256]{2,1,0:T(8,128)(2,1)S(1)}, u32[]{:S(2)}, u32[]{:S(2)}) collective-permute-start(bf16[1,128,256]{2,1,0:T(8,128)(2,1)S(1)} %get-tuple-element.36), channel_id=1, source_target_pairs={{0,6},{1,7},{2,4},{3,5},{4,2},{5,3},{6,0},{7,1},{8,14},{9,15},{10,... | collective-permute-start | bytes 196616 | tf_op jit(solution)/shard_map/ppermute | solution.py:20
  21.3 0.6 %collective-permute-start.11 = (bf16[1,128,256]{2,1,0:T(8,128)(2,1)S(1)}, bf16[1,128,256]{2,1,0:T(8,128)(2,1)S(1)}, u32[]{:S(2)}, u32[]{:S(2)}) collective-permute-start(bf16[1,128,256]{2,1,0:T(8,128)(2,1)S(1)} %get-tuple-element.37), channel_id=1, source_target_pairs={{0,2},{1,3},{2,0},{3,1},{4,6},{5,7},{6,4},{7,5},{8,10},{9,11},{10,... | collective-permute-start | bytes 196616 | tf_op jit(solution)/shard_map/ppermute | solution.py:20
  21.9 1.3 %collective-permute-start.12 = (bf16[1,128,256]{2,1,0:T(8,128)(2,1)S(1)}, bf16[1,128,256]{2,1,0:T(8,128)(2,1)S(1)}, u32[]{:S(2)}, u32[]{:S(2)}) collective-permute-start(bf16[1,128,256]{2,1,0:T(8,128)(2,1)S(1)} %get-tuple-element.38), channel_id=1, source_target_pairs={{0,4},{1,5},{2,6},{3,7},{4,0},{5,1},{6,2},{7,3},{8,12},{9,13},{10,... | collective-permute-start | bytes 196616 | tf_op jit(solution)/shard_map/ppermute | solution.py:20
  23.2 1.7 %collective-permute-done.10.refs_0_ = bf16[1,128,256]{2,1,0:T(8,128)(2,1)S(1)} collective-permute-done((bf16[1,128,256]{2,1,0:T(8,128)(2,1)S(1)}, bf16[1,128,256]{2,1,0:T(8,128)(2,1)S(1)}, u32[]{:S(2)}, u32[]{:S(2)}) %collective-permute-start.10) | collective-permute-done | bytes 65568 | tf_op jit(solution)/shard_map/ppermute | solution.py:20
  25.0 1.2 %collective-permute-done.11.refs_1_ = bf16[1,128,256]{2,1,0:T(8,128)(2,1)S(1)} collective-permute-done((bf16[1,128,256]{2,1,0:T(8,128)(2,1)S(1)}, bf16[1,128,256]{2,1,0:T(8,128)(2,1)S(1)}, u32[]{:S(2)}, u32[]{:S(2)}) %collective-permute-start.11) | collective-permute-done | bytes 65568 | tf_op jit(solution)/shard_map/ppermute | solution.py:20
  26.2 0.1 collective-permute-done.12.refs_2_
  26.3 0.8 %shard_map.45 = bf16[1,256,128]{2,1,0:T(8,128)(2,1)} custom-call(s32[1]{0:T(128)} %bitcast.me_ref, bf16[128,128]{1,0:T(8,128)(2,1)S(1)} %shard_map.37.spread_ref, f32[1,128,256]{2,1,0:T(8,128)S(1)} %get-tuple-element.35.own_ref, bf16[1,128,256]{2,1,0:T(8,128)(2,1)S(1)} %collective-permute-done.10.refs_0_, ...), custom_call_target="tpu_custom_call" | custom-call | flops 32768 | bytes 393216 | tf_op jit(solution)/shard_map/pallas_call | solution.py:24
  (9 shorter events, 0.1 us)
Async XLA Ops:
  0.0 7.4 %collective-permute-start = (bf16[3,64,256]{2,1,0:T(8,128)(2,1)}, bf16[3,64,256]{2,1,0:T(8,128)(2,1)S(1)}, u32[]{:S(2)}, u32[]{:S(2)}) collective-permute-start(bf16[3,64,256]{2,1,0:T(8,128)(2,1)} %bitcast.8), channel_id=1, source_target_pairs={{0,6},{1,7},{2,4},{3,5},{4,2},{5,3},{6,0},{7,1},{8,14},{9,15},{10,... | collective-permute-start | bytes 294920 | tf_op jit(solution)/shard_map/ppermute | solution.py:20
  4.0 5.1 %collective-permute-start.4 = (bf16[3,64,256]{2,1,0:T(8,128)(2,1)}, bf16[3,64,256]{2,1,0:T(8,128)(2,1)S(1)}, u32[]{:S(2)}, u32[]{:S(2)}) collective-permute-start(bf16[3,64,256]{2,1,0:T(8,128)(2,1)} %bitcast.9), channel_id=1, source_target_pairs={{0,2},{1,3},{2,0},{3,1},{4,6},{5,7},{6,4},{7,5},{8,10},{9,11},{10,... | collective-permute-start | bytes 294920 | tf_op jit(solution)/shard_map/ppermute | solution.py:20
  4.5 4.8 %collective-permute-start.5 = (bf16[3,64,256]{2,1,0:T(8,128)(2,1)}, bf16[3,64,256]{2,1,0:T(8,128)(2,1)S(1)}, u32[]{:S(2)}, u32[]{:S(2)}) collective-permute-start(bf16[3,64,256]{2,1,0:T(8,128)(2,1)} %bitcast.10), channel_id=1, source_target_pairs={{0,4},{1,5},{2,6},{3,7},{4,0},{5,1},{6,2},{7,3},{8,12},{9,13},{10,... | collective-permute-start | bytes 294920 | tf_op jit(solution)/shard_map/ppermute | solution.py:20
  4.5 2.9 %collective-permute-start.1 = (bf16[9,256,128]{2,1,0:T(8,128)(2,1)}, bf16[9,256,128]{2,1,0:T(8,128)(2,1)S(1)}, u32[]{:S(2)}, u32[]{:S(2)}) collective-permute-start(bf16[9,256,128]{2,1,0:T(8,128)(2,1)} %bitcast.6), channel_id=1, source_target_pairs={{0,1},{1,0},{2,3},{3,2},{4,5},{5,4},{6,7},{7,6},{8,9},{9,8},{10,11... | collective-permute-start | bytes 1769480 | tf_op jit(solution)/shard_map/ppermute | solution.py:20
  4.6 2.9 %copy-start.2 = (bf16[64,3,256]{2,0,1:T(8,128)(2,1)S(1)}, bf16[64,3,256]{2,0,1:T(8,128)(2,1)}, u32[]{:S(2)}) copy-start(bf16[64,3,256]{2,0,1:T(8,128)(2,1)} %param.3) | copy-start | bytes 294916
  4.6 5.1 %copy-start = (bf16[1,27,512,128]{3,2,1,0:T(8,128)(2,1)S(1)}, bf16[1,27,512,128]{3,2,1,0:T(8,128)(2,1)}, u32[]{:S(2)}) copy-start(bf16[1,27,512,128]{3,2,1,0:T(8,128)(2,1)} %param.4) | copy-start | bytes 10616836
  7.5 2.2 %collective-permute-start.2 = (bf16[3,64,256]{2,1,0:T(8,128)(2,1)S(1)}, bf16[3,64,256]{2,1,0:T(8,128)(2,1)S(1)}, u32[]{:S(2)}, u32[]{:S(2)}) collective-permute-start(bf16[3,64,256]{2,1,0:T(8,128)(2,1)S(1)} %bitcast.11), channel_id=1, source_target_pairs={{0,1},{1,0},{2,3},{3,2},{4,5},{5,4},{6,7},{7,6},{8,9},{9,8},{10,11... | collective-permute-start | bytes 294920 | tf_op jit(solution)/shard_map/ppermute | solution.py:20
  7.5 2.1 %collective-permute-start.3 = (bf16[3,64,256]{2,1,0:T(8,128)(2,1)S(1)}, bf16[3,64,256]{2,1,0:T(8,128)(2,1)S(1)}, u32[]{:S(2)}, u32[]{:S(2)}) collective-permute-start(bf16[3,64,256]{2,1,0:T(8,128)(2,1)S(1)} %collective-permute-done.refs_3_), channel_id=1, source_target_pairs={{0,1},{1,0},{2,3},{3,2},{4,5},{5,4},{6,7},{7,6},{8,9},{9,8},{10,11... | collective-permute-start | bytes 294920 | tf_op jit(solution)/shard_map/ppermute | solution.py:20
  9.1 1.6 %collective-permute-start.6 = (bf16[3,64,256]{2,1,0:T(8,128)(2,1)S(1)}, bf16[3,64,256]{2,1,0:T(8,128)(2,1)S(1)}, u32[]{:S(2)}, u32[]{:S(2)}) collective-permute-start(bf16[3,64,256]{2,1,0:T(8,128)(2,1)S(1)} %collective-permute-done.4.refs_5_), channel_id=1, source_target_pairs={{0,1},{1,0},{2,3},{3,2},{4,5},{5,4},{6,7},{7,6},{8,9},{9,8},{10,11... | collective-permute-start | bytes 294920 | tf_op jit(solution)/shard_map/ppermute | solution.py:20
  9.3 1.4 %collective-permute-start.7 = (bf16[3,64,256]{2,1,0:T(8,128)(2,1)S(1)}, bf16[3,64,256]{2,1,0:T(8,128)(2,1)S(1)}, u32[]{:S(2)}, u32[]{:S(2)}) collective-permute-start(bf16[3,64,256]{2,1,0:T(8,128)(2,1)S(1)} %collective-permute-done.5.refs_6_), channel_id=1, source_target_pairs={{0,1},{1,0},{2,3},{3,2},{4,5},{5,4},{6,7},{7,6},{8,9},{9,8},{10,11... | collective-permute-start | bytes 294920 | tf_op jit(solution)/shard_map/ppermute | solution.py:20
  10.7 3.4 %copy-start.1 = (bf16[1,9,256,128]{3,2,1,0:T(8,128)(2,1)S(1)}, bf16[1,9,256,128]{3,2,1,0:T(8,128)(2,1)}, u32[]{:S(2)}) copy-start(bf16[1,9,256,128]{3,2,1,0:T(8,128)(2,1)} %param.5) | copy-start | bytes 1769476
  11.2 6.7 %collective-permute-start.8 = (bf16[256,128]{1,0:T(8,128)(2,1)S(1)}, bf16[256,128]{1,0:T(8,128)(2,1)S(1)}, u32[]{:S(2)}, u32[]{:S(2)}) collective-permute-start(bf16[256,128]{1,0:T(8,128)(2,1)S(1)} %get-tuple-element.29), channel_id=1, source_target_pairs={{0,8},{1,9},{2,10},{3,11},{4,12},{5,13},{6,14},{7,15},{8,0},{9,1},... | collective-permute-start | bytes 196616 | tf_op jit(solution)/shard_map/ppermute | solution.py:20
  18.0 1.3 %collective-permute-start.9 = (bf16[256,128]{1,0:T(8,128)(2,1)S(1)}, bf16[256,128]{1,0:T(8,128)(2,1)S(1)}, u32[]{:S(2)}, u32[]{:S(2)}) collective-permute-start(bf16[256,128]{1,0:T(8,128)(2,1)S(1)} %shard_map.42.hidden_ref), channel_id=1, source_target_pairs={{0,1},{1,0},{2,3},{3,2},{4,5},{5,4},{6,7},{7,6},{8,9},{9,8},{10,11... | collective-permute-start | bytes 196616 | tf_op jit(solution)/shard_map/ppermute | solution.py:20
  19.7 5.3 %collective-permute-start.10 = (bf16[1,128,256]{2,1,0:T(8,128)(2,1)S(1)}, bf16[1,128,256]{2,1,0:T(8,128)(2,1)S(1)}, u32[]{:S(2)}, u32[]{:S(2)}) collective-permute-start(bf16[1,128,256]{2,1,0:T(8,128)(2,1)S(1)} %get-tuple-element.36), channel_id=1, source_target_pairs={{0,6},{1,7},{2,4},{3,5},{4,2},{5,3},{6,0},{7,1},{8,14},{9,15},{10,... | collective-permute-start | bytes 196616 | tf_op jit(solution)/shard_map/ppermute | solution.py:20
  21.3 4.9 %collective-permute-start.11 = (bf16[1,128,256]{2,1,0:T(8,128)(2,1)S(1)}, bf16[1,128,256]{2,1,0:T(8,128)(2,1)S(1)}, u32[]{:S(2)}, u32[]{:S(2)}) collective-permute-start(bf16[1,128,256]{2,1,0:T(8,128)(2,1)S(1)} %get-tuple-element.37), channel_id=1, source_target_pairs={{0,2},{1,3},{2,0},{3,1},{4,6},{5,7},{6,4},{7,5},{8,10},{9,11},{10,... | collective-permute-start | bytes 196616 | tf_op jit(solution)/shard_map/ppermute | solution.py:20
  21.9 4.4 %collective-permute-start.12 = (bf16[1,128,256]{2,1,0:T(8,128)(2,1)S(1)}, bf16[1,128,256]{2,1,0:T(8,128)(2,1)S(1)}, u32[]{:S(2)}, u32[]{:S(2)}) collective-permute-start(bf16[1,128,256]{2,1,0:T(8,128)(2,1)S(1)} %get-tuple-element.38), channel_id=1, source_target_pairs={{0,4},{1,5},{2,6},{3,7},{4,0},{5,1},{6,2},{7,3},{8,12},{9,13},{10,... | collective-permute-start | bytes 196616 | tf_op jit(solution)/shard_map/ppermute | solution.py:20

commit v8 on v7

--- a/solution.py
+++ b/solution.py
@@ -268,7 +268,7 @@
         steps = [()]
         pieces = [jnp.concatenate(pieces, 1)]
     else:
-        steps = [(0, 1, far, far + 1, *near), tuple(mask + 1 for mask in near)]
+        steps = [(0, far, *near, 1, far + 1), tuple(mask + 1 for mask in near)]
 
     before = []
     for i, masks in enumerate(steps):

time: 27.2 us -> 27.2 us (level)
  no operation moved by 1% of the time
where the time goes in v8:
time: 27.2 us; the launch traced here: 27.1 us
  starting transfers between devices  11.8 us (43%)
  waiting for transfers between devices  11.5 us (42%)
  Pallas kernels  3.62 us (13%)
    ppermute x13, starting transfers between devices, swap(): return lax.ppermute(block, 'rows', [(i, i ^ mask) for i in range(count)])  11.8 us
    ppermute x13, waiting for transfers between devices, swap(): return lax.ppermute(block, 'rows', [(i, i ^ mask) for i in range(count)])  11.5 us
    pallas_call x9, Pallas kernels, local(): pl.pallas_call(body, out_shape=outs, in_specs=[SMEM] + [VMEM] * len(args)...  3.62 us
  transfers between devices with their start and end apart: 13, of which 8 were waited for; matrix products, arithmetic and copies ran while one was open for 0% of the time, Pallas kernels for 7%

profile of v8, /device:TPU:0, one launch (start us, length us, event | category | flops | bytes accessed | tf_op | source)
XLA Modules:
  0.0 27.1 jit_solution(4876430869093728744)
XLA Ops:
  0.0 4.0 %collective-permute-start = (bf16[3,64,256]{2,1,0:T(8,128)(2,1)}, bf16[3,64,256]{2,1,0:T(8,128)(2,1)S(1)}, u32[]{:S(2)}, u32[]{:S(2)}) collective-permute-start(bf16[3,64,256]{2,1,0:T(8,128)(2,1)} %bitcast.8), channel_id=1, source_target_pairs={{0,6},{1,7},{2,4},{3,5},{4,2},{5,3},{6,0},{7,1},{8,14},{9,15},{10,... | collective-permute-start | bytes 294920 | tf_op jit(solution)/shard_map/ppermute | solution.py:20
  4.0 0.5 %collective-permute-start.2 = (bf16[3,64,256]{2,1,0:T(8,128)(2,1)}, bf16[3,64,256]{2,1,0:T(8,128)(2,1)S(1)}, u32[]{:S(2)}, u32[]{:S(2)}) collective-permute-start(bf16[3,64,256]{2,1,0:T(8,128)(2,1)} %bitcast.9), channel_id=1, source_target_pairs={{0,2},{1,3},{2,0},{3,1},{4,6},{5,7},{6,4},{7,5},{8,10},{9,11},{10,... | collective-permute-start | bytes 294920 | tf_op jit(solution)/shard_map/ppermute | solution.py:20
  4.5 0.1 collective-permute-start.3
  4.5 0.0 collective-permute-start.1
  4.6 2.9 %collective-permute-done.refs_2_ = bf16[3,64,256]{2,1,0:T(8,128)(2,1)S(1)} collective-permute-done((bf16[3,64,256]{2,1,0:T(8,128)(2,1)}, bf16[3,64,256]{2,1,0:T(8,128)(2,1)S(1)}, u32[]{:S(2)}, u32[]{:S(2)}) %collective-permute-start) | collective-permute-done | bytes 98336 | tf_op jit(solution)/shard_map/ppermute | solution.py:20
  7.5 0.0 collective-permute-done.1.tiles_ref
  7.5 0.0 collective-permute-start.4
  7.5 0.5 %collective-permute-start.5 = (bf16[3,64,256]{2,1,0:T(8,128)(2,1)S(1)}, bf16[3,64,256]{2,1,0:T(8,128)(2,1)S(1)}, u32[]{:S(2)}, u32[]{:S(2)}) collective-permute-start(bf16[3,64,256]{2,1,0:T(8,128)(2,1)S(1)} %collective-permute-done.refs_2_), channel_id=1, source_target_pairs={{0,1},{1,0},{2,3},{3,2},{4,5},{5,4},{6,7},{7,6},{8,9},{9,8},{10,11... | collective-permute-start | bytes 294920 | tf_op jit(solution)/shard_map/ppermute | solution.py:20
  8.0 1.1 %collective-permute-done.2.refs_3_ = bf16[3,64,256]{2,1,0:T(8,128)(2,1)S(1)} collective-permute-done((bf16[3,64,256]{2,1,0:T(8,128)(2,1)}, bf16[3,64,256]{2,1,0:T(8,128)(2,1)S(1)}, u32[]{:S(2)}, u32[]{:S(2)}) %collective-permute-start.2) | collective-permute-done | bytes 98336 | tf_op jit(solution)/shard_map/ppermute | solution.py:20
  9.1 0.0 collective-permute-start.6
  9.1 0.2 collective-permute-done.3.refs_4_
  9.3 0.3 collective-permute-start.7
  9.6 0.0 collective-permute-done.4.refs_5_
  9.6 1.0 %shard_map.38.refs_0_ = f32[9,256,128]{2,1,0:T(8,128)S(1)} custom-call(s32[1]{0:T(128)} %bitcast.me_ref, bf16[27,512,128]{2,1,0:T(8,128)(2,1)S(1)} %bitcast.4, bf16[3,64,256]{2,1,0:T(8,128)(2,1)S(1)} %bitcast.12, bf16[3,64,256]{2,1,0:T(8,128)(2,1)S(1)} %collective-permute-done.refs_2_, bf16[3,64,256]{2,1,0:T(8,128)(2,1)S(1)} %collective-permute-done.2.refs_3_, ...), custom_call_target="tpu_custom_call" | custom-call | flops 679477248 | bytes 2654208 | tf_op jit(solution)/shard_map/pallas_call | solution.py:24
  10.7 0.0 copy-start.1
  10.7 0.0 collective-permute-done.6.refs_2_
  10.7 0.5 %shard_map.39 = (f32[256,128]{1,0:T(8,128)S(1)}, bf16[256,128]{1,0:T(8,128)(2,1)S(1)}) custom-call(s32[1]{0:T(128)} %bitcast.me_ref, f32[9,256,128]{2,1,0:T(8,128)S(1)} %shard_map.38.refs_0_, bf16[27,512,128]{2,1,0:T(8,128)(2,1)S(1)} %bitcast.5, bf16[3,64,256]{2,1,0:T(8,128)(2,1)S(1)} %collective-permute-done.6.refs_2_, ...), custom_call_target="tpu_custom_call" | custom-call | flops 226492416 | bytes 884736 | tf_op jit(solution)/shard_map/pallas_call | solution.py:24
  11.2 2.9 %collective-permute-start.8 = (bf16[256,128]{1,0:T(8,128)(2,1)S(1)}, bf16[256,128]{1,0:T(8,128)(2,1)S(1)}, u32[]{:S(2)}, u32[]{:S(2)}) collective-permute-start(bf16[256,128]{1,0:T(8,128)(2,1)S(1)} %get-tuple-element.29), channel_id=1, source_target_pairs={{0,8},{1,9},{2,10},{3,11},{4,12},{5,13},{6,14},{7,15},{8,0},{9,1},... | collective-permute-start | bytes 196616 | tf_op jit(solution)/shard_map/ppermute | solution.py:20
  14.1 0.3 %shard_map.40.weight_ref = bf16[1,2,512,256]{3,2,1,0:T(8,128)(2,1)S(1)} custom-call(s32[1]{0:T(128)} %bitcast.me_ref, bf16[9,256,128]{2,1,0:T(8,128)(2,1)S(1)} %bitcast.7), custom_call_target="tpu_custom_call" | custom-call | flops 1048576 | bytes 1114112 | tf_op jit(solution)/shard_map/pallas_call | solution.py:24
  14.4 0.3 %shard_map.41.weight_ref = bf16[1,2,512,256]{3,2,1,0:T(8,128)(2,1)S(1)} custom-call(s32[1]{0:T(128)} %bitcast.me_ref, bf16[9,256,128]{2,1,0:T(8,128)(2,1)S(1)} %collective-permute-done.1.tiles_ref), custom_call_target="tpu_custom_call" | custom-call | flops 1048576 | bytes 1114112 | tf_op jit(solution)/shard_map/pallas_call | solution.py:24
  14.7 3.3 %collective-permute-done.8.refs_1_ = bf16[256,128]{1,0:T(8,128)(2,1)S(1)} collective-permute-done((bf16[256,128]{1,0:T(8,128)(2,1)S(1)}, bf16[256,128]{1,0:T(8,128)(2,1)S(1)}, u32[]{:S(2)}, u32[]{:S(2)}) %collective-permute-start.8) | collective-permute-done | bytes 65568 | tf_op jit(solution)/shard_map/ppermute | solution.py:20
  18.0 0.1 collective-permute-start.9
  18.1 0.3 %shard_map.43.before_ref = f32[4,1,128,256]{3,2,1,0:T(8,128)S(1)} custom-call(s32[1]{0:T(128)} %bitcast.me_ref, bf16[256,128]{1,0:T(8,128)(2,1)S(1)} %shard_map.42.hidden_ref, bf16[1,2,512,256]{3,2,1,0:T(8,128)(2,1)S(1)} %shard_map.40.weight_ref), custom_call_target="tpu_custom_call" | custom-call | flops 134217728 | bytes 524288 | tf_op jit(solution)/shard_map/pallas_call | solution.py:24
  18.4 0.9 %collective-permute-done.9.hidden_ref = bf16[256,128]{1,0:T(8,128)(2,1)S(1)} collective-permute-done((bf16[256,128]{1,0:T(8,128)(2,1)S(1)}, bf16[256,128]{1,0:T(8,128)(2,1)S(1)}, u32[]{:S(2)}, u32[]{:S(2)}) %collective-permute-start.9) | collective-permute-done | bytes 65568 | tf_op jit(solution)/shard_map/ppermute | solution.py:20
  19.3 0.3 %shard_map.44 = (f32[1,128,256]{2,1,0:T(8,128)S(1)}, bf16[1,128,256]{2,1,0:T(8,128)(2,1)S(1)}, bf16[1,128,256]{2,1,0:T(8,128)(2,1)S(1)}, bf16[1,128,256]{2,1,0:T(8,128)(2,1)S(1)}) custom-call(s32[1]{0:T(128)} %bitcast.me_ref, f32[4,1,128,256]{3,2,1,0:T(8,128)S(1)} %shard_map.43.before_ref, bf16[256,128]{1,0:T(8,128)(2,1)S(1)} %collective-permute-done.9.hidden_ref, ...), custom_call_target="tpu_custom_call" | custom-call | flops 134217728 | bytes 524288 | tf_op jit(solution)/shard_map/pallas_call | solution.py:24
  19.7 1.7 %collective-permute-start.10 = (bf16[1,128,256]{2,1,0:T(8,128)(2,1)S(1)}, bf16[1,128,256]{2,1,0:T(8,128)(2,1)S(1)}, u32[]{:S(2)}, u32[]{:S(2)}) collective-permute-start(bf16[1,128,256]{2,1,0:T(8,128)(2,1)S(1)} %get-tuple-element.36), channel_id=1, source_target_pairs={{0,6},{1,7},{2,4},{3,5},{4,2},{5,3},{6,0},{7,1},{8,14},{9,15},{10,... | collective-permute-start | bytes 196616 | tf_op jit(solution)/shard_map/ppermute | solution.py:20
  21.4 0.6 %collective-permute-start.11 = (bf16[1,128,256]{2,1,0:T(8,128)(2,1)S(1)}, bf16[1,128,256]{2,1,0:T(8,128)(2,1)S(1)}, u32[]{:S(2)}, u32[]{:S(2)}) collective-permute-start(bf16[1,128,256]{2,1,0:T(8,128)(2,1)S(1)} %get-tuple-element.37), channel_id=1, source_target_pairs={{0,2},{1,3},{2,0},{3,1},{4,6},{5,7},{6,4},{7,5},{8,10},{9,11},{10,... | collective-permute-start | bytes 196616 | tf_op jit(solution)/shard_map/ppermute | solution.py:20
  21.9 1.3 %collective-permute-start.12 = (bf16[1,128,256]{2,1,0:T(8,128)(2,1)S(1)}, bf16[1,128,256]{2,1,0:T(8,128)(2,1)S(1)}, u32[]{:S(2)}, u32[]{:S(2)}) collective-permute-start(bf16[1,128,256]{2,1,0:T(8,128)(2,1)S(1)} %get-tuple-element.38), channel_id=1, source_target_pairs={{0,4},{1,5},{2,6},{3,7},{4,0},{5,1},{6,2},{7,3},{8,12},{9,13},{10,... | collective-permute-start | bytes 196616 | tf_op jit(solution)/shard_map/ppermute | solution.py:20
  23.2 1.7 %collective-permute-done.10.refs_0_ = bf16[1,128,256]{2,1,0:T(8,128)(2,1)S(1)} collective-permute-done((bf16[1,128,256]{2,1,0:T(8,128)(2,1)S(1)}, bf16[1,128,256]{2,1,0:T(8,128)(2,1)S(1)}, u32[]{:S(2)}, u32[]{:S(2)}) %collective-permute-start.10) | collective-permute-done | bytes 65568 | tf_op jit(solution)/shard_map/ppermute | solution.py:20
  25.0 1.2 %collective-permute-done.11.refs_1_ = bf16[1,128,256]{2,1,0:T(8,128)(2,1)S(1)} collective-permute-done((bf16[1,128,256]{2,1,0:T(8,128)(2,1)S(1)}, bf16[1,128,256]{2,1,0:T(8,128)(2,1)S(1)}, u32[]{:S(2)}, u32[]{:S(2)}) %collective-permute-start.11) | collective-permute-done | bytes 65568 | tf_op jit(solution)/shard_map/ppermute | solution.py:20
  26.2 0.1 collective-permute-done.12.refs_2_
  26.3 0.8 %shard_map.45 = bf16[1,256,128]{2,1,0:T(8,128)(2,1)} custom-call(s32[1]{0:T(128)} %bitcast.me_ref, bf16[128,128]{1,0:T(8,128)(2,1)S(1)} %shard_map.37.spread_ref, f32[1,128,256]{2,1,0:T(8,128)S(1)} %get-tuple-element.35.own_ref, bf16[1,128,256]{2,1,0:T(8,128)(2,1)S(1)} %collective-permute-done.10.refs_0_, ...), custom_call_target="tpu_custom_call" | custom-call | flops 32768 | bytes 393216 | tf_op jit(solution)/shard_map/pallas_call | solution.py:24
  (9 shorter events, 0.1 us)
Async XLA Ops:
  0.0 7.4 %collective-permute-start = (bf16[3,64,256]{2,1,0:T(8,128)(2,1)}, bf16[3,64,256]{2,1,0:T(8,128)(2,1)S(1)}, u32[]{:S(2)}, u32[]{:S(2)}) collective-permute-start(bf16[3,64,256]{2,1,0:T(8,128)(2,1)} %bitcast.8), channel_id=1, source_target_pairs={{0,6},{1,7},{2,4},{3,5},{4,2},{5,3},{6,0},{7,1},{8,14},{9,15},{10,... | collective-permute-start | bytes 294920 | tf_op jit(solution)/shard_map/ppermute | solution.py:20
  4.0 5.1 %collective-permute-start.2 = (bf16[3,64,256]{2,1,0:T(8,128)(2,1)}, bf16[3,64,256]{2,1,0:T(8,128)(2,1)S(1)}, u32[]{:S(2)}, u32[]{:S(2)}) collective-permute-start(bf16[3,64,256]{2,1,0:T(8,128)(2,1)} %bitcast.9), channel_id=1, source_target_pairs={{0,2},{1,3},{2,0},{3,1},{4,6},{5,7},{6,4},{7,5},{8,10},{9,11},{10,... | collective-permute-start | bytes 294920 | tf_op jit(solution)/shard_map/ppermute | solution.py:20
  4.5 4.8 %collective-permute-start.3 = (bf16[3,64,256]{2,1,0:T(8,128)(2,1)}, bf16[3,64,256]{2,1,0:T(8,128)(2,1)S(1)}, u32[]{:S(2)}, u32[]{:S(2)}) collective-permute-start(bf16[3,64,256]{2,1,0:T(8,128)(2,1)} %bitcast.10), channel_id=1, source_target_pairs={{0,4},{1,5},{2,6},{3,7},{4,0},{5,1},{6,2},{7,3},{8,12},{9,13},{10,... | collective-permute-start | bytes 294920 | tf_op jit(solution)/shard_map/ppermute | solution.py:20
  4.5 2.9 %collective-permute-start.1 = (bf16[9,256,128]{2,1,0:T(8,128)(2,1)}, bf16[9,256,128]{2,1,0:T(8,128)(2,1)S(1)}, u32[]{:S(2)}, u32[]{:S(2)}) collective-permute-start(bf16[9,256,128]{2,1,0:T(8,128)(2,1)} %bitcast.6), channel_id=1, source_target_pairs={{0,1},{1,0},{2,3},{3,2},{4,5},{5,4},{6,7},{7,6},{8,9},{9,8},{10,11... | collective-permute-start | bytes 1769480 | tf_op jit(solution)/shard_map/ppermute | solution.py:20
  4.6 2.9 %copy-start.2 = (bf16[64,3,256]{2,0,1:T(8,128)(2,1)S(1)}, bf16[64,3,256]{2,0,1:T(8,128)(2,1)}, u32[]{:S(2)}) copy-start(bf16[64,3,256]{2,0,1:T(8,128)(2,1)} %param.3) | copy-start | bytes 294916
  4.6 5.1 %copy-start = (bf16[1,27,512,128]{3,2,1,0:T(8,128)(2,1)S(1)}, bf16[1,27,512,128]{3,2,1,0:T(8,128)(2,1)}, u32[]{:S(2)}) copy-start(bf16[1,27,512,128]{3,2,1,0:T(8,128)(2,1)} %param.4) | copy-start | bytes 10616836
  7.5 2.2 %collective-permute-start.4 = (bf16[3,64,256]{2,1,0:T(8,128)(2,1)S(1)}, bf16[3,64,256]{2,1,0:T(8,128)(2,1)S(1)}, u32[]{:S(2)}, u32[]{:S(2)}) collective-permute-start(bf16[3,64,256]{2,1,0:T(8,128)(2,1)S(1)} %bitcast.11), channel_id=1, source_target_pairs={{0,1},{1,0},{2,3},{3,2},{4,5},{5,4},{6,7},{7,6},{8,9},{9,8},{10,11... | collective-permute-start | bytes 294920 | tf_op jit(solution)/shard_map/ppermute | solution.py:20
  7.5 2.1 %collective-permute-start.5 = (bf16[3,64,256]{2,1,0:T(8,128)(2,1)S(1)}, bf16[3,64,256]{2,1,0:T(8,128)(2,1)S(1)}, u32[]{:S(2)}, u32[]{:S(2)}) collective-permute-start(bf16[3,64,256]{2,1,0:T(8,128)(2,1)S(1)} %collective-permute-done.refs_2_), channel_id=1, source_target_pairs={{0,1},{1,0},{2,3},{3,2},{4,5},{5,4},{6,7},{7,6},{8,9},{9,8},{10,11... | collective-permute-start | bytes 294920 | tf_op jit(solution)/shard_map/ppermute | solution.py:20
  9.1 1.6 %collective-permute-start.6 = (bf16[3,64,256]{2,1,0:T(8,128)(2,1)S(1)}, bf16[3,64,256]{2,1,0:T(8,128)(2,1)S(1)}, u32[]{:S(2)}, u32[]{:S(2)}) collective-permute-start(bf16[3,64,256]{2,1,0:T(8,128)(2,1)S(1)} %collective-permute-done.2.refs_3_), channel_id=1, source_target_pairs={{0,1},{1,0},{2,3},{3,2},{4,5},{5,4},{6,7},{7,6},{8,9},{9,8},{10,11... | collective-permute-start | bytes 294920 | tf_op jit(solution)/shard_map/ppermute | solution.py:20
  9.3 1.4 %collective-permute-start.7 = (bf16[3,64,256]{2,1,0:T(8,128)(2,1)S(1)}, bf16[3,64,256]{2,1,0:T(8,128)(2,1)S(1)}, u32[]{:S(2)}, u32[]{:S(2)}) collective-permute-start(bf16[3,64,256]{2,1,0:T(8,128)(2,1)S(1)} %collective-permute-done.3.refs_4_), channel_id=1, source_target_pairs={{0,1},{1,0},{2,3},{3,2},{4,5},{5,4},{6,7},{7,6},{8,9},{9,8},{10,11... | collective-permute-start | bytes 294920 | tf_op jit(solution)/shard_map/ppermute | solution.py:20
  10.7 3.4 %copy-start.1 = (bf16[1,9,256,128]{3,2,1,0:T(8,128)(2,1)S(1)}, bf16[1,9,256,128]{3,2,1,0:T(8,128)(2,1)}, u32[]{:S(2)}) copy-start(bf16[1,9,256,128]{3,2,1,0:T(8,128)(2,1)} %param.5) | copy-start | bytes 1769476
  11.2 6.7 %collective-permute-start.8 = (bf16[256,128]{1,0:T(8,128)(2,1)S(1)}, bf16[256,128]{1,0:T(8,128)(2,1)S(1)}, u32[]{:S(2)}, u32[]{:S(2)}) collective-permute-start(bf16[256,128]{1,0:T(8,128)(2,1)S(1)} %get-tuple-element.29), channel_id=1, source_target_pairs={{0,8},{1,9},{2,10},{3,11},{4,12},{5,13},{6,14},{7,15},{8,0},{9,1},... | collective-permute-start | bytes 196616 | tf_op jit(solution)/shard_map/ppermute | solution.py:20
  18.0 1.3 %collective-permute-start.9 = (bf16[256,128]{1,0:T(8,128)(2,1)S(1)}, bf16[256,128]{1,0:T(8,128)(2,1)S(1)}, u32[]{:S(2)}, u32[]{:S(2)}) collective-permute-start(bf16[256,128]{1,0:T(8,128)(2,1)S(1)} %shard_map.42.hidden_ref), channel_id=1, source_target_pairs={{0,1},{1,0},{2,3},{3,2},{4,5},{5,4},{6,7},{7,6},{8,9},{9,8},{10,11... | collective-permute-start | bytes 196616 | tf_op jit(solution)/shard_map/ppermute | solution.py:20
  19.7 5.3 %collective-permute-start.10 = (bf16[1,128,256]{2,1,0:T(8,128)(2,1)S(1)}, bf16[1,128,256]{2,1,0:T(8,128)(2,1)S(1)}, u32[]{:S(2)}, u32[]{:S(2)}) collective-permute-start(bf16[1,128,256]{2,1,0:T(8,128)(2,1)S(1)} %get-tuple-element.36), channel_id=1, source_target_pairs={{0,6},{1,7},{2,4},{3,5},{4,2},{5,3},{6,0},{7,1},{8,14},{9,15},{10,... | collective-permute-start | bytes 196616 | tf_op jit(solution)/shard_map/ppermute | solution.py:20
  21.4 4.8 %collective-permute-start.11 = (bf16[1,128,256]{2,1,0:T(8,128)(2,1)S(1)}, bf16[1,128,256]{2,1,0:T(8,128)(2,1)S(1)}, u32[]{:S(2)}, u32[]{:S(2)}) collective-permute-start(bf16[1,128,256]{2,1,0:T(8,128)(2,1)S(1)} %get-tuple-element.37), channel_id=1, source_target_pairs={{0,2},{1,3},{2,0},{3,1},{4,6},{5,7},{6,4},{7,5},{8,10},{9,11},{10,... | collective-permute-start | bytes 196616 | tf_op jit(solution)/shard_map/ppermute | solution.py:20
  21.9 4.4 %collective-permute-start.12 = (bf16[1,128,256]{2,1,0:T(8,128)(2,1)S(1)}, bf16[1,128,256]{2,1,0:T(8,128)(2,1)S(1)}, u32[]{:S(2)}, u32[]{:S(2)}) collective-permute-start(bf16[1,128,256]{2,1,0:T(8,128)(2,1)S(1)} %get-tuple-element.38), channel_id=1, source_target_pairs={{0,4},{1,5},{2,6},{3,7},{4,0},{5,1},{6,2},{7,3},{8,12},{9,13},{10,... | collective-permute-start | bytes 196616 | tf_op jit(solution)/shard_map/ppermute | solution.py:20
